TPU v7x, 32 devices: a whole 2x2x4 slice. The times are simulated.
32 devices in a mesh: groups: 2 (over y), seq: 4 (over z), head: 2 (over x), rep: 2 (over core).
Axes of the slice: x: 2, y: 2, z: 4, core: 2. Of those that a mesh axis runs over, the one named last changes fastest.
Arguments:
- queries: bfloat16 [16384, 2, 128], P(('groups', 'seq', 'rep'), 'head'), parts along dimension 0, may hold values from -160 to 160
- key_rows: bfloat16 [16384, 2, 128], P(('groups', 'seq', 'rep'), 'head'), parts along dimension 0, may hold values from -14 to 14
- value_rows: bfloat16 [16384, 2, 128], P(('groups', 'seq', 'rep'), 'head'), parts along dimension 0, may hold values from -6 to 6
- pattern: int32 [128, 6], P('groups'), parts along dimension 0, may hold values from -1 to 63, as said below
Outputs:
- attended: bfloat16 [16384, 2, 128], P(('groups', 'seq', 'rep'), 'head'), parts along dimension 0
There are 2 independent parts, one for each index of `groups`. A program takes and returns all parts, laid end to end along the dimension named above; each array names one. Nothing has to cross between parts.
Inputs may be any that keep to these rules, and one draw needn't show every extreme that they name: `pattern`: row n lists, in this order, blocks n, n - 1 and n + 1 taken cyclically over the 64 blocks, then 3 entries: some key blocks followed by -1 for the rest; entry 3 + j, when it is not -1, is one of the blocks ((n // 8 + 2 + j) % 8) * 8 to that plus 8 - 1.
All inputs are finite; a program needn't handle non-finite values.
Results may differ from a plain program's by a relative error of at most 0.0049.
Values may be sent and summed in bfloat16 or wider, within the bound.
No kernel may reach another device: no remote copies, remote signals or barrier semaphores. Data moves between devices by JAX's collectives and lax.ppermute only.
A program may use at most 64 MiB of HBM per device.

v0:
```python
from functools import reduce
import math

import jax
import jax.numpy as jnp
from jax import lax
from jax.sharding import PartitionSpec as P

BLOCK = 128
ITERS = 2


def with_halo(block, sides, width):
    for axis, dim in sides:
        count = lax.axis_size(axis)
        forward = [(i, i + 1) for i in range(count - 1)]
        forward.append((count - 1, 0))
        backward = [(target, source) for source, target in forward]
        low = lax.ppermute(
            lax.slice_in_dim(block, block.shape[dim] - width, None, axis=dim), axis, forward
        )
        high = lax.ppermute(lax.slice_in_dim(block, 0, width, axis=dim), axis, backward)
        block = jnp.concatenate([low, block, high], axis=dim)
    return block


def shifted(x, axis, by):
    devices = lax.axis_size(axis)
    return lax.ppermute(x, axis, [(i, (i + by) % devices) for i in range(devices)])


def normalize_rows(weights):
    totals = reduce(jnp.add, [weight.sum(-1) for weight in weights])
    return [weight / totals[..., None] for weight in weights]


def body(queries, key_rows, value_rows, pattern):
    tok_local, heads_local, width = queries.shape
    blocks = tok_local // BLOCK
    list_len = pattern.shape[1]
    far_count = list_len - 3
    shards = lax.axis_size(("seq", "rep"))
    position = lax.axis_index(("seq", "rep"))
    my_lists = lax.dynamic_slice_in_dim(pattern, position * blocks, blocks, 0)
    present = my_lists >= 0
    far_local = []
    for slot_num in range(far_count):
        source = (position + 2 + slot_num) % shards
        far_local.append(
            jnp.where(present[:, 3 + slot_num], my_lists[:, 3 + slot_num] - source * blocks, 0)
        )
    paired = jnp.concatenate([key_rows, value_rows], axis=2)
    window = with_halo(paired, ((("seq", "rep"), 0),), BLOCK)
    window = window.reshape(blocks + 2, BLOCK, heads_local, 2 * width)
    far_shards = []
    for slot_num in range(far_count):
        far_shards.append(shifted(paired, ("seq", "rep"), shards - 2 - slot_num))
    slot_keys = [window[1 : blocks + 1], window[0:blocks], window[2 : blocks + 2]]
    for slot_num in range(far_count):
        shaped = far_shards[slot_num].reshape(blocks, BLOCK, heads_local, 2 * width)
        slot_keys.append(jnp.take(shaped, far_local[slot_num], axis=0))
    query_blocks = queries.reshape(blocks, BLOCK, heads_local, width)
    scores = []
    for slot, key_block in enumerate(slot_keys):
        score = jnp.einsum(
            "iqhd,iuhd->ihqu",
            query_blocks,
            key_block[..., :width],
            preferred_element_type=jnp.float32,
        ) / math.sqrt(width)
        scores.append(jnp.where(present[:, slot][:, None, None, None], score, -jnp.inf))
    row_peak = reduce(jnp.maximum, [score.max(-1) for score in scores])
    weights = normalize_rows([jnp.exp(score - row_peak[..., None]) for score in scores])
    for number in range(ITERS):
        col_parts = [weight.sum(2) for weight in weights]
        key_index = jnp.where(present, my_lists, 0)
        stacked = jnp.stack(col_parts, axis=1)
        full_sums = jnp.zeros((pattern.shape[0], heads_local, BLOCK), jnp.float32)
        full_sums = full_sums.at[key_index.reshape(-1)].add(stacked.reshape(-1, heads_local, BLOCK))
        full_sums = lax.psum(full_sums, ("seq", "rep"))
        col_sums = [jnp.take(full_sums, key_index[:, slot], axis=0) for slot in range(list_len)]
        weights = normalize_rows(
            [weight / divisor[:, :, None, :] for weight, divisor in zip(weights, col_sums)]
        )
    attended = reduce(
        jnp.add,
        [
            jnp.einsum(
                "ihqu,iuhd->iqhd",
                weight.astype(jnp.bfloat16),
                key_block[..., width:],
                preferred_element_type=jnp.float32,
            )
            for weight, key_block in zip(weights, slot_keys)
        ],
    )
    return attended.reshape(tok_local, heads_local, width).astype(jnp.bfloat16)


def solution(mesh):
    in_specs = (
        P(("groups", "seq", "rep"), "head", None),
        P(("groups", "seq", "rep"), "head", None),
        P(("groups", "seq", "rep"), "head", None),
        P("groups", None),
    )
    out_specs = P(("groups", "seq", "rep"), "head", None)
    return jax.shard_map(body, mesh=mesh, in_specs=in_specs, out_specs=out_specs, check_vma=False)
```

profile of v0, /device:TPU:0, one launch (start us, length us, event | category | flops | bytes accessed | tf_op | source)
XLA Modules:
  0.0 143.2 jit_solution(14322862773397153718)
XLA Ops:
  0.0 1.1 constant_dynamic-update-slice_fusion.1
  1.2 5.1 %collective-permute-start.2 = (bf16[1024,1,256]{2,0,1:T(8,128)(2,1)S(1)}, bf16[1024,1,256]{2,0,1:T(8,128)(2,1)S(1)}, u32[]{:S(2)}, u32[]{:S(2)}) collective-permute-start(bf16[1024,1,256]{2,0,1:T(8,128)(2,1)S(1)} %constant_dynamic-update-slice_fusion), channel_id=1, source_target_pairs={{0,12},{1,13},{4,0},{5,1},{8,4},{9,5},{12,8},{13,9},{2,14},{3,15},... | collective-permute-start | bytes 1572872 | tf_op jit(solution)/shard_map/ppermute | solution.py:29
  6.3 1.8 %collective-permute-start.3 = (bf16[1024,1,256]{2,0,1:T(8,128)(2,1)S(1)}, bf16[1024,1,256]{2,0,1:T(8,128)(2,1)}, u32[]{:S(2)}, u32[]{:S(2)}) collective-permute-start(bf16[1024,1,256]{2,0,1:T(8,128)(2,1)S(1)} %constant_dynamic-update-slice_fusion), channel_id=1, source_target_pairs={{0,9},{1,12},{4,13},{5,0},{8,1},{9,4},{12,5},{13,8},{2,11},{3,14},... | collective-permute-start | bytes 1572872 | tf_op jit(solution)/shard_map/ppermute | solution.py:29
  8.1 2.4 %collective-permute-start.1 = (bf16[128,1,256]{2,0,1:T(8,128)(2,1)S(1)}, bf16[128,1,256]{2,0,1:T(8,128)(2,1)S(1)}, u32[]{:S(2)}, u32[]{:S(2)}) collective-permute-start(bf16[128,1,256]{2,0,1:T(8,128)(2,1)S(1)} %get-tuple-element.58), channel_id=1, source_target_pairs={{1,0},{4,1},{5,4},{8,5},{9,8},{12,9},{13,12},{0,13},{3,2},{6,3},{7... | collective-permute-start | bytes 196616 | tf_op jit(solution)/shard_map/ppermute | solution.py:22
  10.4 0.7 copy-done.27
  11.3 0.6 compare_and_fusion
  12.0 0.6 fusion.125
  12.7 0.3 fusion.131
  13.0 28.4 %collective-permute-done.1 = bf16[128,1,256]{2,0,1:T(8,128)(2,1)S(1)} collective-permute-done((bf16[128,1,256]{2,0,1:T(8,128)(2,1)S(1)}, bf16[128,1,256]{2,0,1:T(8,128)(2,1)S(1)}, u32[]{:S(2)}, u32[]{:S(2)}) %collective-permute-start.1) | collective-permute-done | bytes 65568 | tf_op jit(solution)/shard_map/ppermute | solution.py:22
  41.5 0.3 fusion.132
  41.8 0.5 copy-done.5
  42.3 0.2 copy-done.3
  42.5 0.3 fusion.130
  42.8 0.6 gather_fusion
  43.4 0.1 bitcast_select_fusion.2
  43.5 0.3 fusion.129
  43.8 0.5 copy-done.7
  44.3 3.1 %collective-permute-done.4 = bf16[1024,1,256]{2,0,1:T(8,128)(2,1)} collective-permute-done((bf16[1024,1,256]{2,0,1:T(8,128)(2,1)S(1)}, bf16[1024,1,256]{2,0,1:T(8,128)(2,1)}, u32[]{:S(2)}, u32[]{:S(2)}) %collective-permute-start.4) | collective-permute-done | bytes 524320 | tf_op jit(solution)/shard_map/ppermute | solution.py:29
  47.4 1.6 %gather_fusion.2 = bf16[8,128,256]{2,1,0:T(8,128)(2,1)S(1)} fusion(bf16[8,128,256]{2,1,0:T(8,128)(2,1)} %bitcast.31, s32[1024]{0:T(1024)S(1)} %pad_clamp_fusion.6), kind=kCustom, calls=%fused_computation.3.clone | custom fusion | bytes 1048608 | tf_op jit(solution)/shard_map/jit(_take)/gather | solution.py:61
  49.0 0.1 bitcast_select_fusion
  49.1 0.3 fusion.127
  49.4 0.5 copy-done.9
  49.9 1.6 %gather_fusion.1 = bf16[8,128,256]{2,1,0:T(8,128)(2,1)S(1)} fusion(bf16[8,128,256]{2,1,0:T(8,128)(2,1)} %bitcast.24, s32[1024]{0:T(1024)S(1)} %pad_clamp_fusion.7), kind=kCustom, calls=%fused_computation.2.clone | custom fusion | bytes 1048608 | tf_op jit(solution)/shard_map/jit(_take)/gather | solution.py:61
  51.6 0.1 bitcast_select_fusion.1
  51.7 0.3 fusion.128
  52.0 0.5 copy-done.11
  52.5 0.6 fusion.104
  53.1 0.9 divide_reduce_fusion
  54.0 0.9 scatter_custom_fusion
  54.9 37.2 %psum.14 = f32[64,1,128]{2,0,1:T(8,128)S(1)} all-reduce(f32[64,1,128]{2,0,1:T(8,128)S(1)} %bitcast.274), channel_id=1, replica_groups=mesh['groups'=2,'seq'=4,'head'=2,'rep'=2] {'seq','rep'}, use_global_device_ids=true, to_apply=%region_19.21 | all-reduce | flops 8192 | bytes 65536 | tf_op jit(solution)/shard_map/psum | solution.py:80
  92.1 0.6 gather_fusion.8
  92.7 0.6 gather_fusion.7
  93.2 0.6 gather_fusion.6
  93.8 0.6 gather_fusion.5
  94.4 0.6 gather_fusion.4
  94.9 0.6 gather_fusion.3
  95.5 0.6 copy-done.25
  96.1 0.6 copy-done.23
  96.8 0.7 copy-done.21
  97.8 1.2 fusion.50
  99.0 1.9 %fusion.55 = (f32[8,128]{1,0:T(8,128)S(1)}, f32[8,128]{1,0:T(8,128)S(1)}, f32[8,128]{1,0:T(8,128)S(1)}, f32[8,128]{1,0:T(8,128)S(1)}, f32[8,128]{1,0:T(8,128)S(1)}, /*index=5*/f32[8,128]{1,0:T(8,128)S(1)}) fusion(f32[8,128]{1,0:T(8,128)S(1)} %add_add_fusion.1, f32[8,128]{1,0:T(8,128)S(1)} %fusion.119, f32[8,128]{1,0:T(8,128)S(1)} %add_add_fusion.2, ...), kind=kLoop, calls=%fused_computation.112 | loop fusion | flops 3926016 | bytes 3207168 | tf_op jit(solution)/shard_map/reduce_sum | solution.py:75
  101.0 0.9 scatter_custom_fusion.1
  101.9 25.9 %psum.15 = f32[64,1,128]{2,0,1:T(8,128)S(1)} all-reduce(f32[64,1,128]{2,0,1:T(8,128)S(1)} %bitcast.273), channel_id=1, replica_groups=mesh['groups'=2,'seq'=4,'head'=2,'rep'=2] {'seq','rep'}, use_global_device_ids=true, to_apply=%region_33.36 | all-reduce | flops 8192 | bytes 65536 | tf_op jit(solution)/shard_map/psum | solution.py:80
  127.8 0.6 gather_fusion.14
  128.4 0.6 gather_fusion.13
  128.9 0.6 gather_fusion.12
  129.5 0.6 gather_fusion.11
  130.0 0.7 gather_fusion.10
  130.7 0.6 gather_fusion.9
  131.4 0.5 copy-done.24
  132.0 0.6 copy-done.22
  132.7 0.6 copy-done.20
  133.3 0.5 copy-done.18
  133.9 0.5 copy-done.16
  134.5 0.4 fusion.66
  134.9 1.8 %fusion.62 = (f32[8,128]{1,0:T(8,128)S(1)}, f32[8,128]{1,0:T(8,128)S(1)}, f32[8,128]{1,0:T(8,128)S(1)}, f32[8,128]{1,0:T(8,128)S(1)}, f32[8,128]{1,0:T(8,128)S(1)}) fusion(f32[8,128]{1,0:T(8,128)S(1)} %fusion.117, f32[8,128]{1,0:T(8,128)S(1)} %add_add_fusion.1, f32[8,128]{1,0:T(8,128)S(1)} %fusion.123, f32[8,128]{1,0:T(8,128)S(1)} %add_add_fusion.2, ...), kind=kLoop, calls=%fused_computation.119 | loop fusion | flops 3927040 | bytes 2695168 | tf_op jit(solution)/shard_map/reduce_sum | solution.py:33
  136.7 0.9 fusion.72
  137.8 0.9 convolution_add_fusion.4
  138.7 0.1 copy-done.4
  138.8 0.9 convolution_add_fusion.3
  139.8 0.1 copy-done.8
  139.9 0.9 convolution_add_fusion.2
  140.9 0.9 convolution_add_fusion.1
  142.0 1.3 fusion.12
  (80 shorter events, 1.8 us)
Async XLA Ops:
  0.0 12.7 %copy-start = (bf16[1024,1,128]{2,0,1:T(8,128)(2,1)S(1)}, bf16[1024,1,128]{2,0,1:T(8,128)(2,1)}, u32[]{:S(2)}) copy-start(bf16[1024,1,128]{2,0,1:T(8,128)(2,1)} %param.8) | copy-start | bytes 786436
  0.0 1.1 copy-start.13
  1.1 40.3 %copy-start.1 = (bf16[1024,1,256]{2,0,1:T(8,128)(2,1)}, bf16[1024,1,256]{2,0,1:T(8,128)(2,1)S(1)}, u32[]{:S(2)}) copy-start(bf16[1024,1,256]{2,0,1:T(8,128)(2,1)S(1)} %constant_dynamic-update-slice_fusion) | copy-start | bytes 1572868
  1.2 41.6 %collective-permute-start.2 = (bf16[1024,1,256]{2,0,1:T(8,128)(2,1)S(1)}, bf16[1024,1,256]{2,0,1:T(8,128)(2,1)S(1)}, u32[]{:S(2)}, u32[]{:S(2)}) collective-permute-start(bf16[1024,1,256]{2,0,1:T(8,128)(2,1)S(1)} %constant_dynamic-update-slice_fusion), channel_id=1, source_target_pairs={{0,12},{1,13},{4,0},{5,1},{8,4},{9,5},{12,8},{13,9},{2,14},{3,15},... | collective-permute-start | bytes 1572872 | tf_op jit(solution)/shard_map/ppermute | solution.py:29
  6.3 41.1 %collective-permute-start.4 = (bf16[1024,1,256]{2,0,1:T(8,128)(2,1)S(1)}, bf16[1024,1,256]{2,0,1:T(8,128)(2,1)}, u32[]{:S(2)}, u32[]{:S(2)}) collective-permute-start(bf16[1024,1,256]{2,0,1:T(8,128)(2,1)S(1)} %constant_dynamic-update-slice_fusion), channel_id=1, source_target_pairs={{0,8},{1,9},{4,12},{5,13},{8,0},{9,1},{12,4},{13,5},{2,10},{3,11},... | collective-permute-start | bytes 1572872 | tf_op jit(solution)/shard_map/ppermute | solution.py:29
  6.3 43.7 %collective-permute-start.3 = (bf16[1024,1,256]{2,0,1:T(8,128)(2,1)S(1)}, bf16[1024,1,256]{2,0,1:T(8,128)(2,1)}, u32[]{:S(2)}, u32[]{:S(2)}) collective-permute-start(bf16[1024,1,256]{2,0,1:T(8,128)(2,1)S(1)} %constant_dynamic-update-slice_fusion), channel_id=1, source_target_pairs={{0,9},{1,12},{4,13},{5,0},{8,1},{9,4},{12,5},{13,8},{2,11},{3,14},... | collective-permute-start | bytes 1572872 | tf_op jit(solution)/shard_map/ppermute | solution.py:29
  8.1 33.3 %collective-permute-start.1 = (bf16[128,1,256]{2,0,1:T(8,128)(2,1)S(1)}, bf16[128,1,256]{2,0,1:T(8,128)(2,1)S(1)}, u32[]{:S(2)}, u32[]{:S(2)}) collective-permute-start(bf16[128,1,256]{2,0,1:T(8,128)(2,1)S(1)} %get-tuple-element.58), channel_id=1, source_target_pairs={{1,0},{4,1},{5,4},{8,5},{9,8},{12,9},{13,12},{0,13},{3,2},{6,3},{7... | collective-permute-start | bytes 196616 | tf_op jit(solution)/shard_map/ppermute | solution.py:22
  10.4 31.0 %collective-permute-start = (bf16[128,1,256]{2,0,1:T(8,128)(2,1)S(1)}, bf16[128,1,256]{2,0,1:T(8,128)(2,1)S(1)}, u32[]{:S(2)}, u32[]{:S(2)}) collective-permute-start(bf16[128,1,256]{2,0,1:T(8,128)(2,1)S(1)} %get-tuple-element.59), channel_id=1, source_target_pairs={{0,1},{1,4},{4,5},{5,8},{8,9},{9,12},{12,13},{13,0},{2,3},{3,6},{6... | collective-permute-start | bytes 196616 | tf_op jit(solution)/shard_map/ppermute | solution.py:19
  10.4 0.7 copy-start.27
  11.9 85.7 %copy-start.19 = (pred[8]{0:T(512)(128)(4,1)}, pred[8]{0:T(512)(128)(4,1)S(1)}, u32[]{:S(2)}) copy-start(pred[8]{0:T(512)(128)(4,1)S(1)} %get-tuple-element.68) | copy-start | bytes 28
  11.9 85.8 %copy-start.17 = (pred[8]{0:T(512)(128)(4,1)}, pred[8]{0:T(512)(128)(4,1)S(1)}, u32[]{:S(2)}) copy-start(pred[8]{0:T(512)(128)(4,1)S(1)} %get-tuple-element.72) | copy-start | bytes 28
  11.9 85.8 %copy-start.15 = (pred[8]{0:T(512)(128)(4,1)}, pred[8]{0:T(512)(128)(4,1)S(1)}, u32[]{:S(2)}) copy-start(pred[8]{0:T(512)(128)(4,1)S(1)} %get-tuple-element.70) | copy-start | bytes 28
  12.7 81.7 %copy-start.14 = (s32[1024]{0:T(1024)}, s32[1024]{0:T(1024)S(1)}, u32[]{:S(2)}) copy-start(s32[1024]{0:T(1024)S(1)} %get-tuple-element.96) | copy-start | bytes 12292
  41.5 0.8 copy-start.5
  41.5 1.0 copy-start.3
  43.5 0.8 copy-start.7
  49.1 0.8 copy-start.9
  51.7 0.8 copy-start.11
  95.5 0.6 copy-start.25
  96.1 0.6 copy-start.23
  96.8 0.7 copy-start.21
  130.7 0.6 copy-start.26
  131.3 0.6 copy-start.24
  131.9 0.7 copy-start.22
  132.6 0.7 copy-start.20
  133.3 0.6 copy-start.18
  133.8 0.6 copy-start.16
  134.9 1.8 %copy-start.2 = (bf16[1024,1,256]{2,0,1:T(8,128)(2,1)S(1)}, bf16[1024,1,256]{2,0,1:T(8,128)(2,1)}, u32[]{:S(2)}) copy-start(bf16[1024,1,256]{2,0,1:T(8,128)(2,1)} %copy-done.1) | copy-start | bytes 1572868
  136.7 1.0 copy-start.6
  137.8 1.0 copy-start.4
  138.8 1.0 copy-start.8
  139.9 1.0 copy-start.12
  140.9 1.0 copy-start.10
where the time goes:
time: 144 us; the launch traced here: 143 us
  blocking collectives  63.1 us (44%)
  waiting for transfers between devices  31.5 us (22%)
  local copies, waits for them, and re-layouts  20 us (14%)
  other arithmetic  11.1 us (8%)
  starting transfers between devices  9.26 us (6%)
  matrix products  7.77 us (5%)
    psum x2, blocking collectives, body(): full_sums = lax.psum(full_sums, ('seq', 'rep'))  63.1 us
    ppermute x1, waiting for transfers between devices, with_halo(): lax.ppermute(lax.slice_in_dim(block, 0, width, axis=dim), axis, backward)  28.4 us
    unnamed x57, local copies, waits for them, and re-layouts  9.06 us
    ppermute x3, starting transfers between devices, shifted(): lax.ppermute(x, axis, [(i, (i + by) % devices) for i in range(devices)])  6.91 us
    gather x12, local copies, waits for them, and re-layouts, body(): jnp.take(full_sums, key_index[:, slot], axis=0)  6.79 us
    dot_general x6, matrix products, body(): jnp.einsum('ihqu,iuhd->iqhd', weight.astype(jnp.bfloat16), key_block[...,...  5.92 us
    reduce_sum x4, other arithmetic, normalize_rows(): totals = reduce(jnp.add, [weight.sum(-1) for weight in weights])  3.91 us
    gather x3, local copies, waits for them, and re-layouts, body(): slot_keys.append(jnp.take(shaped, far_local[slot_num], axis=0))  3.82 us
  transfers between devices with their start and end apart: 5, of which 2 were waited for; matrix products, arithmetic and copies ran while one was open for 4% of the time, Pallas kernels for 0%

commit v1 on v0

v1 whole, which is shorter than its diff:
```python
import math

import jax
import jax.numpy as jnp
from jax import lax
from jax.experimental import pallas as pl
from jax.experimental.pallas import tpu as pltpu
from jax.sharding import PartitionSpec as P

BLOCK = 128
ITERS = 2
VMEM = pl.BlockSpec(memory_space=pltpu.VMEM)
SMEM = pl.BlockSpec(memory_space=pltpu.SMEM)
LIMIT = 32 * 1024 * 1024


def block_rows(ref, index):
    start = index * BLOCK
    if not isinstance(index, int):
        start = pl.multiple_of(start, BLOCK)
    return ref[pl.ds(start, BLOCK), :]


def slot_blocks(i, blocks, within_ref, own, low, high, fars):
    before = low[...] if i == 0 else block_rows(own, i - 1)
    after = high[...] if i == blocks - 1 else block_rows(own, i + 1)
    listed = [block_rows(own, i), before, after]
    for slot, far in enumerate(fars):
        listed.append(block_rows(far, within_ref[i, slot]))
    return listed


def add_columns(sums_ref, index_ref, i, weights):
    for slot, weight in enumerate(weights):
        at = pl.ds(index_ref[i, slot], 1)
        sums_ref[at, :] += jnp.sum(weight, axis=0, keepdims=True)


def row_total(parts):
    total = parts[0]
    for part in parts[1:]:
        total = total + part
    return jnp.sum(total, axis=1, keepdims=True)


def score_kernel(blocks, index_ref, within_ref, bias_ref, q_ref, own, low, high, *rest):
    fars, (exp_ref, sums_ref) = rest[:-2], rest[-2:]
    sums_ref[...] = jnp.zeros_like(sums_ref)
    for i in range(blocks):
        query = block_rows(q_ref, i)
        scores = []
        for slot, key in enumerate(slot_blocks(i, blocks, within_ref, own, low, high, fars)):
            score = lax.dot_general(
                query, key, (((1,), (1,)), ((), ())), preferred_element_type=jnp.float32
            )
            scores.append(score * (1.0 / math.sqrt(key.shape[1])) + bias_ref[i, slot])
        peak = scores[0]
        for score in scores[1:]:
            peak = jnp.maximum(peak, score)
        peak = jnp.max(peak, axis=1, keepdims=True)
        exps = [jnp.exp(score - peak) for score in scores]
        for slot, value in enumerate(exps):
            exp_ref[i, slot] = value
        scale = 1.0 / row_total(exps)
        add_columns(sums_ref, index_ref, i, [value * scale for value in exps])


def scaled(exp_ref, index_ref, i, factor_refs):
    parts = []
    for slot in range(exp_ref.shape[1]):
        value = exp_ref[i, slot]
        for factor in factor_refs:
            value = value * factor[pl.ds(index_ref[i, slot], 1), :]
        parts.append(value)
    return parts


def round_kernel(blocks, index_ref, exp_ref, sum_a, sum_b, factor_ref, sums_ref):
    factor_ref[...] = 1.0 / (sum_a[...] + sum_b[...])
    sums_ref[...] = jnp.zeros_like(sums_ref)
    for i in range(blocks):
        parts = scaled(exp_ref, index_ref, i, [factor_ref])
        scale = 1.0 / row_total(parts)
        add_columns(sums_ref, index_ref, i, [part * scale for part in parts])


def output_kernel(
    blocks, index_ref, within_ref, exp_ref, factor_ref, sum_a, sum_b, own, low, high, *rest
):
    fars, (out_ref, last_ref) = rest[:-2], rest[-2:]
    last_ref[...] = 1.0 / (sum_a[...] + sum_b[...])
    for i in range(blocks):
        parts = scaled(exp_ref, index_ref, i, [factor_ref, last_ref])
        scale = 1.0 / row_total(parts)
        total = None
        for part, value in zip(
            parts, slot_blocks(i, blocks, within_ref, own, low, high, fars)
        ):
            term = jnp.dot(
                (part * scale).astype(jnp.bfloat16), value, preferred_element_type=jnp.float32
            )
            total = term if total is None else total + term
        out_ref[pl.ds(i * BLOCK, BLOCK), :] = total.astype(out_ref.dtype)


def shifted(x, axis, by):
    devices = lax.axis_size(axis)
    return lax.ppermute(x, axis, [(i, (i + by) % devices) for i in range(devices)])


def swapped(x):
    return lax.ppermute(x, "rep", [(0, 1), (1, 0)])


def over_seq(x):
    devices = lax.axis_size("seq")
    if devices <= 4:
        parts = [
            lax.ppermute(x, "seq", [(i, i ^ by) for i in range(devices)])
            for by in reversed(range(1, devices))
        ]
        for part in parts:
            x = x + part
        return x
    by = 1
    while by < devices:
        x = x + lax.ppermute(x, "seq", [(i, i ^ by) for i in range(devices)])
        by *= 2
    return x


def far_rows(x, rep):
    near = shifted(x, "seq", -1)
    beyond = shifted(x, "seq", -2)
    other = swapped(jnp.where(rep == 0, beyond, near))
    return near, other, beyond


def body(queries, key_rows, value_rows, pattern):
    tok_local, heads_local, width = queries.shape
    assert heads_local == 1
    blocks = tok_local // BLOCK
    list_len = pattern.shape[1]
    far_count = list_len - 3
    total_blocks = pattern.shape[0]
    axes = ("seq", "rep")
    shards = lax.axis_size(axes)
    position = lax.axis_index(axes)
    rep = lax.axis_index("rep")
    q = queries.reshape(tok_local, width)
    k = key_rows.reshape(tok_local, width)
    v = value_rows.reshape(tok_local, width)

    my_lists = lax.dynamic_slice_in_dim(pattern, position * blocks, blocks, 0)
    present = my_lists >= 0
    index = jnp.where(present, my_lists, 0)
    source = (position + 2 + jnp.arange(far_count, dtype=jnp.int32)) % shards
    within = jnp.where(present[:, 3:], my_lists[:, 3:] - source[None, :] * blocks, 0)
    bias = jnp.where(present, 0.0, -jnp.inf).astype(jnp.float32)

    k_far = far_rows(k, rep)
    edges_low = jnp.concatenate([k[-BLOCK:], v[-BLOCK:]], axis=1)
    edges_high = jnp.concatenate([k[:BLOCK], v[:BLOCK]], axis=1)
    low = shifted(edges_low, axes, 1)
    high = shifted(edges_high, axes, -1)

    exps, sums = pl.pallas_call(
        lambda *refs: score_kernel(blocks, *refs),
        out_shape=(
            jax.ShapeDtypeStruct((blocks, list_len, BLOCK, BLOCK), jnp.float32),
            jax.ShapeDtypeStruct((total_blocks, BLOCK), jnp.float32),
        ),
        in_specs=[SMEM] * 3 + [VMEM] * (4 + far_count),
        out_specs=(VMEM, VMEM),
        compiler_params=pltpu.CompilerParams(vmem_limit_bytes=LIMIT),
    )(index, within, bias, q, k, low[:, :width], high[:, :width], *k_far)

    v_in, sums = lax.optimization_barrier((v, sums))
    mine = over_seq(sums)
    v_far = far_rows(v_in, rep)
    factor, sums = pl.pallas_call(
        lambda *refs: round_kernel(blocks, *refs),
        out_shape=(
            jax.ShapeDtypeStruct((total_blocks, BLOCK), jnp.float32),
            jax.ShapeDtypeStruct((total_blocks, BLOCK), jnp.float32),
        ),
        in_specs=[SMEM] + [VMEM] * 3,
        out_specs=(VMEM, VMEM),
        compiler_params=pltpu.CompilerParams(vmem_limit_bytes=LIMIT),
    )(index, exps, mine, swapped(mine))

    mine = over_seq(sums)
    out = pl.pallas_call(
        lambda *refs: output_kernel(blocks, *refs),
        out_shape=jax.ShapeDtypeStruct((tok_local, width), jnp.bfloat16),
        in_specs=[SMEM] * 2 + [VMEM] * (7 + far_count),
        out_specs=VMEM,
        scratch_shapes=[pltpu.VMEM((total_blocks, BLOCK), jnp.float32)],
        compiler_params=pltpu.CompilerParams(vmem_limit_bytes=LIMIT),
    )(index, within, exps, factor, mine, swapped(mine), v, low[:, width:], high[:, width:], *v_far)
    return out.reshape(tok_local, heads_local, width)


def solution(mesh):
    in_specs = (
        P(("groups", "seq", "rep"), "head", None),
        P(("groups", "seq", "rep"), "head", None),
        P(("groups", "seq", "rep"), "head", None),
        P("groups", None),
    )
    out_specs = P(("groups", "seq", "rep"), "head", None)
    return jax.shard_map(body, mesh=mesh, in_specs=in_specs, out_specs=out_specs, check_vma=False)
```

time: 144 us -> 60.6 us (0.42)
  blocking collectives: 63.1 us -> 0 us
  local copies, waits for them, and re-layouts: 20 us -> 3.69 us
  other arithmetic: 11.1 us -> 0.2 us
  starting transfers between devices: 9.26 us -> 19.5 us
  matrix products: 7.77 us -> 0 us
  Pallas kernels: 0 us -> 6 us
    psum x2 -> x0, blocking collectives: 63.1 us -> none  [body(): full_sums = lax.psum(full_sums, ('seq', 'rep'))]
    ppermute x2 -> x10, waiting for transfers between devices: 28.4 us -> 4.61 us  [the longest x4 3.64 us: swapped(): return lax.ppermute(x, 'rep', [(0, 1), (1, 0)])]
    ppermute x3 -> x6, waiting for transfers between devices: 3.08 us -> 26.2 us  [shifted(): lax.ppermute(x, axis, [(i, (i + by) % devices) for i in range(devices)])]
    gather x15 -> x0, local copies, waits for them, and re-layouts: 10.6 us -> none  [the longest x12 6.79 us: body(): jnp.take(full_sums, key_index[:, slot], axis=0)]
    dot_general x12 -> x0, matrix products: 7.77 us -> none  [the longest x6 5.92 us: body(): jnp.einsum('ihqu,iuhd->iqhd', weight.astype(jnp.bfloat16), key_block[...,...]
    ppermute x2 -> x10, starting transfers between devices: 2.36 us -> 10.1 us  [the longest x6 9.52 us: over_seq(): lax.ppermute(x, 'seq', [(i, i ^ by) for i in range(devices)])]
    unnamed x57 -> x9, local copies, waits for them, and re-layouts: 9.06 us -> 1.99 us
    reduce_sum x6 -> x0, other arithmetic: 6.7 us -> none  [the longest x4 3.91 us: normalize_rows(): totals = reduce(jnp.add, [weight.sum(-1) for weight in weights])]
  transfers between devices with their start and end apart: 5 -> 16, of which waited for: 2 -> 8; matrix products, arithmetic and copies ran while one was open for 4% -> 3% of each run, Pallas kernels for 0% -> 2%
where the time goes in v1:
time: 60.6 us; the launch traced here: 60.3 us
  waiting for transfers between devices  30.9 us (51%)
  starting transfers between devices  19.5 us (32%)
  Pallas kernels  6 us (10%)
  local copies, waits for them, and re-layouts  3.69 us (6%)
    ppermute x6, waiting for transfers between devices, shifted(): lax.ppermute(x, axis, [(i, (i + by) % devices) for i in range(devices)])  26.2 us
    ppermute x6, starting transfers between devices, over_seq(): lax.ppermute(x, 'seq', [(i, i ^ by) for i in range(devices)])  9.52 us
    ppermute x6, starting transfers between devices, shifted(): lax.ppermute(x, axis, [(i, (i + by) % devices) for i in range(devices)])  9.4 us
    ppermute x4, waiting for transfers between devices, swapped(): return lax.ppermute(x, 'rep', [(0, 1), (1, 0)])  3.64 us
    pallas_call x1, Pallas kernels, body(): pl.pallas_call(lambda *refs: score_kernel(blocks, *refs), out_shape=(jax....  2.49 us
    pallas_call x1, Pallas kernels, body(): pl.pallas_call(lambda *refs: output_kernel(blocks, *refs), out_shape=jax....  2.37 us
    unnamed x9, local copies, waits for them, and re-layouts  1.99 us
    slice x2, local copies, waits for them, and re-layouts, body(): edges_high = jnp.concatenate([k[:BLOCK], v[:BLOCK]], axis=1)  1.61 us
  transfers between devices with their start and end apart: 16, of which 8 were waited for; matrix products, arithmetic and copies ran while one was open for 3% of the time, Pallas kernels for 2%

profile of v1, /device:TPU:0, one launch (start us, length us, event | category | flops | bytes accessed | tf_op | source)
XLA Modules:
  0.0 60.3 jit_solution(9371938834852828676)
XLA Ops:
  0.0 0.0 copy-start
  0.0 5.0 %collective-permute-start.2 = (bf16[1024,128]{1,0:T(8,128)(2,1)}, bf16[1024,128]{1,0:T(8,128)(2,1)S(1)}, u32[]{:S(2)}, u32[]{:S(2)}) collective-permute-start(bf16[1024,128]{1,0:T(8,128)(2,1)} %bitcast.15), channel_id=1, source_target_pairs={{0,12},{4,0},{8,4},{12,8},{1,13},{5,1},{9,5},{13,9},{2,14},{6,2},{... | collective-permute-start | bytes 786440 | tf_op jit(solution)/shard_map/ppermute | solution.py:108
  5.1 0.0 collective-permute-start.3
  5.1 0.8 %slice_bitcast_fusion.1 = (bf16[128,128]{1,0:T(8,128)(2,1)S(1)}, bf16[128,128]{1,0:T(8,128)(2,1)S(1)}) fusion(bf16[1024,1,128]{2,0,1:T(8,128)(2,1)} %param.5), kind=kLoop, calls=%fused_computation.7 | loop fusion | bytes 131072 | tf_op jit(solution)/shard_map/slice | solution.py:163
  5.9 0.8 %slice_bitcast_fusion = (bf16[128,128]{1,0:T(8,128)(2,1)S(1)}, bf16[128,128]{1,0:T(8,128)(2,1)S(1)}) fusion(bf16[1024,1,128]{2,0,1:T(8,128)(2,1)} %param.6), kind=kLoop, calls=%fused_computation.6 | loop fusion | bytes 131072 | tf_op jit(solution)/shard_map/slice | solution.py:163
  6.7 0.1 collective-permute-start.1
  6.8 0.5 collective-permute-start
  7.3 0.0 copy-done
  7.3 0.1 constant_dynamic-slice_fusion
  7.4 0.1 copy.6
  7.5 0.1 subtract_select_fusion.refs_1_
  7.6 4.5 %collective-permute-done.2.refs_7_ = bf16[1024,128]{1,0:T(8,128)(2,1)S(1)} collective-permute-done((bf16[1024,128]{1,0:T(8,128)(2,1)}, bf16[1024,128]{1,0:T(8,128)(2,1)S(1)}, u32[]{:S(2)}, u32[]{:S(2)}) %collective-permute-start.2) | collective-permute-done | bytes 262176 | tf_op jit(solution)/shard_map/ppermute | solution.py:108
  12.1 10.6 %collective-permute-done.3.refs_9_ = bf16[1024,128]{1,0:T(8,128)(2,1)S(1)} collective-permute-done((bf16[1024,128]{1,0:T(8,128)(2,1)}, bf16[1024,128]{1,0:T(8,128)(2,1)S(1)}, u32[]{:S(2)}, u32[]{:S(2)}) %collective-permute-start.3) | collective-permute-done | bytes 262176 | tf_op jit(solution)/shard_map/ppermute | solution.py:108
  22.7 0.0 copy-start.1
  22.7 0.1 collective-permute-start.4
  22.8 0.0 collective-permute-done.1
  22.8 0.0 collective-permute-done
  22.8 1.5 %collective-permute-done.4.refs_8_ = bf16[1024,128]{1,0:T(8,128)(2,1)S(1)} collective-permute-done((bf16[1024,128]{1,0:T(8,128)(2,1)S(1)}, bf16[1024,128]{1,0:T(8,128)(2,1)S(1)}, u32[]{:S(2)}, u32[]{:S(2)}) %collective-permute-start.4) | collective-permute-done | bytes 262176 | tf_op jit(solution)/shard_map/ppermute | solution.py:112
  24.3 0.0 copy-start.2
  24.3 0.9 %copy-done.2 = bf16[1024,1,128]{2,0,1:T(8,128)(2,1)S(1)} copy-done((bf16[1024,1,128]{2,0,1:T(8,128)(2,1)S(1)}, bf16[1024,1,128]{2,0,1:T(8,128)(2,1)}, u32[]{:S(2)}) %copy-start.2) | copy-done | bytes 262168
  25.3 0.0 copy-start.3
  25.3 0.9 %copy-done.3 = bf16[1024,1,128]{2,0,1:T(8,128)(2,1)S(1)} copy-done((bf16[1024,1,128]{2,0,1:T(8,128)(2,1)S(1)}, bf16[1024,1,128]{2,0,1:T(8,128)(2,1)}, u32[]{:S(2)}) %copy-start.3) | copy-done | bytes 262168
  26.2 2.5 %shard_map.46 = (f32[8,6,128,128]{3,2,1,0:T(8,128)S(1)}, f32[64,128]{1,0:T(8,128)S(1)}) custom-call(s32[8,6]{1,0:T(8,128)S(1)} %broadcast_select_fusion.3.refs_0_, s32[8,3]{1,0:T(8,128)S(1)} %subtract_select_fusion.refs_1_, f32[8,6]{1,0:T(8,128)S(1)} %get-tuple-element.17.refs_2_, bf16[1024,128]{1,0:T(8,128)(2,1)S(1)} %bitcast.18, ...), custom_call_target="tpu_custom_call" | custom-call | tf_op jit(solution)/shard_map/pallas_call | solution.py:167
  28.7 4.4 %collective-permute-start.5 = (f32[64,128]{1,0:T(8,128)S(1)}, f32[64,128]{1,0:T(8,128)S(1)}, u32[]{:S(2)}, u32[]{:S(2)}) collective-permute-start(f32[64,128]{1,0:T(8,128)S(1)} %get-tuple-element.13), channel_id=1, source_target_pairs={{0,12},{4,8},{8,4},{12,0},{1,13},{5,9},{9,5},{13,1},{2,14},{6,10},... | collective-permute-start | bytes 98312 | tf_op jit(solution)/shard_map/ppermute | solution.py:119
  33.1 0.0 collective-permute-start.6
  33.1 0.6 %collective-permute-start.7 = (f32[64,128]{1,0:T(8,128)S(1)}, f32[64,128]{1,0:T(8,128)S(1)}, u32[]{:S(2)}, u32[]{:S(2)}) collective-permute-start(f32[64,128]{1,0:T(8,128)S(1)} %get-tuple-element.13), channel_id=1, source_target_pairs={{0,4},{4,0},{8,12},{12,8},{1,5},{5,1},{9,13},{13,9},{2,6},{6,2},{1... | collective-permute-start | bytes 98312 | tf_op jit(solution)/shard_map/ppermute | solution.py:119
  33.8 3.7 %collective-permute-start.13 = (bf16[1024,128]{1,0:T(8,128)(2,1)}, bf16[1024,128]{1,0:T(8,128)(2,1)S(1)}, u32[]{:S(2)}, u32[]{:S(2)}) collective-permute-start(bf16[1024,128]{1,0:T(8,128)(2,1)} %bitcast.12), channel_id=1, source_target_pairs={{0,12},{4,0},{8,4},{12,8},{1,13},{5,1},{9,5},{13,9},{2,14},{6,2},{... | collective-permute-start | bytes 786440 | tf_op jit(solution)/shard_map/ppermute | solution.py:108
  37.5 0.0 collective-permute-start.14
  37.5 0.0 collective-permute-done.5
  37.5 0.7 %collective-permute-done.6 = f32[64,128]{1,0:T(8,128)S(1)} collective-permute-done((f32[64,128]{1,0:T(8,128)S(1)}, f32[64,128]{1,0:T(8,128)S(1)}, u32[]{:S(2)}, u32[]{:S(2)}) %collective-permute-start.6) | collective-permute-done | bytes 32800 | tf_op jit(solution)/shard_map/ppermute | solution.py:119
  38.2 0.0 collective-permute-done.7
  38.2 0.1 collective-permute-start.8
  38.3 1.2 %collective-permute-done.8.refs_3_ = f32[64,128]{1,0:T(8,128)S(1)} collective-permute-done((f32[64,128]{1,0:T(8,128)S(1)}, f32[64,128]{1,0:T(8,128)S(1)}, u32[]{:S(2)}, u32[]{:S(2)}) %collective-permute-start.8) | collective-permute-done | bytes 32800 | tf_op jit(solution)/shard_map/ppermute | solution.py:112
  39.5 1.1 %shard_map.47 = (f32[64,128]{1,0:T(8,128)S(1)}, f32[64,128]{1,0:T(8,128)S(1)}) custom-call(s32[8,6]{1,0:T(8,128)S(1)} %broadcast_select_fusion.3.refs_0_, f32[8,6,128,128]{3,2,1,0:T(8,128)S(1)} %get-tuple-element.11.refs_1_.refs_2_, f32[64,128]{1,0:T(8,128)S(1)} %add_add_fusion.1.refs_2_, f32[64,128]{1,0:T(8,128)S(1)} %collective-permute-done.8.refs_3_), custom_call_target="tpu_custom_call" | custom-call | tf_op jit(solution)/shard_map/pallas_call | solution.py:181
  40.7 2.3 %collective-permute-start.10 = (f32[64,128]{1,0:T(8,128)S(1)}, f32[64,128]{1,0:T(8,128)S(1)}, u32[]{:S(2)}, u32[]{:S(2)}) collective-permute-start(f32[64,128]{1,0:T(8,128)S(1)} %get-tuple-element.15), channel_id=1, source_target_pairs={{0,8},{4,12},{8,0},{12,4},{1,9},{5,13},{9,1},{13,5},{2,10},{6,14},... | collective-permute-start | bytes 98312 | tf_op jit(solution)/shard_map/ppermute | solution.py:119
  43.0 0.0 collective-permute-start.11
  43.0 2.2 %collective-permute-start.9 = (f32[64,128]{1,0:T(8,128)S(1)}, f32[64,128]{1,0:T(8,128)S(1)}, u32[]{:S(2)}, u32[]{:S(2)}) collective-permute-start(f32[64,128]{1,0:T(8,128)S(1)} %get-tuple-element.15), channel_id=1, source_target_pairs={{0,12},{4,8},{8,4},{12,0},{1,13},{5,9},{9,5},{13,1},{2,14},{6,10},... | collective-permute-start | bytes 98312 | tf_op jit(solution)/shard_map/ppermute | solution.py:119
  45.1 0.0 collective-permute-done.13.refs_9_
  45.1 11.2 %collective-permute-done.14.refs_11_ = bf16[1024,128]{1,0:T(8,128)(2,1)S(1)} collective-permute-done((bf16[1024,128]{1,0:T(8,128)(2,1)}, bf16[1024,128]{1,0:T(8,128)(2,1)S(1)}, u32[]{:S(2)}, u32[]{:S(2)}) %collective-permute-start.14) | collective-permute-done | bytes 262176 | tf_op jit(solution)/shard_map/ppermute | solution.py:108
  56.3 0.1 collective-permute-start.15
  56.4 0.2 collective-permute-done.10
  56.6 0.0 collective-permute-done.11
  56.6 0.0 collective-permute-done.9
  56.7 0.3 collective-permute-start.12
  57.0 1.0 %collective-permute-done.12.refs_5_ = f32[64,128]{1,0:T(8,128)S(1)} collective-permute-done((f32[64,128]{1,0:T(8,128)S(1)}, f32[64,128]{1,0:T(8,128)S(1)}, u32[]{:S(2)}, u32[]{:S(2)}) %collective-permute-start.12) | collective-permute-done | bytes 32800 | tf_op jit(solution)/shard_map/ppermute | solution.py:112
  58.0 0.0 collective-permute-done.15.refs_10_
  58.0 0.0 copy-done.1
  58.0 2.4 %shard_map.48 = bf16[1024,128]{1,0:T(8,128)(2,1)} custom-call(s32[8,6]{1,0:T(8,128)S(1)} %broadcast_select_fusion.3.refs_0_, s32[8,3]{1,0:T(8,128)S(1)} %subtract_select_fusion.refs_1_, f32[8,6,128,128]{3,2,1,0:T(8,128)S(1)} %get-tuple-element.11.refs_1_.refs_2_, f32[64,128]{1,0:T(8,128)S(1)} %get-tuple-element.14.refs_3_, ...), custom_call_target="tpu_custom_call" | custom-call | tf_op jit(solution)/shard_map/pallas_call | solution.py:193
  (11 shorter events, 0.1 us)
Async XLA Ops:
  0.0 7.3 %copy-start = (s32[64,6]{0,1:T(8,128)S(1)}, s32[64,6]{0,1:T(8,128)}, u32[]{:S(2)}) copy-start(s32[64,6]{0,1:T(8,128)} %param.7) | copy-start | bytes 4612
  0.0 12.1 %collective-permute-start.2 = (bf16[1024,128]{1,0:T(8,128)(2,1)}, bf16[1024,128]{1,0:T(8,128)(2,1)S(1)}, u32[]{:S(2)}, u32[]{:S(2)}) collective-permute-start(bf16[1024,128]{1,0:T(8,128)(2,1)} %bitcast.15), channel_id=1, source_target_pairs={{0,12},{4,0},{8,4},{12,8},{1,13},{5,1},{9,5},{13,9},{2,14},{6,2},{... | collective-permute-start | bytes 786440 | tf_op jit(solution)/shard_map/ppermute | solution.py:108
  5.1 17.6 %collective-permute-start.3 = (bf16[1024,128]{1,0:T(8,128)(2,1)}, bf16[1024,128]{1,0:T(8,128)(2,1)S(1)}, u32[]{:S(2)}, u32[]{:S(2)}) collective-permute-start(bf16[1024,128]{1,0:T(8,128)(2,1)} %bitcast.16), channel_id=1, source_target_pairs={{0,8},{4,12},{8,0},{12,4},{1,9},{5,13},{9,1},{13,5},{2,10},{6,14},... | collective-permute-start | bytes 786440 | tf_op jit(solution)/shard_map/ppermute | solution.py:108
  6.7 16.1 %collective-permute-start.1 = (bf16[128,256]{1,0:T(8,128)(2,1)S(1)}, bf16[128,256]{1,0:T(8,128)(2,1)S(1)}, u32[]{:S(2)}, u32[]{:S(2)}) collective-permute-start(bf16[128,256]{1,0:T(8,128)(2,1)S(1)} %pad_maximum_fusion.1), channel_id=1, source_target_pairs={{0,13},{1,0},{4,1},{5,4},{8,5},{9,8},{12,9},{13,12},{2,15},{3,2},{... | collective-permute-start | bytes 196616 | tf_op jit(solution)/shard_map/ppermute | solution.py:108
  6.8 16.0 %collective-permute-start = (bf16[128,256]{1,0:T(8,128)(2,1)S(1)}, bf16[128,256]{1,0:T(8,128)(2,1)S(1)}, u32[]{:S(2)}, u32[]{:S(2)}) collective-permute-start(bf16[128,256]{1,0:T(8,128)(2,1)S(1)} %pad_maximum_fusion), channel_id=1, source_target_pairs={{0,1},{1,4},{4,5},{5,8},{8,9},{9,12},{12,13},{13,0},{2,3},{3,6},{6... | collective-permute-start | bytes 196616 | tf_op jit(solution)/shard_map/ppermute | solution.py:108
  22.7 35.3 %copy-start.1 = (bf16[1024,1,128]{2,0,1:T(8,128)(2,1)S(1)}, bf16[1024,1,128]{2,0,1:T(8,128)(2,1)}, u32[]{:S(2)}) copy-start(bf16[1024,1,128]{2,0,1:T(8,128)(2,1)} %param.6) | copy-start | bytes 786436
  22.7 1.6 %collective-permute-start.4 = (bf16[1024,128]{1,0:T(8,128)(2,1)S(1)}, bf16[1024,128]{1,0:T(8,128)(2,1)S(1)}, u32[]{:S(2)}, u32[]{:S(2)}) collective-permute-start(bf16[1024,128]{1,0:T(8,128)(2,1)S(1)} %broadcast_select_fusion.1), channel_id=1, source_target_pairs={{0,1},{1,0},{2,3},{3,2},{4,5},{5,4},{6,7},{7,6},{8,9},{9,8},{10,11... | collective-permute-start | bytes 786440 | tf_op jit(solution)/shard_map/ppermute | solution.py:112
  24.3 1.0 %copy-start.2 = (bf16[1024,1,128]{2,0,1:T(8,128)(2,1)S(1)}, bf16[1024,1,128]{2,0,1:T(8,128)(2,1)}, u32[]{:S(2)}) copy-start(bf16[1024,1,128]{2,0,1:T(8,128)(2,1)} %param.5) | copy-start | bytes 786436
  25.3 0.9 %copy-start.3 = (bf16[1024,1,128]{2,0,1:T(8,128)(2,1)S(1)}, bf16[1024,1,128]{2,0,1:T(8,128)(2,1)}, u32[]{:S(2)}) copy-start(bf16[1024,1,128]{2,0,1:T(8,128)(2,1)} %param.4) | copy-start | bytes 786436
  28.7 8.8 %collective-permute-start.5 = (f32[64,128]{1,0:T(8,128)S(1)}, f32[64,128]{1,0:T(8,128)S(1)}, u32[]{:S(2)}, u32[]{:S(2)}) collective-permute-start(f32[64,128]{1,0:T(8,128)S(1)} %get-tuple-element.13), channel_id=1, source_target_pairs={{0,12},{4,8},{8,4},{12,0},{1,13},{5,9},{9,5},{13,1},{2,14},{6,10},... | collective-permute-start | bytes 98312 | tf_op jit(solution)/shard_map/ppermute | solution.py:119
  33.1 5.1 %collective-permute-start.6 = (f32[64,128]{1,0:T(8,128)S(1)}, f32[64,128]{1,0:T(8,128)S(1)}, u32[]{:S(2)}, u32[]{:S(2)}) collective-permute-start(f32[64,128]{1,0:T(8,128)S(1)} %get-tuple-element.13), channel_id=1, source_target_pairs={{0,8},{4,12},{8,0},{12,4},{1,9},{5,13},{9,1},{13,5},{2,10},{6,14},... | collective-permute-start | bytes 98312 | tf_op jit(solution)/shard_map/ppermute | solution.py:119
  33.1 5.1 %collective-permute-start.7 = (f32[64,128]{1,0:T(8,128)S(1)}, f32[64,128]{1,0:T(8,128)S(1)}, u32[]{:S(2)}, u32[]{:S(2)}) collective-permute-start(f32[64,128]{1,0:T(8,128)S(1)} %get-tuple-element.13), channel_id=1, source_target_pairs={{0,4},{4,0},{8,12},{12,8},{1,5},{5,1},{9,13},{13,9},{2,6},{6,2},{1... | collective-permute-start | bytes 98312 | tf_op jit(solution)/shard_map/ppermute | solution.py:119
  33.8 11.4 %collective-permute-start.13 = (bf16[1024,128]{1,0:T(8,128)(2,1)}, bf16[1024,128]{1,0:T(8,128)(2,1)S(1)}, u32[]{:S(2)}, u32[]{:S(2)}) collective-permute-start(bf16[1024,128]{1,0:T(8,128)(2,1)} %bitcast.12), channel_id=1, source_target_pairs={{0,12},{4,0},{8,4},{12,8},{1,13},{5,1},{9,5},{13,9},{2,14},{6,2},{... | collective-permute-start | bytes 786440 | tf_op jit(solution)/shard_map/ppermute | solution.py:108
  37.5 18.8 %collective-permute-start.14 = (bf16[1024,128]{1,0:T(8,128)(2,1)}, bf16[1024,128]{1,0:T(8,128)(2,1)S(1)}, u32[]{:S(2)}, u32[]{:S(2)}) collective-permute-start(bf16[1024,128]{1,0:T(8,128)(2,1)} %bitcast.13), channel_id=1, source_target_pairs={{0,8},{4,12},{8,0},{12,4},{1,9},{5,13},{9,1},{13,5},{2,10},{6,14},... | collective-permute-start | bytes 786440 | tf_op jit(solution)/shard_map/ppermute | solution.py:108
  38.2 1.3 %collective-permute-start.8 = (f32[64,128]{1,0:T(8,128)S(1)}, f32[64,128]{1,0:T(8,128)S(1)}, u32[]{:S(2)}, u32[]{:S(2)}) collective-permute-start(f32[64,128]{1,0:T(8,128)S(1)} %add_add_fusion.1.refs_2_), channel_id=1, source_target_pairs={{0,1},{1,0},{2,3},{3,2},{4,5},{5,4},{6,7},{7,6},{8,9},{9,8},{10,11... | collective-permute-start | bytes 98312 | tf_op jit(solution)/shard_map/ppermute | solution.py:112
  40.7 16.0 %collective-permute-start.10 = (f32[64,128]{1,0:T(8,128)S(1)}, f32[64,128]{1,0:T(8,128)S(1)}, u32[]{:S(2)}, u32[]{:S(2)}) collective-permute-start(f32[64,128]{1,0:T(8,128)S(1)} %get-tuple-element.15), channel_id=1, source_target_pairs={{0,8},{4,12},{8,0},{12,4},{1,9},{5,13},{9,1},{13,5},{2,10},{6,14},... | collective-permute-start | bytes 98312 | tf_op jit(solution)/shard_map/ppermute | solution.py:119
  43.0 13.7 %collective-permute-start.11 = (f32[64,128]{1,0:T(8,128)S(1)}, f32[64,128]{1,0:T(8,128)S(1)}, u32[]{:S(2)}, u32[]{:S(2)}) collective-permute-start(f32[64,128]{1,0:T(8,128)S(1)} %get-tuple-element.15), channel_id=1, source_target_pairs={{0,4},{4,0},{8,12},{12,8},{1,5},{5,1},{9,13},{13,9},{2,6},{6,2},{1... | collective-permute-start | bytes 98312 | tf_op jit(solution)/shard_map/ppermute | solution.py:119
  43.0 13.7 %collective-permute-start.9 = (f32[64,128]{1,0:T(8,128)S(1)}, f32[64,128]{1,0:T(8,128)S(1)}, u32[]{:S(2)}, u32[]{:S(2)}) collective-permute-start(f32[64,128]{1,0:T(8,128)S(1)} %get-tuple-element.15), channel_id=1, source_target_pairs={{0,12},{4,8},{8,4},{12,0},{1,13},{5,9},{9,5},{13,1},{2,14},{6,10},... | collective-permute-start | bytes 98312 | tf_op jit(solution)/shard_map/ppermute | solution.py:119
  56.3 1.7 %collective-permute-start.15 = (bf16[1024,128]{1,0:T(8,128)(2,1)S(1)}, bf16[1024,128]{1,0:T(8,128)(2,1)S(1)}, u32[]{:S(2)}, u32[]{:S(2)}) collective-permute-start(bf16[1024,128]{1,0:T(8,128)(2,1)S(1)} %broadcast_select_fusion), channel_id=1, source_target_pairs={{0,1},{1,0},{2,3},{3,2},{4,5},{5,4},{6,7},{7,6},{8,9},{9,8},{10,11... | collective-permute-start | bytes 786440 | tf_op jit(solution)/shard_map/ppermute | solution.py:112
  56.7 1.3 %collective-permute-start.12 = (f32[64,128]{1,0:T(8,128)S(1)}, f32[64,128]{1,0:T(8,128)S(1)}, u32[]{:S(2)}, u32[]{:S(2)}) collective-permute-start(f32[64,128]{1,0:T(8,128)S(1)} %add_add_fusion.refs_4_), channel_id=1, source_target_pairs={{0,1},{1,0},{2,3},{3,2},{4,5},{5,4},{6,7},{7,6},{8,9},{9,8},{10,11... | collective-permute-start | bytes 98312 | tf_op jit(solution)/shard_map/ppermute | solution.py:112

commit v2 on v1

--- a/solution.py
+++ b/solution.py
@@ -21,13 +21,21 @@
     return ref[pl.ds(start, BLOCK), :]
 
 
-def slot_blocks(i, blocks, within_ref, own, low, high, fars):
+def near_blocks(i, blocks, own, low, high):
     before = low[...] if i == 0 else block_rows(own, i - 1)
     after = high[...] if i == blocks - 1 else block_rows(own, i + 1)
-    listed = [block_rows(own, i), before, after]
-    for slot, far in enumerate(fars):
-        listed.append(block_rows(far, within_ref[i, slot]))
-    return listed
+    return [block_rows(own, i), before, after]
+
+
+def far_blocks(i, within_ref, fars):
+    return [block_rows(far, within_ref[i, slot]) for slot, far in enumerate(fars)]
+
+
+def score(query, key):
+    product = lax.dot_general(
+        query, key, (((1,), (1,)), ((), ())), preferred_element_type=jnp.float32
+    )
+    return product * (1.0 / math.sqrt(key.shape[1]))
 
 
 def add_columns(sums_ref, index_ref, i, weights):
@@ -43,22 +51,30 @@
     return jnp.sum(total, axis=1, keepdims=True)
 
 
-def score_kernel(blocks, index_ref, within_ref, bias_ref, q_ref, own, low, high, *rest):
+def near_kernel(blocks, q_ref, own, score_ref):
+    for i in range(blocks):
+        query = block_rows(q_ref, i)
+        for slot, other in enumerate((i, i - 1, i + 1)):
+            if 0 <= other < blocks:
+                score_ref[i, slot] = score(query, block_rows(own, other))
+
+
+def score_kernel(blocks, index_ref, within_ref, bias_ref, q_ref, near_ref, low, high, *rest):
     fars, (exp_ref, sums_ref) = rest[:-2], rest[-2:]
+    near = near_ref.shape[1]
     sums_ref[...] = jnp.zeros_like(sums_ref)
     for i in range(blocks):
         query = block_rows(q_ref, i)
-        scores = []
-        for slot, key in enumerate(slot_blocks(i, blocks, within_ref, own, low, high, fars)):
-            score = lax.dot_general(
-                query, key, (((1,), (1,)), ((), ())), preferred_element_type=jnp.float32
-            )
-            scores.append(score * (1.0 / math.sqrt(key.shape[1])) + bias_ref[i, slot])
+        scores = [near_ref[i, 0]]
+        scores.append(score(query, low[...]) if i == 0 else near_ref[i, 1])
+        scores.append(score(query, high[...]) if i == blocks - 1 else near_ref[i, 2])
+        for slot, key in enumerate(far_blocks(i, within_ref, fars)):
+            scores.append(score(query, key) + bias_ref[i, near + slot])
         peak = scores[0]
-        for score in scores[1:]:
-            peak = jnp.maximum(peak, score)
+        for part in scores[1:]:
+            peak = jnp.maximum(peak, part)
         peak = jnp.max(peak, axis=1, keepdims=True)
-        exps = [jnp.exp(score - peak) for score in scores]
+        exps = [jnp.exp(part - peak) for part in scores]
         for slot, value in enumerate(exps):
             exp_ref[i, slot] = value
         scale = 1.0 / row_total(exps)
@@ -93,9 +109,8 @@
         parts = scaled(exp_ref, index_ref, i, [factor_ref, last_ref])
         scale = 1.0 / row_total(parts)
         total = None
-        for part, value in zip(
-            parts, slot_blocks(i, blocks, within_ref, own, low, high, fars)
-        ):
+        values = near_blocks(i, blocks, own, low, high) + far_blocks(i, within_ref, fars)
+        for part, value in zip(parts, values):
             term = jnp.dot(
                 (part * scale).astype(jnp.bfloat16), value, preferred_element_type=jnp.float32
             )
@@ -129,9 +144,13 @@
     return x
 
 
-def far_rows(x, rep):
+def far_rows(x):
     near = shifted(x, "seq", -1)
     beyond = shifted(x, "seq", -2)
+    return near, beyond
+
+
+def with_swap(near, beyond, rep):
     other = swapped(jnp.where(rep == 0, beyond, near))
     return near, other, beyond
 
@@ -158,12 +177,26 @@
     within = jnp.where(present[:, 3:], my_lists[:, 3:] - source[None, :] * blocks, 0)
     bias = jnp.where(present, 0.0, -jnp.inf).astype(jnp.float32)
 
-    k_far = far_rows(k, rep)
     edges_low = jnp.concatenate([k[-BLOCK:], v[-BLOCK:]], axis=1)
     edges_high = jnp.concatenate([k[:BLOCK], v[:BLOCK]], axis=1)
+    beyond = shifted(k, "seq", -2)
+    k_in, edges_low = lax.optimization_barrier((k, edges_low))
+    k_pair = (shifted(k_in, "seq", -1), beyond)
     low = shifted(edges_low, axes, 1)
     high = shifted(edges_high, axes, -1)
 
+    near_scores = pl.pallas_call(
+        lambda *refs: near_kernel(blocks, *refs),
+        out_shape=jax.ShapeDtypeStruct((blocks, 3, BLOCK, BLOCK), jnp.float32),
+        in_specs=[VMEM] * 2,
+        out_specs=VMEM,
+        cost_estimate=pl.CostEstimate(flops=100663296, bytes_accessed=4194304, transcendentals=0),
+        compiler_params=pltpu.CompilerParams(vmem_limit_bytes=LIMIT),
+    )(q, k)
+
+    near_scores, v_in, *k_pair = lax.optimization_barrier((near_scores, v, *k_pair))
+    v_near = shifted(v_in, "seq", -1)
+    k_far = with_swap(*k_pair, rep)
     exps, sums = pl.pallas_call(
         lambda *refs: score_kernel(blocks, *refs),
         out_shape=(
@@ -172,12 +205,15 @@
         ),
         in_specs=[SMEM] * 3 + [VMEM] * (4 + far_count),
         out_specs=(VMEM, VMEM),
-        compiler_params=pltpu.CompilerParams(vmem_limit_bytes=LIMIT),
-    )(index, within, bias, q, k, low[:, :width], high[:, :width], *k_far)
+        cost_estimate=pl.CostEstimate(flops=100663296, bytes_accessed=6291456, transcendentals=786432),
+        compiler_params=pltpu.CompilerParams(vmem_limit_bytes=LIMIT),
+    )(index, within, bias, q, near_scores, low[:, :width], high[:, :width], *k_far)
 
     v_in, sums = lax.optimization_barrier((v, sums))
     mine = over_seq(sums)
-    v_far = far_rows(v_in, rep)
+    v_beyond = shifted(v_in, "seq", -2)
+    mine, v_near = lax.optimization_barrier((mine, v_near))
+    v_far = with_swap(v_near, v_beyond, rep)
     factor, sums = pl.pallas_call(
         lambda *refs: round_kernel(blocks, *refs),
         out_shape=(
@@ -186,6 +222,7 @@
         ),
         in_specs=[SMEM] + [VMEM] * 3,
         out_specs=(VMEM, VMEM),
+        cost_estimate=pl.CostEstimate(flops=7864320, bytes_accessed=4194304, transcendentals=0),
         compiler_params=pltpu.CompilerParams(vmem_limit_bytes=LIMIT),
     )(index, exps, mine, swapped(mine))
 
@@ -196,6 +233,7 @@
         in_specs=[SMEM] * 2 + [VMEM] * (7 + far_count),
         out_specs=VMEM,
         scratch_shapes=[pltpu.VMEM((total_blocks, BLOCK), jnp.float32)],
+        cost_estimate=pl.CostEstimate(flops=201326592, bytes_accessed=6291456, transcendentals=0),
         compiler_params=pltpu.CompilerParams(vmem_limit_bytes=LIMIT),
     )(index, within, exps, factor, mine, swapped(mine), v, low[:, width:], high[:, width:], *v_far)
     return out.reshape(tok_local, heads_local, width)

time: 60.6 us -> 56.7 us (0.936)
  waiting for transfers between devices: 30.9 us -> 14.3 us
  starting transfers between devices: 19.5 us -> 31.8 us
    ppermute x6, waiting for transfers between devices: 26.2 us -> 5.39 us  [shifted(): lax.ppermute(x, axis, [(i, (i + by) % devices) for i in range(devices)])]
    ppermute x6, starting transfers between devices: 9.4 us -> 16.4 us  [shifted(): lax.ppermute(x, axis, [(i, (i + by) % devices) for i in range(devices)])]
    ppermute x6, starting transfers between devices: 9.52 us -> 15.1 us  [over_seq(): lax.ppermute(x, 'seq', [(i, i ^ by) for i in range(devices)])]
    ppermute x6, waiting for transfers between devices: 0.96 us -> 6.51 us  [over_seq(): lax.ppermute(x, 'seq', [(i, i ^ by) for i in range(devices)])]
    ppermute x4, waiting for transfers between devices: 3.64 us -> 2.39 us  [swapped(): return lax.ppermute(x, 'rep', [(0, 1), (1, 0)])]
    pallas_call x0 -> x1, Pallas kernels: none -> 0.62 us  [body(): pl.pallas_call(lambda *refs: near_kernel(blocks, *refs), out_shape=jax.Sh...]
  transfers between devices with their start and end apart: 16 -> 16, of which waited for: 8 -> 7; matrix products, arithmetic and copies ran while one was open for 3% -> 3% of each run, Pallas kernels for 2% -> 7%
where the time goes in v2:
time: 56.7 us; the launch traced here: 56.4 us
  starting transfers between devices  31.8 us (56%)
  waiting for transfers between devices  14.3 us (25%)
  Pallas kernels  6.3 us (11%)
  local copies, waits for them, and re-layouts  3.65 us (6%)
    ppermute x6, starting transfers between devices, shifted(): lax.ppermute(x, axis, [(i, (i + by) % devices) for i in range(devices)])  16.4 us
    ppermute x6, starting transfers between devices, over_seq(): lax.ppermute(x, 'seq', [(i, i ^ by) for i in range(devices)])  15.1 us
    ppermute x6, waiting for transfers between devices, over_seq(): lax.ppermute(x, 'seq', [(i, i ^ by) for i in range(devices)])  6.51 us
    ppermute x6, waiting for transfers between devices, shifted(): lax.ppermute(x, axis, [(i, (i + by) % devices) for i in range(devices)])  5.39 us
    ppermute x4, waiting for transfers between devices, swapped(): return lax.ppermute(x, 'rep', [(0, 1), (1, 0)])  2.39 us
    pallas_call x1, Pallas kernels, body(): pl.pallas_call(lambda *refs: output_kernel(blocks, *refs), out_shape=jax....  2.38 us
    pallas_call x1, Pallas kernels, body(): pl.pallas_call(lambda *refs: score_kernel(blocks, *refs), out_shape=(jax....  2.14 us
    unnamed x9, local copies, waits for them, and re-layouts  1.99 us
  transfers between devices with their start and end apart: 16, of which 7 were waited for; matrix products, arithmetic and copies ran while one was open for 3% of the time, Pallas kernels for 7%

profile of v2, /device:TPU:0, one launch (start us, length us, event | category | flops | bytes accessed | tf_op | source)
XLA Modules:
  0.0 56.4 jit_solution(3158970289046935840)
XLA Ops:
  0.0 0.0 copy-start
  0.0 0.0 copy-start.2
  0.0 4.0 %collective-permute-start.1 = (bf16[1024,128]{1,0:T(8,128)(2,1)}, bf16[1024,128]{1,0:T(8,128)(2,1)S(1)}, u32[]{:S(2)}, u32[]{:S(2)}) collective-permute-start(bf16[1024,128]{1,0:T(8,128)(2,1)} %bitcast.17), channel_id=1, source_target_pairs={{0,8},{4,12},{8,0},{12,4},{1,9},{5,13},{9,1},{13,5},{2,10},{6,14},... | collective-permute-start | bytes 786440 | tf_op jit(solution)/shard_map/ppermute | solution.py:123
  4.0 0.8 %slice_bitcast_fusion.1 = (bf16[128,128]{1,0:T(8,128)(2,1)S(1)}, bf16[128,128]{1,0:T(8,128)(2,1)S(1)}) fusion(bf16[1024,1,128]{2,0,1:T(8,128)(2,1)} %param.5), kind=kLoop, calls=%fused_computation.7 | loop fusion | bytes 131072 | tf_op jit(solution)/shard_map/slice | solution.py:181
  4.8 0.8 %slice_bitcast_fusion = (bf16[128,128]{1,0:T(8,128)(2,1)S(1)}, bf16[128,128]{1,0:T(8,128)(2,1)S(1)}) fusion(bf16[1024,1,128]{2,0,1:T(8,128)(2,1)} %param.6), kind=kLoop, calls=%fused_computation.6 | loop fusion | bytes 131072 | tf_op jit(solution)/shard_map/slice | solution.py:181
  5.6 1.4 %collective-permute-start = (bf16[1024,128]{1,0:T(8,128)(2,1)}, bf16[1024,128]{1,0:T(8,128)(2,1)S(1)}, u32[]{:S(2)}, u32[]{:S(2)}) collective-permute-start(bf16[1024,128]{1,0:T(8,128)(2,1)} %bitcast.18), channel_id=1, source_target_pairs={{0,12},{4,0},{8,4},{12,8},{1,13},{5,1},{9,5},{13,9},{2,14},{6,2},{... | collective-permute-start | bytes 786440 | tf_op jit(solution)/shard_map/ppermute | solution.py:123
  7.0 0.0 collective-permute-start.2
  7.0 3.6 %collective-permute-start.3 = (bf16[128,256]{1,0:T(8,128)(2,1)S(1)}, bf16[128,256]{1,0:T(8,128)(2,1)S(1)}, u32[]{:S(2)}, u32[]{:S(2)}) collective-permute-start(bf16[128,256]{1,0:T(8,128)(2,1)S(1)} %pad_maximum_fusion.1), channel_id=1, source_target_pairs={{0,13},{1,0},{4,1},{5,4},{8,5},{9,8},{12,9},{13,12},{2,15},{3,2},{... | collective-permute-start | bytes 196616 | tf_op jit(solution)/shard_map/ppermute | solution.py:123
  10.6 0.0 copy-done
  10.6 0.1 constant_dynamic-slice_fusion
  10.7 0.1 copy.6
  10.8 0.0 copy-start.1
  10.8 0.9 %copy-done.1 = bf16[1024,1,128]{2,0,1:T(8,128)(2,1)S(1)} copy-done((bf16[1024,1,128]{2,0,1:T(8,128)(2,1)S(1)}, bf16[1024,1,128]{2,0,1:T(8,128)(2,1)}, u32[]{:S(2)}) %copy-start.1) | copy-done | bytes 262168
  11.8 0.0 copy-start.3
  11.8 0.9 %copy-done.3 = bf16[1024,1,128]{2,0,1:T(8,128)(2,1)S(1)} copy-done((bf16[1024,1,128]{2,0,1:T(8,128)(2,1)S(1)}, bf16[1024,1,128]{2,0,1:T(8,128)(2,1)}, u32[]{:S(2)}) %copy-start.3) | copy-done | bytes 262168
  12.7 0.6 %shard_map.46.refs_4_ = f32[8,3,128,128]{3,2,1,0:T(8,128)S(1)} custom-call(bf16[1024,128]{1,0:T(8,128)(2,1)S(1)} %bitcast.12, bf16[1024,128]{1,0:T(8,128)(2,1)S(1)} %bitcast.19), custom_call_target="tpu_custom_call" | custom-call | flops 100663296 | bytes 4194304 | tf_op jit(solution)/shard_map/pallas_call | solution.py:188
  13.4 0.1 subtract_select_fusion.refs_1_
  13.4 5.4 %collective-permute-done.refs_7_ = bf16[1024,128]{1,0:T(8,128)(2,1)S(1)} collective-permute-done((bf16[1024,128]{1,0:T(8,128)(2,1)}, bf16[1024,128]{1,0:T(8,128)(2,1)S(1)}, u32[]{:S(2)}, u32[]{:S(2)}) %collective-permute-start) | collective-permute-done | bytes 262176 | tf_op jit(solution)/shard_map/ppermute | solution.py:123
  18.8 0.0 collective-permute-done.1.refs_9_
  18.9 0.1 collective-permute-start.4
  18.9 0.0 collective-permute-done.2
  19.0 0.0 collective-permute-done.3
  19.0 0.0 copy-done.2
  19.0 7.4 %collective-permute-start.8 = (bf16[1024,128]{1,0:T(8,128)(2,1)S(1)}, bf16[1024,128]{1,0:T(8,128)(2,1)S(1)}, u32[]{:S(2)}, u32[]{:S(2)}) collective-permute-start(bf16[1024,128]{1,0:T(8,128)(2,1)S(1)} %bitcast.14), channel_id=1, source_target_pairs={{0,12},{4,0},{8,4},{12,8},{1,13},{5,1},{9,5},{13,9},{2,14},{6,2},{... | collective-permute-start | bytes 786440 | tf_op jit(solution)/shard_map/ppermute | solution.py:123
  26.4 0.0 collective-permute-done.4.refs_8_
  26.4 2.1 %shard_map.47 = (f32[8,6,128,128]{3,2,1,0:T(8,128)S(1)}, f32[64,128]{1,0:T(8,128)S(1)}) custom-call(s32[8,6]{1,0:T(8,128)S(1)} %broadcast_select_fusion.3.refs_0_, s32[8,3]{1,0:T(8,128)S(1)} %subtract_select_fusion.refs_1_, f32[8,6]{1,0:T(8,128)S(1)} %get-tuple-element.33.refs_2_, bf16[1024,128]{1,0:T(8,128)(2,1)S(1)} %bitcast.13, ...), custom_call_target="tpu_custom_call" | custom-call | flops 100663296 | bytes 6291456 | tf_op jit(solution)/shard_map/pallas_call | solution.py:200
  28.5 1.5 %collective-permute-start.5 = (f32[64,128]{1,0:T(8,128)S(1)}, f32[64,128]{1,0:T(8,128)S(1)}, u32[]{:S(2)}, u32[]{:S(2)}) collective-permute-start(f32[64,128]{1,0:T(8,128)S(1)} %get-tuple-element.26), channel_id=1, source_target_pairs={{0,12},{4,8},{8,4},{12,0},{1,13},{5,9},{9,5},{13,1},{2,14},{6,10},... | collective-permute-start | bytes 98312 | tf_op jit(solution)/shard_map/ppermute | solution.py:134
  30.0 0.0 collective-permute-start.6
  30.0 3.0 %collective-permute-start.7 = (f32[64,128]{1,0:T(8,128)S(1)}, f32[64,128]{1,0:T(8,128)S(1)}, u32[]{:S(2)}, u32[]{:S(2)}) collective-permute-start(f32[64,128]{1,0:T(8,128)S(1)} %get-tuple-element.26), channel_id=1, source_target_pairs={{0,4},{4,0},{8,12},{12,8},{1,5},{5,1},{9,13},{13,9},{2,6},{6,2},{1... | collective-permute-start | bytes 98312 | tf_op jit(solution)/shard_map/ppermute | solution.py:134
  33.0 0.0 collective-permute-start.14
  33.0 1.5 %collective-permute-done.5 = f32[64,128]{1,0:T(8,128)S(1)} collective-permute-done((f32[64,128]{1,0:T(8,128)S(1)}, f32[64,128]{1,0:T(8,128)S(1)}, u32[]{:S(2)}, u32[]{:S(2)}) %collective-permute-start.5) | collective-permute-done | bytes 32800 | tf_op jit(solution)/shard_map/ppermute | solution.py:134
  34.5 0.9 %collective-permute-done.6 = f32[64,128]{1,0:T(8,128)S(1)} collective-permute-done((f32[64,128]{1,0:T(8,128)S(1)}, f32[64,128]{1,0:T(8,128)S(1)}, u32[]{:S(2)}, u32[]{:S(2)}) %collective-permute-start.6) | collective-permute-done | bytes 32800 | tf_op jit(solution)/shard_map/ppermute | solution.py:134
  35.4 0.0 collective-permute-done.7
  35.4 0.0 collective-permute-done.8.refs_9_
  35.4 0.1 collective-permute-start.9
  35.5 1.2 %collective-permute-done.9.refs_3_ = f32[64,128]{1,0:T(8,128)S(1)} collective-permute-done((f32[64,128]{1,0:T(8,128)S(1)}, f32[64,128]{1,0:T(8,128)S(1)}, u32[]{:S(2)}, u32[]{:S(2)}) %collective-permute-start.9) | collective-permute-done | bytes 32800 | tf_op jit(solution)/shard_map/ppermute | solution.py:127
  36.7 1.2 %shard_map.48 = (f32[64,128]{1,0:T(8,128)S(1)}, f32[64,128]{1,0:T(8,128)S(1)}) custom-call(s32[8,6]{1,0:T(8,128)S(1)} %broadcast_select_fusion.3.refs_0_, f32[8,6,128,128]{3,2,1,0:T(8,128)S(1)} %get-tuple-element.24.refs_1_.refs_2_, f32[64,128]{1,0:T(8,128)S(1)} %add_add_fusion.1.refs_2_, f32[64,128]{1,0:T(8,128)S(1)} %collective-permute-done.9.refs_3_), custom_call_target="tpu_custom_call" | custom-call | flops 7864320 | bytes 4194304 | tf_op jit(solution)/shard_map/pallas_call | solution.py:217
  37.9 10.0 %collective-permute-start.10 = (f32[64,128]{1,0:T(8,128)S(1)}, f32[64,128]{1,0:T(8,128)S(1)}, u32[]{:S(2)}, u32[]{:S(2)}) collective-permute-start(f32[64,128]{1,0:T(8,128)S(1)} %get-tuple-element.30), channel_id=1, source_target_pairs={{0,12},{4,8},{8,4},{12,0},{1,13},{5,9},{9,5},{13,1},{2,14},{6,10},... | collective-permute-start | bytes 98312 | tf_op jit(solution)/shard_map/ppermute | solution.py:134
  47.9 0.0 collective-permute-start.11
  47.9 0.6 %collective-permute-start.12 = (f32[64,128]{1,0:T(8,128)S(1)}, f32[64,128]{1,0:T(8,128)S(1)}, u32[]{:S(2)}, u32[]{:S(2)}) collective-permute-start(f32[64,128]{1,0:T(8,128)S(1)} %get-tuple-element.30), channel_id=1, source_target_pairs={{0,4},{4,0},{8,12},{12,8},{1,5},{5,1},{9,13},{13,9},{2,6},{6,2},{1... | collective-permute-start | bytes 98312 | tf_op jit(solution)/shard_map/ppermute | solution.py:134
  48.5 0.0 collective-permute-done.14.refs_11_
  48.6 0.1 collective-permute-start.15
  48.6 1.2 %collective-permute-done.10 = f32[64,128]{1,0:T(8,128)S(1)} collective-permute-done((f32[64,128]{1,0:T(8,128)S(1)}, f32[64,128]{1,0:T(8,128)S(1)}, u32[]{:S(2)}, u32[]{:S(2)}) %collective-permute-start.10) | collective-permute-done | bytes 32800 | tf_op jit(solution)/shard_map/ppermute | solution.py:134
  49.9 2.8 %collective-permute-done.11 = f32[64,128]{1,0:T(8,128)S(1)} collective-permute-done((f32[64,128]{1,0:T(8,128)S(1)}, f32[64,128]{1,0:T(8,128)S(1)}, u32[]{:S(2)}, u32[]{:S(2)}) %collective-permute-start.11) | collective-permute-done | bytes 32800 | tf_op jit(solution)/shard_map/ppermute | solution.py:134
  52.7 0.0 collective-permute-done.12
  52.7 0.1 collective-permute-start.13
  52.8 1.2 %collective-permute-done.13.refs_5_ = f32[64,128]{1,0:T(8,128)S(1)} collective-permute-done((f32[64,128]{1,0:T(8,128)S(1)}, f32[64,128]{1,0:T(8,128)S(1)}, u32[]{:S(2)}, u32[]{:S(2)}) %collective-permute-start.13) | collective-permute-done | bytes 32800 | tf_op jit(solution)/shard_map/ppermute | solution.py:127
  54.0 0.0 collective-permute-done.15.refs_10_
  54.0 2.4 %shard_map.49 = bf16[1024,128]{1,0:T(8,128)(2,1)} custom-call(s32[8,6]{1,0:T(8,128)S(1)} %broadcast_select_fusion.3.refs_0_, s32[8,3]{1,0:T(8,128)S(1)} %subtract_select_fusion.refs_1_, f32[8,6,128,128]{3,2,1,0:T(8,128)S(1)} %get-tuple-element.24.refs_1_.refs_2_, f32[64,128]{1,0:T(8,128)S(1)} %get-tuple-element.29.refs_3_, ...), custom_call_target="tpu_custom_call" | custom-call | flops 201326592 | bytes 6291456 | tf_op jit(solution)/shard_map/pallas_call | solution.py:230
  (11 shorter events, 0.1 us)
Async XLA Ops:
  0.0 10.6 %copy-start = (s32[64,6]{0,1:T(8,128)S(1)}, s32[64,6]{0,1:T(8,128)}, u32[]{:S(2)}) copy-start(s32[64,6]{0,1:T(8,128)} %param.7) | copy-start | bytes 4612
  0.0 19.0 %copy-start.2 = (bf16[1024,1,128]{2,0,1:T(8,128)(2,1)S(1)}, bf16[1024,1,128]{2,0,1:T(8,128)(2,1)}, u32[]{:S(2)}) copy-start(bf16[1024,1,128]{2,0,1:T(8,128)(2,1)} %param.6) | copy-start | bytes 786436
  0.0 18.8 %collective-permute-start.1 = (bf16[1024,128]{1,0:T(8,128)(2,1)}, bf16[1024,128]{1,0:T(8,128)(2,1)S(1)}, u32[]{:S(2)}, u32[]{:S(2)}) collective-permute-start(bf16[1024,128]{1,0:T(8,128)(2,1)} %bitcast.17), channel_id=1, source_target_pairs={{0,8},{4,12},{8,0},{12,4},{1,9},{5,13},{9,1},{13,5},{2,10},{6,14},... | collective-permute-start | bytes 786440 | tf_op jit(solution)/shard_map/ppermute | solution.py:123
  5.6 13.2 %collective-permute-start = (bf16[1024,128]{1,0:T(8,128)(2,1)}, bf16[1024,128]{1,0:T(8,128)(2,1)S(1)}, u32[]{:S(2)}, u32[]{:S(2)}) collective-permute-start(bf16[1024,128]{1,0:T(8,128)(2,1)} %bitcast.18), channel_id=1, source_target_pairs={{0,12},{4,0},{8,4},{12,8},{1,13},{5,1},{9,5},{13,9},{2,14},{6,2},{... | collective-permute-start | bytes 786440 | tf_op jit(solution)/shard_map/ppermute | solution.py:123
  7.0 11.9 %collective-permute-start.2 = (bf16[128,256]{1,0:T(8,128)(2,1)S(1)}, bf16[128,256]{1,0:T(8,128)(2,1)S(1)}, u32[]{:S(2)}, u32[]{:S(2)}) collective-permute-start(bf16[128,256]{1,0:T(8,128)(2,1)S(1)} %pad_maximum_fusion), channel_id=1, source_target_pairs={{0,1},{1,4},{4,5},{5,8},{8,9},{9,12},{12,13},{13,0},{2,3},{3,6},{6... | collective-permute-start | bytes 196616 | tf_op jit(solution)/shard_map/ppermute | solution.py:123
  7.0 11.9 %collective-permute-start.3 = (bf16[128,256]{1,0:T(8,128)(2,1)S(1)}, bf16[128,256]{1,0:T(8,128)(2,1)S(1)}, u32[]{:S(2)}, u32[]{:S(2)}) collective-permute-start(bf16[128,256]{1,0:T(8,128)(2,1)S(1)} %pad_maximum_fusion.1), channel_id=1, source_target_pairs={{0,13},{1,0},{4,1},{5,4},{8,5},{9,8},{12,9},{13,12},{2,15},{3,2},{... | collective-permute-start | bytes 196616 | tf_op jit(solution)/shard_map/ppermute | solution.py:123
  10.8 1.0 %copy-start.1 = (bf16[1024,1,128]{2,0,1:T(8,128)(2,1)S(1)}, bf16[1024,1,128]{2,0,1:T(8,128)(2,1)}, u32[]{:S(2)}) copy-start(bf16[1024,1,128]{2,0,1:T(8,128)(2,1)} %param.4) | copy-start | bytes 786436
  11.8 0.9 %copy-start.3 = (bf16[1024,1,128]{2,0,1:T(8,128)(2,1)S(1)}, bf16[1024,1,128]{2,0,1:T(8,128)(2,1)}, u32[]{:S(2)}) copy-start(bf16[1024,1,128]{2,0,1:T(8,128)(2,1)} %param.5) | copy-start | bytes 786436
  18.9 7.5 %collective-permute-start.4 = (bf16[1024,128]{1,0:T(8,128)(2,1)S(1)}, bf16[1024,128]{1,0:T(8,128)(2,1)S(1)}, u32[]{:S(2)}, u32[]{:S(2)}) collective-permute-start(bf16[1024,128]{1,0:T(8,128)(2,1)S(1)} %broadcast_select_fusion.1), channel_id=1, source_target_pairs={{0,1},{1,0},{2,3},{3,2},{4,5},{5,4},{6,7},{7,6},{8,9},{9,8},{10,11... | collective-permute-start | bytes 786440 | tf_op jit(solution)/shard_map/ppermute | solution.py:127
  19.0 16.4 %collective-permute-start.8 = (bf16[1024,128]{1,0:T(8,128)(2,1)S(1)}, bf16[1024,128]{1,0:T(8,128)(2,1)S(1)}, u32[]{:S(2)}, u32[]{:S(2)}) collective-permute-start(bf16[1024,128]{1,0:T(8,128)(2,1)S(1)} %bitcast.14), channel_id=1, source_target_pairs={{0,12},{4,0},{8,4},{12,8},{1,13},{5,1},{9,5},{13,9},{2,14},{6,2},{... | collective-permute-start | bytes 786440 | tf_op jit(solution)/shard_map/ppermute | solution.py:123
  28.5 6.0 %collective-permute-start.5 = (f32[64,128]{1,0:T(8,128)S(1)}, f32[64,128]{1,0:T(8,128)S(1)}, u32[]{:S(2)}, u32[]{:S(2)}) collective-permute-start(f32[64,128]{1,0:T(8,128)S(1)} %get-tuple-element.26), channel_id=1, source_target_pairs={{0,12},{4,8},{8,4},{12,0},{1,13},{5,9},{9,5},{13,1},{2,14},{6,10},... | collective-permute-start | bytes 98312 | tf_op jit(solution)/shard_map/ppermute | solution.py:134
  30.0 5.4 %collective-permute-start.6 = (f32[64,128]{1,0:T(8,128)S(1)}, f32[64,128]{1,0:T(8,128)S(1)}, u32[]{:S(2)}, u32[]{:S(2)}) collective-permute-start(f32[64,128]{1,0:T(8,128)S(1)} %get-tuple-element.26), channel_id=1, source_target_pairs={{0,8},{4,12},{8,0},{12,4},{1,9},{5,13},{9,1},{13,5},{2,10},{6,14},... | collective-permute-start | bytes 98312 | tf_op jit(solution)/shard_map/ppermute | solution.py:134
  30.0 5.4 %collective-permute-start.7 = (f32[64,128]{1,0:T(8,128)S(1)}, f32[64,128]{1,0:T(8,128)S(1)}, u32[]{:S(2)}, u32[]{:S(2)}) collective-permute-start(f32[64,128]{1,0:T(8,128)S(1)} %get-tuple-element.26), channel_id=1, source_target_pairs={{0,4},{4,0},{8,12},{12,8},{1,5},{5,1},{9,13},{13,9},{2,6},{6,2},{1... | collective-permute-start | bytes 98312 | tf_op jit(solution)/shard_map/ppermute | solution.py:134
  33.0 15.6 %collective-permute-start.14 = (bf16[1024,128]{1,0:T(8,128)(2,1)S(1)}, bf16[1024,128]{1,0:T(8,128)(2,1)S(1)}, u32[]{:S(2)}, u32[]{:S(2)}) collective-permute-start(bf16[1024,128]{1,0:T(8,128)(2,1)S(1)} %bitcast.15), channel_id=1, source_target_pairs={{0,8},{4,12},{8,0},{12,4},{1,9},{5,13},{9,1},{13,5},{2,10},{6,14},... | collective-permute-start | bytes 786440 | tf_op jit(solution)/shard_map/ppermute | solution.py:123
  35.4 1.3 %collective-permute-start.9 = (f32[64,128]{1,0:T(8,128)S(1)}, f32[64,128]{1,0:T(8,128)S(1)}, u32[]{:S(2)}, u32[]{:S(2)}) collective-permute-start(f32[64,128]{1,0:T(8,128)S(1)} %add_add_fusion.1.refs_2_), channel_id=1, source_target_pairs={{0,1},{1,0},{2,3},{3,2},{4,5},{5,4},{6,7},{7,6},{8,9},{9,8},{10,11... | collective-permute-start | bytes 98312 | tf_op jit(solution)/shard_map/ppermute | solution.py:127
  37.9 12.0 %collective-permute-start.10 = (f32[64,128]{1,0:T(8,128)S(1)}, f32[64,128]{1,0:T(8,128)S(1)}, u32[]{:S(2)}, u32[]{:S(2)}) collective-permute-start(f32[64,128]{1,0:T(8,128)S(1)} %get-tuple-element.30), channel_id=1, source_target_pairs={{0,12},{4,8},{8,4},{12,0},{1,13},{5,9},{9,5},{13,1},{2,14},{6,10},... | collective-permute-start | bytes 98312 | tf_op jit(solution)/shard_map/ppermute | solution.py:134
  47.9 4.8 %collective-permute-start.11 = (f32[64,128]{1,0:T(8,128)S(1)}, f32[64,128]{1,0:T(8,128)S(1)}, u32[]{:S(2)}, u32[]{:S(2)}) collective-permute-start(f32[64,128]{1,0:T(8,128)S(1)} %get-tuple-element.30), channel_id=1, source_target_pairs={{0,8},{4,12},{8,0},{12,4},{1,9},{5,13},{9,1},{13,5},{2,10},{6,14},... | collective-permute-start | bytes 98312 | tf_op jit(solution)/shard_map/ppermute | solution.py:134
  47.9 4.8 %collective-permute-start.12 = (f32[64,128]{1,0:T(8,128)S(1)}, f32[64,128]{1,0:T(8,128)S(1)}, u32[]{:S(2)}, u32[]{:S(2)}) collective-permute-start(f32[64,128]{1,0:T(8,128)S(1)} %get-tuple-element.30), channel_id=1, source_target_pairs={{0,4},{4,0},{8,12},{12,8},{1,5},{5,1},{9,13},{13,9},{2,6},{6,2},{1... | collective-permute-start | bytes 98312 | tf_op jit(solution)/shard_map/ppermute | solution.py:134
  48.6 5.4 %collective-permute-start.15 = (bf16[1024,128]{1,0:T(8,128)(2,1)S(1)}, bf16[1024,128]{1,0:T(8,128)(2,1)S(1)}, u32[]{:S(2)}, u32[]{:S(2)}) collective-permute-start(bf16[1024,128]{1,0:T(8,128)(2,1)S(1)} %broadcast_select_fusion), channel_id=1, source_target_pairs={{0,1},{1,0},{2,3},{3,2},{4,5},{5,4},{6,7},{7,6},{8,9},{9,8},{10,11... | collective-permute-start | bytes 786440 | tf_op jit(solution)/shard_map/ppermute | solution.py:127
  52.7 1.3 %collective-permute-start.13 = (f32[64,128]{1,0:T(8,128)S(1)}, f32[64,128]{1,0:T(8,128)S(1)}, u32[]{:S(2)}, u32[]{:S(2)}) collective-permute-start(f32[64,128]{1,0:T(8,128)S(1)} %add_add_fusion.refs_4_), channel_id=1, source_target_pairs={{0,1},{1,0},{2,3},{3,2},{4,5},{5,4},{6,7},{7,6},{8,9},{9,8},{10,11... | collective-permute-start | bytes 98312 | tf_op jit(solution)/shard_map/ppermute | solution.py:127

commit v3 on v2

v3 whole, which is shorter than its diff:
```python
import math

import jax
import jax.numpy as jnp
from jax import lax
from jax.experimental import pallas as pl
from jax.experimental.pallas import tpu as pltpu
from jax.sharding import PartitionSpec as P

BLOCK = 128
ITERS = 2
VMEM = pl.BlockSpec(memory_space=pltpu.VMEM)
ANY = pl.BlockSpec(memory_space=pl.ANY)
HBM = pl.BlockSpec(memory_space=pltpu.HBM)
SMEM = pl.BlockSpec(memory_space=pltpu.SMEM)
LIMIT = 32 * 1024 * 1024


def block_rows(ref, index):
    start = index * BLOCK
    if not isinstance(index, int):
        start = pl.multiple_of(start, BLOCK)
    return ref[pl.ds(start, BLOCK), :]


def near_blocks(i, blocks, own, low, high):
    before = low[...] if i == 0 else block_rows(own, i - 1)
    after = high[...] if i == blocks - 1 else block_rows(own, i + 1)
    return [block_rows(own, i), before, after]


def far_blocks(i, within_ref, fars):
    return [block_rows(far, within_ref[i, slot]) for slot, far in enumerate(fars)]


def score(query, key):
    product = lax.dot_general(
        query, key, (((1,), (1,)), ((), ())), preferred_element_type=jnp.float32
    )
    return product * (1.0 / math.sqrt(key.shape[1]))


def add_columns(sums_ref, lists_ref, i, weights):
    for slot, weight in enumerate(weights):
        at = pl.ds(jnp.maximum(lists_ref[i, slot], 0), 1)
        sums_ref[at, :] += jnp.sum(weight, axis=0, keepdims=True)


def row_total(parts):
    total = parts[0]
    for part in parts[1:]:
        total = total + part
    return jnp.sum(total, axis=1, keepdims=True)


def listed_bits(pattern_ref, blocks, shards, source, first_core):
    wanted = jnp.int32(0)
    for back, column, counted in ((4, 5, True), (3, 4, first_core)):
        if counted is False:
            continue
        first = (source + shards - back) % shards * blocks
        for i in range(blocks):
            entry = pattern_ref[column, first + i]
            bit = jnp.left_shift(jnp.int32(1), jnp.maximum(entry - source * blocks, 0))
            hit = entry >= 0 if counted is True else (entry >= 0) & counted
            wanted = jnp.where(hit, wanted | bit, wanted)
    return [jnp.bitwise_and(jnp.right_shift(wanted, b), 1) for b in range(blocks)]


class Copies:
    def __init__(self, sems):
        self.sems, self.started = sems, []

    def start(self, source, target):
        copy = pltpu.make_async_copy(source, target, self.sems.at[len(self.started)])
        copy.start()
        self.started.append(copy)

    def wait(self):
        for copy in self.started:
            copy.wait()


def pack(pattern_ref, blocks, shards, caps, rows, outs, order_ref, copies):
    position, rep = lax.axis_index(("seq", "rep")), lax.axis_index("rep")
    bits = listed_bits(pattern_ref, blocks, shards, position, rep == 0)
    rank, spare = jnp.int32(0), sum(bits)
    for b, bit in enumerate(bits):
        order_ref[jnp.where(bit == 1, rank, spare)] = b
        rank, spare = rank + bit, spare + 1 - bit
    for out, first in zip(outs, (0, 0, caps[1])):
        for t in range(out.shape[0] // BLOCK):
            begin = pl.multiple_of(order_ref[first + t] * BLOCK, BLOCK)
            copies.start(rows.at[pl.ds(begin, BLOCK), :], out.at[pl.ds(t * BLOCK, BLOCK), :])


def load(source, target, sem):
    copy = pltpu.make_async_copy(source, target, sem)
    copy.start()
    copy.wait()


def key_kernel(blocks, shards, caps, pattern_hbm, k_ref, *refs):
    outs, (pattern_ref, order_ref, sems, sem) = refs[:3], refs[3:]
    load(pattern_hbm, pattern_ref, sem)
    copies = Copies(sems)
    pack(pattern_ref, blocks, shards, caps, k_ref, outs, order_ref, copies)
    copies.wait()


def plan_kernel(blocks, shards, caps, pattern_hbm, k_ref, v_ref, *refs):
    outs, edges = refs[:3], refs[3:5]
    lists_ref, within_ref, crowded_ref, pattern_ref, order_ref, rank_ref, sems, sem = refs[5:]
    position, rep = lax.axis_index(("seq", "rep")), lax.axis_index("rep")
    width = k_ref.shape[1]
    copies = Copies(sems)
    for edge, begin in zip(edges, ((blocks - 1) * BLOCK, 0)):
        for at, rows in enumerate((k_ref, v_ref)):
            copies.start(rows.at[pl.ds(begin, BLOCK), :], edge.at[:, pl.ds(at * width, width)])
    load(pattern_hbm, pattern_ref, sem)
    pack(pattern_ref, blocks, shards, caps, v_ref, outs, order_ref, copies)
    for at, ahead in enumerate((3, 4)):
        source = lax.rem(position + ahead, shards)
        bits = listed_bits(
            pattern_ref, blocks, shards, source, (rep == 0) if ahead == 4 else True
        )
        rank = jnp.int32(0)
        for b, bit in enumerate(bits):
            rank_ref[at, b] = rank if ahead == 4 else jnp.where(rep == 1, rank, b)
            rank = rank + bit
    for i in range(blocks):
        for slot in range(pattern_ref.shape[0]):
            entry = pattern_ref[slot, position * blocks + i]
            lists_ref[i, slot] = entry
            if slot >= 3:
                source = lax.rem(position + slot - 1, shards)
                at = jnp.where(entry >= 0, entry - source * blocks, 0)
                within_ref[i, slot - 3] = at if slot == 3 else rank_ref[slot - 4, at]
    crowded = jnp.int32(0)
    for source in range(shards):
        count = sum(listed_bits(pattern_ref, blocks, shards, source, source % 2 == 0))
        crowded = jnp.maximum(crowded, jnp.where(count > caps[source % 2], 1, 0))
    crowded_ref[0] = crowded
    copies.wait()


def packed_shapes(blocks, caps, rows):
    sizes = (caps[0], caps[1], blocks - caps[1])
    return [jax.ShapeDtypeStruct((n * BLOCK, rows.shape[1]), rows.dtype) for n in sizes]


def pack_keys(blocks, shards, caps, columns, k):
    return pl.pallas_call(
        lambda *refs: key_kernel(blocks, shards, caps, *refs),
        out_shape=packed_shapes(blocks, caps, k),
        in_specs=[HBM] * 2,
        out_specs=[VMEM] * 3,
        scratch_shapes=[
            pltpu.SMEM(columns.shape, jnp.int32),
            pltpu.SMEM((blocks,), jnp.int32),
            pltpu.SemaphoreType.DMA((2 * blocks,)),
            pltpu.SemaphoreType.DMA,
        ],
    )(columns, k)


def plan(blocks, shards, caps, columns, k, v):
    width, list_len = k.shape[1], columns.shape[0]
    return pl.pallas_call(
        lambda *refs: plan_kernel(blocks, shards, caps, *refs),
        out_shape=packed_shapes(blocks, caps, v)
        + [jax.ShapeDtypeStruct((BLOCK, 2 * width), k.dtype)] * 2
        + [
            jax.ShapeDtypeStruct((blocks, list_len), jnp.int32),
            jax.ShapeDtypeStruct((blocks, list_len - 3), jnp.int32),
            jax.ShapeDtypeStruct((1,), jnp.int32),
        ],
        in_specs=[HBM] * 3,
        out_specs=[VMEM] * 5 + [SMEM] * 3,
        scratch_shapes=[
            pltpu.SMEM(columns.shape, jnp.int32),
            pltpu.SMEM((blocks,), jnp.int32),
            pltpu.SMEM((2, blocks), jnp.int32),
            pltpu.SemaphoreType.DMA((2 * blocks + 4,)),
            pltpu.SemaphoreType.DMA,
        ],
    )(columns, k, v)


def gather(rep, caps, wide, slim, rest, whole, sems, act):
    for core, first, skip in ((0, wide, caps[0] - caps[1]), (1, slim, 0)):

        @pl.when(rep == core)
        def _():
            used = first.shape[0]
            left = whole.shape[0] - used
            act(pltpu.make_async_copy(first, whole.at[pl.ds(0, used), :], sems.at[0]))
            act(
                pltpu.make_async_copy(
                    rest.at[pl.ds(skip * BLOCK, left), :], whole.at[pl.ds(used, left), :], sems.at[1]
                )
            )


def present(scores, entry):
    return scores + jnp.where(entry >= 0, 0.0, -jnp.inf).astype(jnp.float32)


def near_kernel(blocks, q_hbm, k_hbm, score_ref, q_ref, own, sems):
    copies = Copies(sems)
    copies.start(q_hbm, q_ref)
    copies.start(k_hbm, own)
    copies.wait()
    for i in range(blocks):
        query = block_rows(q_ref, i)
        for slot, other in enumerate((i, i - 1, i + 1)):
            if 0 <= other < blocks:
                score_ref[i, slot] = score(query, block_rows(own, other))


def score_kernel(
    blocks, caps, lists_ref, within_ref, q_ref, near_ref, low, high,
    near_far, other_far, wide, slim, rest, exp_ref, sums_ref, whole, sems,
):
    rep = lax.axis_index("rep")
    gather(rep, caps, wide, slim, rest, whole, sems, lambda copy: copy.start())
    near = near_ref.shape[1]
    sums_ref[...] = jnp.zeros_like(sums_ref)
    for i in range(blocks):
        query = block_rows(q_ref, i)
        for slot, key in enumerate(far_blocks(i, within_ref, (near_far, other_far))):
            exp_ref[i, near + slot] = present(score(query, key), lists_ref[i, near + slot])
    gather(rep, caps, wide, slim, rest, whole, sems, lambda copy: copy.wait())
    for i in range(blocks):
        query = block_rows(q_ref, i)
        scores = [near_ref[i, 0]]
        scores.append(score(query, low[...]) if i == 0 else near_ref[i, 1])
        scores.append(score(query, high[...]) if i == blocks - 1 else near_ref[i, 2])
        scores.extend([exp_ref[i, near], exp_ref[i, near + 1]])
        last = score(query, block_rows(whole, within_ref[i, 2]))
        scores.append(present(last, lists_ref[i, near + 2]))
        peak = scores[0]
        for part in scores[1:]:
            peak = jnp.maximum(peak, part)
        peak = jnp.max(peak, axis=1, keepdims=True)
        exps = [jnp.exp(part - peak) for part in scores]
        for slot, value in enumerate(exps):
            exp_ref[i, slot] = value
        scale = 1.0 / row_total(exps)
        add_columns(sums_ref, lists_ref, i, [value * scale for value in exps])


def scaled(exp_ref, lists_ref, i, factor_refs):
    parts = []
    for slot in range(exp_ref.shape[1]):
        value = exp_ref[i, slot]
        for factor in factor_refs:
            value = value * factor[pl.ds(jnp.maximum(lists_ref[i, slot], 0), 1), :]
        parts.append(value)
    return parts


def round_kernel(blocks, lists_ref, exp_ref, sum_a, sum_b, factor_ref, sums_ref):
    factor_ref[...] = 1.0 / (sum_a[...] + sum_b[...])
    sums_ref[...] = jnp.zeros_like(sums_ref)
    for i in range(blocks):
        parts = scaled(exp_ref, lists_ref, i, [factor_ref])
        scale = 1.0 / row_total(parts)
        add_columns(sums_ref, lists_ref, i, [part * scale for part in parts])


def output_kernel(
    blocks, caps, lists_ref, within_ref, exp_ref, factor_ref, sum_a, sum_b, own, low, high,
    near_far, other_far, wide, slim, rest, out_ref, last_ref, whole, partial_ref, weight_ref, sems,
):
    rep = lax.axis_index("rep")
    gather(rep, caps, wide, slim, rest, whole, sems, lambda copy: copy.start())
    last_ref[...] = 1.0 / (sum_a[...] + sum_b[...])
    for i in range(blocks):
        parts = scaled(exp_ref, lists_ref, i, [factor_ref, last_ref])
        scale = 1.0 / row_total(parts)
        values = near_blocks(i, blocks, own, low, high)
        values += far_blocks(i, within_ref, (near_far, other_far))
        parts = [(part * scale).astype(jnp.bfloat16) for part in parts]
        total = None
        for part, value in zip(parts, values):
            term = jnp.dot(part, value, preferred_element_type=jnp.float32)
            total = term if total is None else total + term
        partial_ref[i] = total
        weight_ref[i] = parts[-1]
    gather(rep, caps, wide, slim, rest, whole, sems, lambda copy: copy.wait())
    for i in range(blocks):
        value = block_rows(whole, within_ref[i, 2])
        total = partial_ref[i] + jnp.dot(weight_ref[i], value, preferred_element_type=jnp.float32)
        out_ref[pl.ds(i * BLOCK, BLOCK), :] = total.astype(out_ref.dtype)


def shifted(x, axis, by):
    devices = lax.axis_size(axis)
    return lax.ppermute(x, axis, [(i, (i + by) % devices) for i in range(devices)])


def swapped(x):
    return lax.ppermute(x, "rep", [(0, 1), (1, 0)])


def over_seq(x):
    devices = lax.axis_size("seq")
    if devices <= 4:
        parts = [
            lax.ppermute(x, "seq", [(i, i ^ by) for i in range(devices)])
            for by in reversed(range(1, devices))
        ]
        for part in parts:
            x = x + part
        return x
    by = 1
    while by < devices:
        x = x + lax.ppermute(x, "seq", [(i, i ^ by) for i in range(devices)])
        by *= 2
    return x


def two_away(wide, slim):
    chips = lax.axis_size("seq")
    moves = [(i, (i - 2) % chips) for i in range(chips)]
    axes = ("seq", "rep")
    return (
        lax.ppermute(wide, axes, [(2 * i, 2 * j) for i, j in moves]),
        lax.ppermute(slim, axes, [(2 * i + 1, 2 * j + 1) for i, j in moves]),
    )


def remainder(crowded, *rest):
    return lax.cond(
        crowded,
        lambda *x: tuple(shifted(part, "seq", -2) for part in x),
        lambda *x: tuple(jnp.zeros_like(part) for part in x),
        *rest,
    )


def with_swap(near, wide, rest, caps, rep):
    beyond = jnp.concatenate([wide, rest[(caps[0] - caps[1]) * BLOCK :]], axis=0)
    return swapped(jnp.where(rep == 0, beyond, near))


def body(queries, key_rows, value_rows, pattern):
    tok_local, heads_local, width = queries.shape
    assert heads_local == 1
    blocks = tok_local // BLOCK
    list_len = pattern.shape[1]
    far_count = list_len - 3
    total_blocks = pattern.shape[0]
    axes = ("seq", "rep")
    shards = lax.axis_size(axes)
    rep = lax.axis_index("rep")
    q = queries.reshape(tok_local, width)
    k = key_rows.reshape(tok_local, width)
    v = value_rows.reshape(tok_local, width)

    caps = (blocks - blocks // 8, blocks - 3 * blocks // 8)
    columns = pattern.T
    k_near = shifted(k, "seq", -1)
    k_wide, k_slim, k_rest = pack_keys(blocks, shards, caps, columns, k)
    k_in, columns, k_wide, k_slim, k_rest = lax.optimization_barrier(
        (k, columns, k_wide, k_slim, k_rest)
    )
    *v_packs, edges_low, edges_high, lists, within, crowded = plan(
        blocks, shards, caps, columns, k_in, v
    )
    v_wide, v_slim, v_rest = v_packs
    k_wide, k_slim = two_away(k_wide, k_slim)
    k_rest, v_rest = remainder(crowded[0] > 0, k_rest, v_rest)
    low = shifted(edges_low, axes, 1)
    high = shifted(edges_high, axes, -1)

    near_scores, q_held = pl.pallas_call(
        lambda *refs: near_kernel(blocks, *refs),
        out_shape=(
            jax.ShapeDtypeStruct((blocks, 3, BLOCK, BLOCK), jnp.float32),
            jax.ShapeDtypeStruct((tok_local, width), jnp.bfloat16),
        ),
        in_specs=[HBM] * 2,
        out_specs=(VMEM, VMEM),
        scratch_shapes=[
            pltpu.VMEM((tok_local, width), jnp.bfloat16),
            pltpu.SemaphoreType.DMA((2,)),
        ],
        cost_estimate=pl.CostEstimate(flops=100663296, bytes_accessed=4194304, transcendentals=0),
        compiler_params=pltpu.CompilerParams(vmem_limit_bytes=LIMIT),
    )(q, k)

    near_scores, v_in, k_near, k_wide, k_slim = lax.optimization_barrier(
        (near_scores, v, k_near, k_wide, k_slim)
    )
    v_near = shifted(v_in, "seq", -1)
    k_other = with_swap(k_near, k_wide, k_rest, caps, rep)
    exps, sums = pl.pallas_call(
        lambda *refs: score_kernel(blocks, caps, *refs),
        out_shape=(
            jax.ShapeDtypeStruct((blocks, list_len, BLOCK, BLOCK), jnp.float32),
            jax.ShapeDtypeStruct((total_blocks, BLOCK), jnp.float32),
        ),
        in_specs=[SMEM] * 2 + [VMEM] * 6 + [ANY] * 3,
        out_specs=(VMEM, VMEM),
        scratch_shapes=[
            pltpu.VMEM((tok_local, width), jnp.bfloat16),
            pltpu.SemaphoreType.DMA((2,)),
        ],
        cost_estimate=pl.CostEstimate(flops=100663296, bytes_accessed=6291456, transcendentals=786432),
        compiler_params=pltpu.CompilerParams(vmem_limit_bytes=LIMIT),
    )(
        lists, within, q_held, near_scores, low[:, :width], high[:, :width],
        k_near, k_other, k_wide, k_slim, k_rest,
    )

    v_wide, v_slim, sums = lax.optimization_barrier((v_wide, v_slim, sums))
    mine = over_seq(sums)
    v_wide, v_slim = two_away(v_wide, v_slim)
    mine, v_near = lax.optimization_barrier((mine, v_near))
    v_wide, v_slim = lax.optimization_barrier((v_wide, v_slim))
    v_other = with_swap(v_near, v_wide, v_rest, caps, rep)
    factor, sums = pl.pallas_call(
        lambda *refs: round_kernel(blocks, *refs),
        out_shape=(
            jax.ShapeDtypeStruct((total_blocks, BLOCK), jnp.float32),
            jax.ShapeDtypeStruct((total_blocks, BLOCK), jnp.float32),
        ),
        in_specs=[SMEM] + [VMEM] * 3,
        out_specs=(VMEM, VMEM),
        cost_estimate=pl.CostEstimate(flops=7864320, bytes_accessed=4194304, transcendentals=0),
        compiler_params=pltpu.CompilerParams(vmem_limit_bytes=LIMIT),
    )(lists, exps, mine, swapped(mine))

    mine = over_seq(sums)
    out = pl.pallas_call(
        lambda *refs: output_kernel(blocks, caps, *refs),
        out_shape=jax.ShapeDtypeStruct((tok_local, width), jnp.bfloat16),
        in_specs=[SMEM] * 2 + [VMEM] * 9 + [ANY] * 3,
        out_specs=VMEM,
        scratch_shapes=[
            pltpu.VMEM((total_blocks, BLOCK), jnp.float32),
            pltpu.VMEM((tok_local, width), jnp.bfloat16),
            pltpu.VMEM((blocks, BLOCK, width), jnp.float32),
            pltpu.VMEM((blocks, BLOCK, BLOCK), jnp.bfloat16),
            pltpu.SemaphoreType.DMA((2,)),
        ],
        cost_estimate=pl.CostEstimate(flops=201326592, bytes_accessed=6291456, transcendentals=0),
        compiler_params=pltpu.CompilerParams(vmem_limit_bytes=LIMIT),
    )(
        lists, within, exps, factor, mine, swapped(mine), v, low[:, width:], high[:, width:],
        v_near, v_other, v_wide, v_slim, v_rest,
    )
    return out.reshape(tok_local, heads_local, width)


def solution(mesh):
    in_specs = (
        P(("groups", "seq", "rep"), "head", None),
        P(("groups", "seq", "rep"), "head", None),
        P(("groups", "seq", "rep"), "head", None),
        P("groups", None),
    )
    out_specs = P(("groups", "seq", "rep"), "head", None)
    return jax.shard_map(body, mesh=mesh, in_specs=in_specs, out_specs=out_specs, check_vma=False)
```

time: 56.7 us -> 52.8 us (0.931)
  waiting for transfers between devices: 14.3 us -> 6.12 us
  Pallas kernels: 6.3 us -> 13.4 us
  starting transfers between devices: 31.8 us -> 26.9 us
  local copies, waits for them, and re-layouts: 3.65 us -> 4.59 us
  between operations: 0.13 us -> 0.93 us
    pallas_call x3 -> x5, Pallas kernels: 5.14 us -> 12.2 us  [the longest x1 3.17 us: plan(): pl.pallas_call(lambda *refs: plan_kernel(blocks, shards, caps, *refs), ou...]
    ppermute x0 -> x4, starting transfers between devices: none -> 6.14 us  [the longest x2 4.81 us: two_away(): lax.ppermute(wide, axes, [(2 * i, 2 * j) for i, j in moves])]
    ppermute x6, waiting for transfers between devices: 6.51 us -> 0.79 us  [over_seq(): lax.ppermute(x, 'seq', [(i, i ^ by) for i in range(devices)])]
    ppermute x6, starting transfers between devices: 15.1 us -> 9.39 us  [over_seq(): lax.ppermute(x, 'seq', [(i, i ^ by) for i in range(devices)])]
    ppermute x6 -> x4, waiting for transfers between devices: 5.39 us -> 0.08 us  [shifted(): lax.ppermute(x, axis, [(i, (i + by) % devices) for i in range(devices)])]
    ppermute x6 -> x4, starting transfers between devices: 16.4 us -> 11.1 us  [shifted(): lax.ppermute(x, axis, [(i, (i + by) % devices) for i in range(devices)])]
    ppermute x0 -> x4, waiting for transfers between devices: none -> 2.86 us  [the longest x2 2.86 us: two_away(): lax.ppermute(wide, axes, [(2 * i, 2 * j) for i, j in moves])]
    slice x2, local copies, waits for them, and re-layouts: 1.58 us -> 0.01 us  [with_swap(): beyond = jnp.concatenate([wide, rest[(caps[0] - caps[1]) * BLOCK:]], axis=0)]
  transfers between devices with their start and end apart: 16 -> 18, of which waited for: 7 -> 5; matrix products, arithmetic and copies ran while one was open for 3% -> 3% of each run, Pallas kernels for 7% -> 20%
where the time goes in v3:
time: 52.8 us; the launch traced here: 52.1 us
  starting transfers between devices  26.9 us (51%)
  Pallas kernels  13.4 us (25%)
  waiting for transfers between devices  6.12 us (12%)
  local copies, waits for them, and re-layouts  4.59 us (9%)
  between operations  0.93 us (2%)
    ppermute x4, starting transfers between devices, shifted(): lax.ppermute(x, axis, [(i, (i + by) % devices) for i in range(devices)])  11.1 us
    ppermute x6, starting transfers between devices, over_seq(): lax.ppermute(x, 'seq', [(i, i ^ by) for i in range(devices)])  9.39 us
    ppermute x2, starting transfers between devices, two_away(): lax.ppermute(wide, axes, [(2 * i, 2 * j) for i, j in moves])  4.81 us
    unnamed x16, local copies, waits for them, and re-layouts  3.27 us
    pallas_call x1, Pallas kernels, plan(): pl.pallas_call(lambda *refs: plan_kernel(blocks, shards, caps, *refs), ou...  3.17 us
    pallas_call x1, Pallas kernels, body(): pl.pallas_call(lambda *refs: score_kernel(blocks, caps, *refs), out_shape...  2.88 us
    ppermute x2, waiting for transfers between devices, two_away(): lax.ppermute(wide, axes, [(2 * i, 2 * j) for i, j in moves])  2.86 us
    pallas_call x1, Pallas kernels, body(): pl.pallas_call(lambda *refs: output_kernel(blocks, caps, *refs), out_shap...  2.78 us
  transfers between devices with their start and end apart: 18, of which 5 were waited for; matrix products, arithmetic and copies ran while one was open for 3% of the time, Pallas kernels for 20%

profile of v3, /device:TPU:0, one launch (start us, length us, event | category | flops | bytes accessed | tf_op | source)
XLA Modules:
  0.0 52.1 jit_solution(2486307746534556048)
XLA Ops:
  0.0 5.0 %collective-permute-start.2 = (bf16[1024,128]{1,0:T(8,128)(2,1)}, bf16[1024,128]{1,0:T(8,128)(2,1)S(1)}, u32[]{:S(2)}, u32[]{:S(2)}) collective-permute-start(bf16[1024,128]{1,0:T(8,128)(2,1)} %bitcast.6), channel_id=1, source_target_pairs={{0,12},{4,0},{8,4},{12,8},{1,13},{5,1},{9,5},{13,9},{2,14},{6,2},{... | collective-permute-start | bytes 786440 | tf_op jit(solution)/shard_map/ppermute | solution.py:300
  5.0 2.7 %shard_map.46 = (bf16[896,128]{1,0:T(8,128)(2,1)}, bf16[640,128]{1,0:T(8,128)(2,1)}, bf16[384,128]{1,0:T(8,128)(2,1)S(1)}) custom-call(s32[6,64]{1,0:T(8,128)} %bitcast.14, bf16[1024,128]{1,0:T(8,128)(2,1)} %bitcast.7), custom_call_target="tpu_custom_call" | custom-call | tf_op jit(solution)/shard_map/pallas_call | solution.py:153
  7.7 1.9 %collective-permute-start.3 = (bf16[896,128]{1,0:T(8,128)(2,1)}, bf16[896,128]{1,0:T(8,128)(2,1)S(1)}, u32[]{:S(2)}, u32[]{:S(2)}) collective-permute-start(bf16[896,128]{1,0:T(8,128)(2,1)} %get-tuple-element.60), channel_id=1, source_target_pairs={{0,8},{4,12},{8,0},{12,4},{2,10},{6,14},{10,2},{14,6},{16,24},{20,... | collective-permute-start | bytes 688136 | tf_op jit(solution)/shard_map/ppermute | solution.py:329
  9.7 0.7 %collective-permute-start.4 = (bf16[640,128]{1,0:T(8,128)(2,1)}, bf16[640,128]{1,0:T(8,128)(2,1)S(1)}, u32[]{:S(2)}, u32[]{:S(2)}) collective-permute-start(bf16[640,128]{1,0:T(8,128)(2,1)} %get-tuple-element.61), channel_id=1, source_target_pairs={{1,9},{5,13},{9,1},{13,5},{3,11},{7,15},{11,3},{15,7},{17,25},{21,... | collective-permute-start | bytes 491528 | tf_op jit(solution)/shard_map/ppermute | solution.py:330
  10.3 3.2 %shard_map.47 = (bf16[896,128]{1,0:T(8,128)(2,1)}, bf16[640,128]{1,0:T(8,128)(2,1)}, bf16[384,128]{1,0:T(8,128)(2,1)S(1)}, bf16[128,256]{1,0:T(8,128)(2,1)}, bf1...) custom-call(s32[6,64]{1,0:T(8,128)} %bitcast.15, bf16[1024,128]{1,0:T(8,128)(2,1)} %bitcast.8, ...), custom_call_target="tpu_custom_call" | custom-call | tf_op jit(solution)/shard_map/pallas_call | solution.py:169
  13.5 0.0 copy-start.7
  13.5 0.0 copy-start.6
  14.2 1.3 %conditional.1 = (bf16[384,128]{1,0:T(8,128)(2,1)}, bf16[384,128]{1,0:T(8,128)(2,1)}, bf16[128,128]{1,0:T(8,128)(2,1)S(1)}, bf16[128,128]{1,0:T(8,128)(2,1)S(1)}) conditional(s32[]{:T(128)} %bitcast.4, () %tuple.24, (bf16[384,128]{1,0:T(8,128)(2,1)S(1)}, bf16[384,128]{1,0:T(8,128)(2,1)S(1)}) %tuple.25), branch_computations={%region_0.0_spmd, %region_1.0_spmd} | conditional | bytes 917616 | solution.py:335
  14.3 0.6 %broadcast.4.clone = bf16[384,128]{1,0:T(8,128)(2,1)} broadcast(bf16[]{:T(256)} %constant.2.clone), dimensions={} | broadcast | bytes 98306 | tf_op jit(solution)/shard_map/broadcast.1
  14.9 0.7 %broadcast.4 = bf16[384,128]{1,0:T(8,128)(2,1)} broadcast(bf16[]{:T(256)} %constant.2.clone), dimensions={} | broadcast | bytes 98306 | tf_op jit(solution)/shard_map/broadcast.1
  15.6 0.0 collective-permute-start.5
  15.6 3.5 %collective-permute-start.6 = (bf16[128,256]{1,0:T(8,128)(2,1)}, bf16[128,256]{1,0:T(8,128)(2,1)S(1)}, u32[]{:S(2)}, u32[]{:S(2)}) collective-permute-start(bf16[128,256]{1,0:T(8,128)(2,1)} %get-tuple-element.64), channel_id=1, source_target_pairs={{0,13},{1,0},{4,1},{5,4},{8,5},{9,8},{12,9},{13,12},{2,15},{3,2},{... | collective-permute-start | bytes 196616 | tf_op jit(solution)/shard_map/ppermute | solution.py:300
  19.1 0.0 copy-start
  19.1 0.9 %copy-done = bf16[1024,1,128]{2,0,1:T(8,128)(2,1)S(1)} copy-done((bf16[1024,1,128]{2,0,1:T(8,128)(2,1)S(1)}, bf16[1024,1,128]{2,0,1:T(8,128)(2,1)}, u32[]{:S(2)}) %copy-start) | copy-done | bytes 262168
  20.1 0.0 copy-start.2
  20.1 0.9 %copy-done.2 = bf16[1024,1,128]{2,0,1:T(8,128)(2,1)S(1)} copy-done((bf16[1024,1,128]{2,0,1:T(8,128)(2,1)S(1)}, bf16[1024,1,128]{2,0,1:T(8,128)(2,1)}, u32[]{:S(2)}) %copy-start.2) | copy-done | bytes 262168
  21.0 0.7 %shard_map.48 = (f32[8,3,128,128]{3,2,1,0:T(8,128)S(1)}, bf16[1024,128]{1,0:T(8,128)(2,1)S(1)}) custom-call(bf16[1024,128]{1,0:T(8,128)(2,1)S(1)} %bitcast.13, bf16[1024,128]{1,0:T(8,128)(2,1)S(1)} %bitcast.9), custom_call_target="tpu_custom_call" | custom-call | flops 100663296 | bytes 4194304 | tf_op jit(solution)/shard_map/pallas_call | solution.py:378
  21.7 0.0 collective-permute-done.4.refs_9_
  21.7 0.0 collective-permute-done.3.refs_8_
  21.7 0.0 collective-permute-done.2.refs_6_
  21.8 0.1 maximum_select_fusion
  21.8 0.1 collective-permute-start.7
  21.9 0.1 collective-permute-done.5
  22.0 0.0 collective-permute-done.6
  22.0 2.5 %collective-permute-start.11 = (bf16[1024,128]{1,0:T(8,128)(2,1)}, bf16[1024,128]{1,0:T(8,128)(2,1)S(1)}, u32[]{:S(2)}, u32[]{:S(2)}) collective-permute-start(bf16[1024,128]{1,0:T(8,128)(2,1)} %bitcast.11), channel_id=1, source_target_pairs={{0,12},{4,0},{8,4},{12,8},{1,13},{5,1},{9,5},{13,9},{2,14},{6,2},{... | collective-permute-start | bytes 786440 | tf_op jit(solution)/shard_map/ppermute | solution.py:300
  24.5 0.0 collective-permute-done.7.refs_7_
  24.5 0.0 copy-start.3
  24.5 0.7 %copy-done.3 = s32[8,6]{1,0:T(8,128)S(1)} copy-done((s32[8,6]{1,0:T(8,128)S(1)}, s32[8,6]{1,0:T(8,128)}, u32[]{:S(2)}) %copy-start.3) | copy-done | bytes 216
  25.2 0.0 copy-start.4
  25.2 0.7 %copy-done.4 = s32[8,3]{1,0:T(8,128)S(1)} copy-done((s32[8,3]{1,0:T(8,128)S(1)}, s32[8,3]{1,0:T(8,128)}, u32[]{:S(2)}) %copy-start.4) | copy-done | bytes 120
  25.9 0.0 copy-start.1
  25.9 0.0 copy-start.5
  25.9 2.9 %shard_map.49 = (f32[8,6,128,128]{3,2,1,0:T(8,128)S(1)}, f32[64,128]{1,0:T(8,128)S(1)}) custom-call(s32[8,6]{1,0:T(8,128)S(1)} %copy-done.3, s32[8,3]{1,0:T(8,128)S(1)} %copy-done.4, bf16[1024,128]{1,0:T(8,128)(2,1)S(1)} %get-tuple-element.58.refs_2_, f32[8,3,128,128]{3,2,1,0:T(8,128)S(1)} %get-tuple-element.62.refs_3_, ...), custom_call_target="tpu_custom_call" | custom-call | flops 100663296 | bytes 6291456 | tf_op jit(solution)/shard_map/pallas_call | solution.py:399
  28.8 0.1 collective-permute-start.10
  28.9 2.0 %collective-permute-start.9 = (f32[64,128]{1,0:T(8,128)S(1)}, f32[64,128]{1,0:T(8,128)S(1)}, u32[]{:S(2)}, u32[]{:S(2)}) collective-permute-start(f32[64,128]{1,0:T(8,128)S(1)} %get-tuple-element.77), channel_id=1, source_target_pairs={{0,8},{4,12},{8,0},{12,4},{1,9},{5,13},{9,1},{13,5},{2,10},{6,14},... | collective-permute-start | bytes 98312 | tf_op jit(solution)/shard_map/ppermute | solution.py:311
  30.8 2.4 %collective-permute-start.8 = (f32[64,128]{1,0:T(8,128)S(1)}, f32[64,128]{1,0:T(8,128)S(1)}, u32[]{:S(2)}, u32[]{:S(2)}) collective-permute-start(f32[64,128]{1,0:T(8,128)S(1)} %get-tuple-element.77), channel_id=1, source_target_pairs={{0,12},{4,8},{8,4},{12,0},{1,13},{5,9},{9,5},{13,1},{2,14},{6,10},... | collective-permute-start | bytes 98312 | tf_op jit(solution)/shard_map/ppermute | solution.py:311
  33.2 0.0 copy-done.7
  33.2 0.7 %collective-permute-start.18 = (bf16[640,128]{1,0:T(8,128)(2,1)S(1)}, bf16[640,128]{1,0:T(8,128)(2,1)S(1)}, u32[]{:S(2)}, u32[]{:S(2)}) collective-permute-start(bf16[640,128]{1,0:T(8,128)(2,1)S(1)} %copy-done.7), channel_id=1, source_target_pairs={{1,9},{5,13},{9,1},{13,5},{3,11},{7,15},{11,3},{15,7},{17,25},{21,... | collective-permute-start | bytes 491528 | tf_op jit(solution)/shard_map/ppermute | solution.py:330
  33.9 0.0 collective-permute-done.10
  33.9 0.0 copy-done.6
  33.9 2.9 %collective-permute-start.17 = (bf16[896,128]{1,0:T(8,128)(2,1)S(1)}, bf16[896,128]{1,0:T(8,128)(2,1)S(1)}, u32[]{:S(2)}, u32[]{:S(2)}) collective-permute-start(bf16[896,128]{1,0:T(8,128)(2,1)S(1)} %copy-done.6), channel_id=1, source_target_pairs={{0,8},{4,12},{8,0},{12,4},{2,10},{6,14},{10,2},{14,6},{16,24},{20,... | collective-permute-start | bytes 688136 | tf_op jit(solution)/shard_map/ppermute | solution.py:329
  36.8 0.0 collective-permute-done.9
  36.8 0.0 collective-permute-done.8
  36.9 0.0 collective-permute-done.11.refs_9_
  36.9 0.1 collective-permute-start.12
  37.0 1.2 %collective-permute-done.12.refs_3_ = f32[64,128]{1,0:T(8,128)S(1)} collective-permute-done((f32[64,128]{1,0:T(8,128)S(1)}, f32[64,128]{1,0:T(8,128)S(1)}, u32[]{:S(2)}, u32[]{:S(2)}) %collective-permute-start.12) | collective-permute-done | bytes 32800 | tf_op jit(solution)/shard_map/ppermute | solution.py:304
  38.1 1.2 %shard_map.50 = (f32[64,128]{1,0:T(8,128)S(1)}, f32[64,128]{1,0:T(8,128)S(1)}) custom-call(s32[8,6]{1,0:T(8,128)S(1)} %copy-done.3, f32[8,6,128,128]{3,2,1,0:T(8,128)S(1)} %get-tuple-element.73.refs_1_.refs_2_, f32[64,128]{1,0:T(8,128)S(1)} %add_add_fusion.1.refs_2_, f32[64,128]{1,0:T(8,128)S(1)} %collective-permute-done.12.refs_3_), custom_call_target="tpu_custom_call" | custom-call | flops 7864320 | bytes 4194304 | tf_op jit(solution)/shard_map/pallas_call | solution.py:424
  39.3 2.5 %collective-permute-start.15 = (f32[64,128]{1,0:T(8,128)S(1)}, f32[64,128]{1,0:T(8,128)S(1)}, u32[]{:S(2)}, u32[]{:S(2)}) collective-permute-start(f32[64,128]{1,0:T(8,128)S(1)} %get-tuple-element.81), channel_id=1, source_target_pairs={{0,4},{4,0},{8,12},{12,8},{1,5},{5,1},{9,13},{13,9},{2,6},{6,2},{1... | collective-permute-start | bytes 98312 | tf_op jit(solution)/shard_map/ppermute | solution.py:311
  41.8 0.2 collective-permute-start.14
  42.0 2.2 %collective-permute-start.13 = (f32[64,128]{1,0:T(8,128)S(1)}, f32[64,128]{1,0:T(8,128)S(1)}, u32[]{:S(2)}, u32[]{:S(2)}) collective-permute-start(f32[64,128]{1,0:T(8,128)S(1)} %get-tuple-element.81), channel_id=1, source_target_pairs={{0,12},{4,8},{8,4},{12,0},{1,13},{5,9},{9,5},{13,1},{2,14},{6,10},... | collective-permute-start | bytes 98312 | tf_op jit(solution)/shard_map/ppermute | solution.py:311
  44.3 0.0 collective-permute-done.18.refs_12_
  44.3 2.9 %collective-permute-done.17.refs_11_ = bf16[896,128]{1,0:T(8,128)(2,1)S(1)} collective-permute-done((bf16[896,128]{1,0:T(8,128)(2,1)S(1)}, bf16[896,128]{1,0:T(8,128)(2,1)S(1)}, u32[]{:S(2)}, u32[]{:S(2)}) %collective-permute-start.17) | collective-permute-done | bytes 229408 | tf_op jit(solution)/shard_map/ppermute | solution.py:329
  47.1 0.1 maximum_select_fusion.1
  47.2 0.1 collective-permute-start.19
  47.3 0.0 collective-permute-done.15
  47.3 0.8 %collective-permute-done.14 = f32[64,128]{1,0:T(8,128)S(1)} collective-permute-done((f32[64,128]{1,0:T(8,128)S(1)}, f32[64,128]{1,0:T(8,128)S(1)}, u32[]{:S(2)}, u32[]{:S(2)}) %collective-permute-start.14) | collective-permute-done | bytes 32800 | tf_op jit(solution)/shard_map/ppermute | solution.py:311
  48.1 0.0 collective-permute-done.13
  48.1 0.1 collective-permute-start.16
  48.2 1.2 %collective-permute-done.16.refs_5_ = f32[64,128]{1,0:T(8,128)S(1)} collective-permute-done((f32[64,128]{1,0:T(8,128)S(1)}, f32[64,128]{1,0:T(8,128)S(1)}, u32[]{:S(2)}, u32[]{:S(2)}) %collective-permute-start.16) | collective-permute-done | bytes 32800 | tf_op jit(solution)/shard_map/ppermute | solution.py:304
  49.4 0.0 collective-permute-done.19.refs_10_
  49.4 0.0 copy-done.1
  49.4 0.0 copy-done.5
  49.4 2.8 %shard_map.51 = bf16[1024,128]{1,0:T(8,128)(2,1)} custom-call(s32[8,6]{1,0:T(8,128)S(1)} %copy-done.3, s32[8,3]{1,0:T(8,128)S(1)} %copy-done.5, f32[8,6,128,128]{3,2,1,0:T(8,128)S(1)} %get-tuple-element.73.refs_1_.refs_2_, f32[64,128]{1,0:T(8,128)S(1)} %get-tuple-element.80.refs_3_, f32[64,128]{1,0:T(8,128)S(1)} %add_add_fusion.refs_4_, ...), custom_call_target="tpu_custom_call" | custom-call | flops 201326592 | bytes 6291456 | tf_op jit(solution)/shard_map/pallas_call | solution.py:437
  (6 shorter events, 0.1 us)
Async XLA Ops:
  0.0 21.7 %collective-permute-start.2 = (bf16[1024,128]{1,0:T(8,128)(2,1)}, bf16[1024,128]{1,0:T(8,128)(2,1)S(1)}, u32[]{:S(2)}, u32[]{:S(2)}) collective-permute-start(bf16[1024,128]{1,0:T(8,128)(2,1)} %bitcast.6), channel_id=1, source_target_pairs={{0,12},{4,0},{8,4},{12,8},{1,13},{5,1},{9,5},{13,9},{2,14},{6,2},{... | collective-permute-start | bytes 786440 | tf_op jit(solution)/shard_map/ppermute | solution.py:300
  7.7 14.0 %collective-permute-start.3 = (bf16[896,128]{1,0:T(8,128)(2,1)}, bf16[896,128]{1,0:T(8,128)(2,1)S(1)}, u32[]{:S(2)}, u32[]{:S(2)}) collective-permute-start(bf16[896,128]{1,0:T(8,128)(2,1)} %get-tuple-element.60), channel_id=1, source_target_pairs={{0,8},{4,12},{8,0},{12,4},{2,10},{6,14},{10,2},{14,6},{16,24},{20,... | collective-permute-start | bytes 688136 | tf_op jit(solution)/shard_map/ppermute | solution.py:329
  9.7 12.1 %collective-permute-start.4 = (bf16[640,128]{1,0:T(8,128)(2,1)}, bf16[640,128]{1,0:T(8,128)(2,1)S(1)}, u32[]{:S(2)}, u32[]{:S(2)}) collective-permute-start(bf16[640,128]{1,0:T(8,128)(2,1)} %get-tuple-element.61), channel_id=1, source_target_pairs={{1,9},{5,13},{9,1},{13,5},{3,11},{7,15},{11,3},{15,7},{17,25},{21,... | collective-permute-start | bytes 491528 | tf_op jit(solution)/shard_map/ppermute | solution.py:330
  13.5 19.7 %copy-start.7 = (bf16[640,128]{1,0:T(8,128)(2,1)S(1)}, bf16[640,128]{1,0:T(8,128)(2,1)}, u32[]{:S(2)}) copy-start(bf16[640,128]{1,0:T(8,128)(2,1)} %get-tuple-element.84) | copy-start | bytes 491524
  13.5 20.4 %copy-start.6 = (bf16[896,128]{1,0:T(8,128)(2,1)S(1)}, bf16[896,128]{1,0:T(8,128)(2,1)}, u32[]{:S(2)}) copy-start(bf16[896,128]{1,0:T(8,128)(2,1)} %get-tuple-element.83) | copy-start | bytes 688132
  15.6 6.4 %collective-permute-start.5 = (bf16[128,256]{1,0:T(8,128)(2,1)}, bf16[128,256]{1,0:T(8,128)(2,1)S(1)}, u32[]{:S(2)}, u32[]{:S(2)}) collective-permute-start(bf16[128,256]{1,0:T(8,128)(2,1)} %get-tuple-element.63), channel_id=1, source_target_pairs={{0,1},{1,4},{4,5},{5,8},{8,9},{9,12},{12,13},{13,0},{2,3},{3,6},{6... | collective-permute-start | bytes 196616 | tf_op jit(solution)/shard_map/ppermute | solution.py:300
  15.6 6.4 %collective-permute-start.6 = (bf16[128,256]{1,0:T(8,128)(2,1)}, bf16[128,256]{1,0:T(8,128)(2,1)S(1)}, u32[]{:S(2)}, u32[]{:S(2)}) collective-permute-start(bf16[128,256]{1,0:T(8,128)(2,1)} %get-tuple-element.64), channel_id=1, source_target_pairs={{0,13},{1,0},{4,1},{5,4},{8,5},{9,8},{12,9},{13,12},{2,15},{3,2},{... | collective-permute-start | bytes 196616 | tf_op jit(solution)/shard_map/ppermute | solution.py:300
  19.1 0.9 %copy-start = (bf16[1024,1,128]{2,0,1:T(8,128)(2,1)S(1)}, bf16[1024,1,128]{2,0,1:T(8,128)(2,1)}, u32[]{:S(2)}) copy-start(bf16[1024,1,128]{2,0,1:T(8,128)(2,1)} %param.7) | copy-start | bytes 786436
  20.1 0.9 %copy-start.2 = (bf16[1024,1,128]{2,0,1:T(8,128)(2,1)S(1)}, bf16[1024,1,128]{2,0,1:T(8,128)(2,1)}, u32[]{:S(2)}) copy-start(bf16[1024,1,128]{2,0,1:T(8,128)(2,1)} %param.6) | copy-start | bytes 786436
  21.8 2.7 %collective-permute-start.7 = (bf16[1024,128]{1,0:T(8,128)(2,1)S(1)}, bf16[1024,128]{1,0:T(8,128)(2,1)S(1)}, u32[]{:S(2)}, u32[]{:S(2)}) collective-permute-start(bf16[1024,128]{1,0:T(8,128)(2,1)S(1)} %maximum_select_fusion), channel_id=1, source_target_pairs={{0,1},{1,0},{2,3},{3,2},{4,5},{5,4},{6,7},{7,6},{8,9},{9,8},{10,11... | collective-permute-start | bytes 786440 | tf_op jit(solution)/shard_map/ppermute | solution.py:304
  22.0 14.9 %collective-permute-start.11 = (bf16[1024,128]{1,0:T(8,128)(2,1)}, bf16[1024,128]{1,0:T(8,128)(2,1)S(1)}, u32[]{:S(2)}, u32[]{:S(2)}) collective-permute-start(bf16[1024,128]{1,0:T(8,128)(2,1)} %bitcast.11), channel_id=1, source_target_pairs={{0,12},{4,0},{8,4},{12,8},{1,13},{5,1},{9,5},{13,9},{2,14},{6,2},{... | collective-permute-start | bytes 786440 | tf_op jit(solution)/shard_map/ppermute | solution.py:300
  24.5 0.7 %copy-start.3 = (s32[8,6]{1,0:T(8,128)S(1)}, s32[8,6]{1,0:T(8,128)}, u32[]{:S(2)}) copy-start(s32[8,6]{1,0:T(8,128)} %get-tuple-element.56.refs_0_) | copy-start | bytes 580
  25.2 0.7 %copy-start.4 = (s32[8,3]{1,0:T(8,128)S(1)}, s32[8,3]{1,0:T(8,128)}, u32[]{:S(2)}) copy-start(s32[8,3]{1,0:T(8,128)} %get-tuple-element.57.refs_1_) | copy-start | bytes 292
  25.9 23.5 %copy-start.1 = (bf16[1024,1,128]{2,0,1:T(8,128)(2,1)S(1)}, bf16[1024,1,128]{2,0,1:T(8,128)(2,1)}, u32[]{:S(2)}) copy-start(bf16[1024,1,128]{2,0,1:T(8,128)(2,1)} %param.8) | copy-start | bytes 786436
  25.9 23.5 %copy-start.5 = (s32[8,3]{1,0:T(8,128)S(1)}, s32[8,3]{1,0:T(8,128)}, u32[]{:S(2)}) copy-start(s32[8,3]{1,0:T(8,128)} %get-tuple-element.57.refs_1_) | copy-start | bytes 292
  28.8 5.1 %collective-permute-start.10 = (f32[64,128]{1,0:T(8,128)S(1)}, f32[64,128]{1,0:T(8,128)S(1)}, u32[]{:S(2)}, u32[]{:S(2)}) collective-permute-start(f32[64,128]{1,0:T(8,128)S(1)} %get-tuple-element.77), channel_id=1, source_target_pairs={{0,4},{4,0},{8,12},{12,8},{1,5},{5,1},{9,13},{13,9},{2,6},{6,2},{1... | collective-permute-start | bytes 98312 | tf_op jit(solution)/shard_map/ppermute | solution.py:311
  28.9 8.0 %collective-permute-start.9 = (f32[64,128]{1,0:T(8,128)S(1)}, f32[64,128]{1,0:T(8,128)S(1)}, u32[]{:S(2)}, u32[]{:S(2)}) collective-permute-start(f32[64,128]{1,0:T(8,128)S(1)} %get-tuple-element.77), channel_id=1, source_target_pairs={{0,8},{4,12},{8,0},{12,4},{1,9},{5,13},{9,1},{13,5},{2,10},{6,14},... | collective-permute-start | bytes 98312 | tf_op jit(solution)/shard_map/ppermute | solution.py:311
  30.8 6.0 %collective-permute-start.8 = (f32[64,128]{1,0:T(8,128)S(1)}, f32[64,128]{1,0:T(8,128)S(1)}, u32[]{:S(2)}, u32[]{:S(2)}) collective-permute-start(f32[64,128]{1,0:T(8,128)S(1)} %get-tuple-element.77), channel_id=1, source_target_pairs={{0,12},{4,8},{8,4},{12,0},{1,13},{5,9},{9,5},{13,1},{2,14},{6,10},... | collective-permute-start | bytes 98312 | tf_op jit(solution)/shard_map/ppermute | solution.py:311
  33.2 11.0 %collective-permute-start.18 = (bf16[640,128]{1,0:T(8,128)(2,1)S(1)}, bf16[640,128]{1,0:T(8,128)(2,1)S(1)}, u32[]{:S(2)}, u32[]{:S(2)}) collective-permute-start(bf16[640,128]{1,0:T(8,128)(2,1)S(1)} %copy-done.7), channel_id=1, source_target_pairs={{1,9},{5,13},{9,1},{13,5},{3,11},{7,15},{11,3},{15,7},{17,25},{21,... | collective-permute-start | bytes 491528 | tf_op jit(solution)/shard_map/ppermute | solution.py:330
  33.9 13.2 %collective-permute-start.17 = (bf16[896,128]{1,0:T(8,128)(2,1)S(1)}, bf16[896,128]{1,0:T(8,128)(2,1)S(1)}, u32[]{:S(2)}, u32[]{:S(2)}) collective-permute-start(bf16[896,128]{1,0:T(8,128)(2,1)S(1)} %copy-done.6), channel_id=1, source_target_pairs={{0,8},{4,12},{8,0},{12,4},{2,10},{6,14},{10,2},{14,6},{16,24},{20,... | collective-permute-start | bytes 688136 | tf_op jit(solution)/shard_map/ppermute | solution.py:329
  36.9 1.3 %collective-permute-start.12 = (f32[64,128]{1,0:T(8,128)S(1)}, f32[64,128]{1,0:T(8,128)S(1)}, u32[]{:S(2)}, u32[]{:S(2)}) collective-permute-start(f32[64,128]{1,0:T(8,128)S(1)} %add_add_fusion.1.refs_2_), channel_id=1, source_target_pairs={{0,1},{1,0},{2,3},{3,2},{4,5},{5,4},{6,7},{7,6},{8,9},{9,8},{10,11... | collective-permute-start | bytes 98312 | tf_op jit(solution)/shard_map/ppermute | solution.py:304
  39.3 8.0 %collective-permute-start.15 = (f32[64,128]{1,0:T(8,128)S(1)}, f32[64,128]{1,0:T(8,128)S(1)}, u32[]{:S(2)}, u32[]{:S(2)}) collective-permute-start(f32[64,128]{1,0:T(8,128)S(1)} %get-tuple-element.81), channel_id=1, source_target_pairs={{0,4},{4,0},{8,12},{12,8},{1,5},{5,1},{9,13},{13,9},{2,6},{6,2},{1... | collective-permute-start | bytes 98312 | tf_op jit(solution)/shard_map/ppermute | solution.py:311
  41.8 6.2 %collective-permute-start.14 = (f32[64,128]{1,0:T(8,128)S(1)}, f32[64,128]{1,0:T(8,128)S(1)}, u32[]{:S(2)}, u32[]{:S(2)}) collective-permute-start(f32[64,128]{1,0:T(8,128)S(1)} %get-tuple-element.81), channel_id=1, source_target_pairs={{0,8},{4,12},{8,0},{12,4},{1,9},{5,13},{9,1},{13,5},{2,10},{6,14},... | collective-permute-start | bytes 98312 | tf_op jit(solution)/shard_map/ppermute | solution.py:311
  42.0 6.0 %collective-permute-start.13 = (f32[64,128]{1,0:T(8,128)S(1)}, f32[64,128]{1,0:T(8,128)S(1)}, u32[]{:S(2)}, u32[]{:S(2)}) collective-permute-start(f32[64,128]{1,0:T(8,128)S(1)} %get-tuple-element.81), channel_id=1, source_target_pairs={{0,12},{4,8},{8,4},{12,0},{1,13},{5,9},{9,5},{13,1},{2,14},{6,10},... | collective-permute-start | bytes 98312 | tf_op jit(solution)/shard_map/ppermute | solution.py:311
  47.2 2.2 %collective-permute-start.19 = (bf16[1024,128]{1,0:T(8,128)(2,1)S(1)}, bf16[1024,128]{1,0:T(8,128)(2,1)S(1)}, u32[]{:S(2)}, u32[]{:S(2)}) collective-permute-start(bf16[1024,128]{1,0:T(8,128)(2,1)S(1)} %maximum_select_fusion.1), channel_id=1, source_target_pairs={{0,1},{1,0},{2,3},{3,2},{4,5},{5,4},{6,7},{7,6},{8,9},{9,8},{10,11... | collective-permute-start | bytes 786440 | tf_op jit(solution)/shard_map/ppermute | solution.py:304
  48.1 1.3 %collective-permute-start.16 = (f32[64,128]{1,0:T(8,128)S(1)}, f32[64,128]{1,0:T(8,128)S(1)}, u32[]{:S(2)}, u32[]{:S(2)}) collective-permute-start(f32[64,128]{1,0:T(8,128)S(1)} %add_add_fusion.refs_4_), channel_id=1, source_target_pairs={{0,1},{1,0},{2,3},{3,2},{4,5},{5,4},{6,7},{7,6},{8,9},{9,8},{10,11... | collective-permute-start | bytes 98312 | tf_op jit(solution)/shard_map/ppermute | solution.py:304

commit v4 on v3

--- a/solution.py
+++ b/solution.py
@@ -9,6 +9,8 @@
 
 BLOCK = 128
 ITERS = 2
+LISTED = 6
+SENT = jnp.float32
 VMEM = pl.BlockSpec(memory_space=pltpu.VMEM)
 ANY = pl.BlockSpec(memory_space=pl.ANY)
 HBM = pl.BlockSpec(memory_space=pltpu.HBM)
@@ -29,8 +31,8 @@
     return [block_rows(own, i), before, after]
 
 
-def far_blocks(i, within_ref, fars):
-    return [block_rows(far, within_ref[i, slot]) for slot, far in enumerate(fars)]
+def far_blocks(i, lists_ref, fars):
+    return [block_rows(far, lists_ref[i, LISTED + slot]) for slot, far in enumerate(fars)]
 
 
 def score(query, key):
@@ -108,11 +110,15 @@
     copies.wait()
 
 
-def plan_kernel(blocks, shards, caps, pattern_hbm, k_ref, v_ref, *refs):
+def plan_kernel(blocks, shards, caps, pattern_hbm, q_hbm, k_ref, v_ref, *refs):
     outs, edges = refs[:3], refs[3:5]
-    lists_ref, within_ref, crowded_ref, pattern_ref, order_ref, rank_ref, sems, sem = refs[5:]
+    score_ref, q_ref, lists_ref, crowded_ref = refs[5:9]
+    own, pattern_ref, order_ref, rank_ref, sems, near_sems, sem = refs[9:]
     position, rep = lax.axis_index(("seq", "rep")), lax.axis_index("rep")
     width = k_ref.shape[1]
+    held = Copies(near_sems)
+    held.start(q_hbm, q_ref)
+    held.start(k_ref, own)
     copies = Copies(sems)
     for edge, begin in zip(edges, ((blocks - 1) * BLOCK, 0)):
         for at, rows in enumerate((k_ref, v_ref)):
@@ -135,12 +141,19 @@
             if slot >= 3:
                 source = lax.rem(position + slot - 1, shards)
                 at = jnp.where(entry >= 0, entry - source * blocks, 0)
-                within_ref[i, slot - 3] = at if slot == 3 else rank_ref[slot - 4, at]
+                at = at if slot == 3 else rank_ref[slot - 4, at]
+                lists_ref[i, pattern_ref.shape[0] + slot - 3] = at
     crowded = jnp.int32(0)
     for source in range(shards):
         count = sum(listed_bits(pattern_ref, blocks, shards, source, source % 2 == 0))
         crowded = jnp.maximum(crowded, jnp.where(count > caps[source % 2], 1, 0))
     crowded_ref[0] = crowded
+    held.wait()
+    for i in range(blocks):
+        query = block_rows(q_ref, i)
+        for slot, other in enumerate((i, i - 1, i + 1)):
+            if 0 <= other < blocks:
+                score_ref[i, slot] = score(query, block_rows(own, other))
     copies.wait()
 
 
@@ -164,80 +177,92 @@
     )(columns, k)
 
 
-def plan(blocks, shards, caps, columns, k, v):
+def plan(blocks, shards, caps, columns, q, k, v):
     width, list_len = k.shape[1], columns.shape[0]
     return pl.pallas_call(
         lambda *refs: plan_kernel(blocks, shards, caps, *refs),
         out_shape=packed_shapes(blocks, caps, v)
         + [jax.ShapeDtypeStruct((BLOCK, 2 * width), k.dtype)] * 2
         + [
-            jax.ShapeDtypeStruct((blocks, list_len), jnp.int32),
-            jax.ShapeDtypeStruct((blocks, list_len - 3), jnp.int32),
+            jax.ShapeDtypeStruct((blocks, 3, BLOCK, BLOCK), jnp.float32),
+            jax.ShapeDtypeStruct(q.shape, q.dtype),
+            jax.ShapeDtypeStruct((blocks, 2 * list_len - 3), jnp.int32),
             jax.ShapeDtypeStruct((1,), jnp.int32),
         ],
-        in_specs=[HBM] * 3,
-        out_specs=[VMEM] * 5 + [SMEM] * 3,
+        in_specs=[HBM] * 4,
+        out_specs=[VMEM] * 7 + [SMEM] * 2,
         scratch_shapes=[
+            pltpu.VMEM(k.shape, k.dtype),
             pltpu.SMEM(columns.shape, jnp.int32),
             pltpu.SMEM((blocks,), jnp.int32),
             pltpu.SMEM((2, blocks), jnp.int32),
             pltpu.SemaphoreType.DMA((2 * blocks + 4,)),
+            pltpu.SemaphoreType.DMA((2,)),
             pltpu.SemaphoreType.DMA,
         ],
-    )(columns, k, v)
-
-
-def gather(rep, caps, wide, slim, rest, whole, sems, act):
-    for core, first, skip in ((0, wide, caps[0] - caps[1]), (1, slim, 0)):
-
-        @pl.when(rep == core)
-        def _():
-            used = first.shape[0]
-            left = whole.shape[0] - used
-            act(pltpu.make_async_copy(first, whole.at[pl.ds(0, used), :], sems.at[0]))
-            act(
-                pltpu.make_async_copy(
-                    rest.at[pl.ds(skip * BLOCK, left), :], whole.at[pl.ds(used, left), :], sems.at[1]
-                )
-            )
+        cost_estimate=pl.CostEstimate(flops=100663296, bytes_accessed=4194304, transcendentals=0),
+        compiler_params=pltpu.CompilerParams(vmem_limit_bytes=LIMIT),
+    )(columns, q, k, v)
+
+
+class Whole:
+    def __init__(self, caps, wide, slim, rest, whole, lists_hbm, lists_ref, sems):
+        self.parts = (0, wide, caps[0] - caps[1]), (1, slim, 0)
+        self.rest, self.whole, self.sem = rest, whole, sems.at[0]
+        self.lists = pltpu.make_async_copy(lists_hbm, lists_ref, sems.at[1])
+
+    def left(self, used, skip):
+        count = self.whole.shape[0] - used
+        return pltpu.make_async_copy(
+            self.rest.at[pl.ds(skip * BLOCK, count), :], self.whole.at[pl.ds(used, count), :], self.sem
+        )
+
+    def on_core(self, act):
+        for core, first, skip in self.parts:
+
+            @pl.when(lax.axis_index("rep") == core)
+            def _():
+                act(first, skip)
+
+    def start(self):
+        self.lists.start()
+
+        def begin(first, skip):
+            self.left(first.shape[0], skip).start()
+            self.whole[: first.shape[0], :] = first[...]
+
+        self.on_core(begin)
+
+    def wait(self):
+        self.on_core(lambda first, skip: self.left(first.shape[0], skip).wait())
 
 
 def present(scores, entry):
     return scores + jnp.where(entry >= 0, 0.0, -jnp.inf).astype(jnp.float32)
 
 
-def near_kernel(blocks, q_hbm, k_hbm, score_ref, q_ref, own, sems):
-    copies = Copies(sems)
-    copies.start(q_hbm, q_ref)
-    copies.start(k_hbm, own)
-    copies.wait()
-    for i in range(blocks):
-        query = block_rows(q_ref, i)
-        for slot, other in enumerate((i, i - 1, i + 1)):
-            if 0 <= other < blocks:
-                score_ref[i, slot] = score(query, block_rows(own, other))
-
-
 def score_kernel(
-    blocks, caps, lists_ref, within_ref, q_ref, near_ref, low, high,
-    near_far, other_far, wide, slim, rest, exp_ref, sums_ref, whole, sems,
+    blocks, caps, lists_hbm, q_ref, near_ref, low, high,
+    near_far, other_far, wide, slim, rest, exp_ref, sums_ref, sent_ref,
+    whole, lists_ref, sems,
 ):
-    rep = lax.axis_index("rep")
-    gather(rep, caps, wide, slim, rest, whole, sems, lambda copy: copy.start())
+    gathered = Whole(caps, wide, slim, rest, whole, lists_hbm, lists_ref, sems)
+    gathered.start()
     near = near_ref.shape[1]
     sums_ref[...] = jnp.zeros_like(sums_ref)
+    gathered.lists.wait()
     for i in range(blocks):
         query = block_rows(q_ref, i)
-        for slot, key in enumerate(far_blocks(i, within_ref, (near_far, other_far))):
+        for slot, key in enumerate(far_blocks(i, lists_ref, (near_far, other_far))):
             exp_ref[i, near + slot] = present(score(query, key), lists_ref[i, near + slot])
-    gather(rep, caps, wide, slim, rest, whole, sems, lambda copy: copy.wait())
+    gathered.wait()
     for i in range(blocks):
         query = block_rows(q_ref, i)
         scores = [near_ref[i, 0]]
         scores.append(score(query, low[...]) if i == 0 else near_ref[i, 1])
         scores.append(score(query, high[...]) if i == blocks - 1 else near_ref[i, 2])
         scores.extend([exp_ref[i, near], exp_ref[i, near + 1]])
-        last = score(query, block_rows(whole, within_ref[i, 2]))
+        last = score(query, block_rows(whole, lists_ref[i, LISTED + 2]))
         scores.append(present(last, lists_ref[i, near + 2]))
         peak = scores[0]
         for part in scores[1:]:
@@ -248,6 +273,7 @@
             exp_ref[i, slot] = value
         scale = 1.0 / row_total(exps)
         add_columns(sums_ref, lists_ref, i, [value * scale for value in exps])
+    sent_ref[...] = sums_ref[...].astype(sent_ref.dtype)
 
 
 def scaled(exp_ref, lists_ref, i, factor_refs):
@@ -260,27 +286,33 @@
     return parts
 
 
-def round_kernel(blocks, lists_ref, exp_ref, sum_a, sum_b, factor_ref, sums_ref):
-    factor_ref[...] = 1.0 / (sum_a[...] + sum_b[...])
+def round_kernel(
+    blocks, lists_hbm, exp_ref, sum_a, sum_b, factor_ref, sums_ref, sent_ref, lists_ref, sem
+):
+    load(lists_hbm, lists_ref, sem)
+    factor_ref[...] = 1.0 / (sum_a[...] + sum_b[...].astype(jnp.float32))
     sums_ref[...] = jnp.zeros_like(sums_ref)
     for i in range(blocks):
         parts = scaled(exp_ref, lists_ref, i, [factor_ref])
         scale = 1.0 / row_total(parts)
         add_columns(sums_ref, lists_ref, i, [part * scale for part in parts])
+    sent_ref[...] = sums_ref[...].astype(sent_ref.dtype)
 
 
 def output_kernel(
-    blocks, caps, lists_ref, within_ref, exp_ref, factor_ref, sum_a, sum_b, own, low, high,
-    near_far, other_far, wide, slim, rest, out_ref, last_ref, whole, partial_ref, weight_ref, sems,
+    blocks, caps, lists_hbm, exp_ref, factor_ref, sum_a, sum_b, own, low, high,
+    near_far, other_far, wide, slim, rest, out_ref, last_ref, whole, partial_ref, weight_ref,
+    lists_ref, sems,
 ):
-    rep = lax.axis_index("rep")
-    gather(rep, caps, wide, slim, rest, whole, sems, lambda copy: copy.start())
-    last_ref[...] = 1.0 / (sum_a[...] + sum_b[...])
+    gathered = Whole(caps, wide, slim, rest, whole, lists_hbm, lists_ref, sems)
+    gathered.start()
+    last_ref[...] = 1.0 / (sum_a[...] + sum_b[...].astype(jnp.float32))
+    gathered.lists.wait()
     for i in range(blocks):
         parts = scaled(exp_ref, lists_ref, i, [factor_ref, last_ref])
         scale = 1.0 / row_total(parts)
         values = near_blocks(i, blocks, own, low, high)
-        values += far_blocks(i, within_ref, (near_far, other_far))
+        values += far_blocks(i, lists_ref, (near_far, other_far))
         parts = [(part * scale).astype(jnp.bfloat16) for part in parts]
         total = None
         for part, value in zip(parts, values):
@@ -288,9 +320,9 @@
             total = term if total is None else total + term
         partial_ref[i] = total
         weight_ref[i] = parts[-1]
-    gather(rep, caps, wide, slim, rest, whole, sems, lambda copy: copy.wait())
-    for i in range(blocks):
-        value = block_rows(whole, within_ref[i, 2])
+    gathered.wait()
+    for i in range(blocks):
+        value = block_rows(whole, lists_ref[i, LISTED + 2])
         total = partial_ref[i] + jnp.dot(weight_ref[i], value, preferred_element_type=jnp.float32)
         out_ref[pl.ds(i * BLOCK, BLOCK), :] = total.astype(out_ref.dtype)
 
@@ -304,21 +336,17 @@
     return lax.ppermute(x, "rep", [(0, 1), (1, 0)])
 
 
-def over_seq(x):
+def over_seq(mine, sent):
     devices = lax.axis_size("seq")
+    pairs = lambda by: [(i, i ^ by) for i in range(devices)]
     if devices <= 4:
-        parts = [
-            lax.ppermute(x, "seq", [(i, i ^ by) for i in range(devices)])
-            for by in reversed(range(1, devices))
-        ]
-        for part in parts:
-            x = x + part
-        return x
+        parts = [lax.ppermute(sent, "seq", pairs(by)) for by in reversed(range(1, devices))]
+        return sum([part.astype(mine.dtype) for part in parts], mine)
     by = 1
     while by < devices:
-        x = x + lax.ppermute(x, "seq", [(i, i ^ by) for i in range(devices)])
+        mine = mine + lax.ppermute(mine, "seq", pairs(by))
         by *= 2
-    return x
+    return mine
 
 
 def two_away(wide, slim):
@@ -335,7 +363,7 @@
     return lax.cond(
         crowded,
         lambda *x: tuple(shifted(part, "seq", -2) for part in x),
-        lambda *x: tuple(jnp.zeros_like(part) for part in x),
+        lambda *x: x,
         *rest,
     )
 
@@ -366,8 +394,8 @@
     k_in, columns, k_wide, k_slim, k_rest = lax.optimization_barrier(
         (k, columns, k_wide, k_slim, k_rest)
     )
-    *v_packs, edges_low, edges_high, lists, within, crowded = plan(
-        blocks, shards, caps, columns, k_in, v
+    *v_packs, edges_low, edges_high, near_scores, q_held, lists, crowded = plan(
+        blocks, shards, caps, columns, q, k_in, v
     )
     v_wide, v_slim, v_rest = v_packs
     k_wide, k_slim = two_away(k_wide, k_slim)
@@ -375,81 +403,73 @@
     low = shifted(edges_low, axes, 1)
     high = shifted(edges_high, axes, -1)
 
-    near_scores, q_held = pl.pallas_call(
-        lambda *refs: near_kernel(blocks, *refs),
-        out_shape=(
-            jax.ShapeDtypeStruct((blocks, 3, BLOCK, BLOCK), jnp.float32),
-            jax.ShapeDtypeStruct((tok_local, width), jnp.bfloat16),
-        ),
-        in_specs=[HBM] * 2,
-        out_specs=(VMEM, VMEM),
-        scratch_shapes=[
-            pltpu.VMEM((tok_local, width), jnp.bfloat16),
-            pltpu.SemaphoreType.DMA((2,)),
-        ],
-        cost_estimate=pl.CostEstimate(flops=100663296, bytes_accessed=4194304, transcendentals=0),
-        compiler_params=pltpu.CompilerParams(vmem_limit_bytes=LIMIT),
-    )(q, k)
-
     near_scores, v_in, k_near, k_wide, k_slim = lax.optimization_barrier(
         (near_scores, v, k_near, k_wide, k_slim)
     )
     v_near = shifted(v_in, "seq", -1)
     k_other = with_swap(k_near, k_wide, k_rest, caps, rep)
-    exps, sums = pl.pallas_call(
+    exps, sums, sent = pl.pallas_call(
         lambda *refs: score_kernel(blocks, caps, *refs),
         out_shape=(
             jax.ShapeDtypeStruct((blocks, list_len, BLOCK, BLOCK), jnp.float32),
             jax.ShapeDtypeStruct((total_blocks, BLOCK), jnp.float32),
+            jax.ShapeDtypeStruct((total_blocks, BLOCK), SENT),
         ),
-        in_specs=[SMEM] * 2 + [VMEM] * 6 + [ANY] * 3,
-        out_specs=(VMEM, VMEM),
+        in_specs=[HBM] + [VMEM] * 8 + [ANY],
+        out_specs=(VMEM, VMEM, VMEM),
         scratch_shapes=[
             pltpu.VMEM((tok_local, width), jnp.bfloat16),
+            pltpu.SMEM((blocks, 2 * list_len - 3), jnp.int32),
             pltpu.SemaphoreType.DMA((2,)),
         ],
         cost_estimate=pl.CostEstimate(flops=100663296, bytes_accessed=6291456, transcendentals=786432),
         compiler_params=pltpu.CompilerParams(vmem_limit_bytes=LIMIT),
     )(
-        lists, within, q_held, near_scores, low[:, :width], high[:, :width],
+        lists, q_held, near_scores, low[:, :width], high[:, :width],
         k_near, k_other, k_wide, k_slim, k_rest,
     )
 
-    v_wide, v_slim, sums = lax.optimization_barrier((v_wide, v_slim, sums))
-    mine = over_seq(sums)
+    v_wide, v_slim, sent = lax.optimization_barrier((v_wide, v_slim, sent))
+    mine = over_seq(sums, sent)
     v_wide, v_slim = two_away(v_wide, v_slim)
     mine, v_near = lax.optimization_barrier((mine, v_near))
     v_wide, v_slim = lax.optimization_barrier((v_wide, v_slim))
     v_other = with_swap(v_near, v_wide, v_rest, caps, rep)
-    factor, sums = pl.pallas_call(
+    factor, sums, sent = pl.pallas_call(
         lambda *refs: round_kernel(blocks, *refs),
         out_shape=(
             jax.ShapeDtypeStruct((total_blocks, BLOCK), jnp.float32),
             jax.ShapeDtypeStruct((total_blocks, BLOCK), jnp.float32),
+            jax.ShapeDtypeStruct((total_blocks, BLOCK), SENT),
         ),
-        in_specs=[SMEM] + [VMEM] * 3,
-        out_specs=(VMEM, VMEM),
+        in_specs=[HBM] + [VMEM] * 3,
+        out_specs=(VMEM, VMEM, VMEM),
+        scratch_shapes=[
+            pltpu.SMEM((blocks, 2 * list_len - 3), jnp.int32),
+            pltpu.SemaphoreType.DMA,
+        ],
         cost_estimate=pl.CostEstimate(flops=7864320, bytes_accessed=4194304, transcendentals=0),
         compiler_params=pltpu.CompilerParams(vmem_limit_bytes=LIMIT),
-    )(lists, exps, mine, swapped(mine))
-
-    mine = over_seq(sums)
+    )(lists, exps, mine, swapped(mine.astype(SENT)))
+
+    mine = over_seq(sums, sent)
     out = pl.pallas_call(
         lambda *refs: output_kernel(blocks, caps, *refs),
         out_shape=jax.ShapeDtypeStruct((tok_local, width), jnp.bfloat16),
-        in_specs=[SMEM] * 2 + [VMEM] * 9 + [ANY] * 3,
+        in_specs=[HBM] + [VMEM] * 11 + [ANY],
         out_specs=VMEM,
         scratch_shapes=[
             pltpu.VMEM((total_blocks, BLOCK), jnp.float32),
             pltpu.VMEM((tok_local, width), jnp.bfloat16),
             pltpu.VMEM((blocks, BLOCK, width), jnp.float32),
             pltpu.VMEM((blocks, BLOCK, BLOCK), jnp.bfloat16),
+            pltpu.SMEM((blocks, 2 * list_len - 3), jnp.int32),
             pltpu.SemaphoreType.DMA((2,)),
         ],
         cost_estimate=pl.CostEstimate(flops=201326592, bytes_accessed=6291456, transcendentals=0),
         compiler_params=pltpu.CompilerParams(vmem_limit_bytes=LIMIT),
     )(
-        lists, within, exps, factor, mine, swapped(mine), v, low[:, width:], high[:, width:],
+        lists, exps, factor, mine, swapped(mine.astype(SENT)), v, low[:, width:], high[:, width:],
         v_near, v_other, v_wide, v_slim, v_rest,
     )
     return out.reshape(tok_local, heads_local, width)

time: 52.8 us -> 51.5 us (0.975)
  waiting for transfers between devices: 6.12 us -> 13.2 us
  starting transfers between devices: 26.9 us -> 21.6 us
  Pallas kernels: 13.4 us -> 11.8 us
  local copies, waits for them, and re-layouts: 4.59 us -> 3.55 us
    ppermute x4, starting transfers between devices: 11.1 us -> 6.35 us  [shifted(): lax.ppermute(x, axis, [(i, (i + by) % devices) for i in range(devices)])]
    ppermute x4, waiting for transfers between devices: 0.08 us -> 3.89 us  [shifted(): lax.ppermute(x, axis, [(i, (i + by) % devices) for i in range(devices)])]
    ppermute x2, waiting for transfers between devices: 2.86 us -> 6.45 us  [two_away(): lax.ppermute(wide, axes, [(2 * i, 2 * j) for i, j in moves])]
    another operation x2 -> x0, local copies, waits for them, and re-layouts: 1.3 us -> none
    ppermute x6, starting transfers between devices: 9.39 us -> 8.46 us  [over_seq(): lax.ppermute(sent, 'seq', pairs(by))]
    pallas_call x1 -> x0, Pallas kernels: 0.69 us -> none  [body(): pl.pallas_call(lambda *refs: near_kernel(blocks, *refs), out_shape=(jax.S...]
    pallas_call x1, Pallas kernels: 2.88 us -> 2.2 us  [body(): pl.pallas_call(lambda *refs: score_kernel(blocks, caps, *refs), out_shape...]
    ppermute x4, starting transfers between devices: 0.28 us -> 0.87 us  [swapped(): return lax.ppermute(x, 'rep', [(0, 1), (1, 0)])]
  transfers between devices with their start and end apart: 18 -> 18, of which waited for: 5 -> 7; matrix products, arithmetic and copies ran while one was open for 3% -> 0% of each run, Pallas kernels for 20% -> 19%
where the time goes in v4:
time: 51.5 us; the launch traced here: 51.1 us
  starting transfers between devices  21.6 us (42%)
  waiting for transfers between devices  13.2 us (26%)
  Pallas kernels  11.8 us (23%)
  local copies, waits for them, and re-layouts  3.55 us (7%)
  between operations  0.75 us (1%)
    ppermute x6, starting transfers between devices, over_seq(): lax.ppermute(sent, 'seq', pairs(by))  8.46 us
    ppermute x2, waiting for transfers between devices, two_away(): lax.ppermute(wide, axes, [(2 * i, 2 * j) for i, j in moves])  6.45 us
    ppermute x4, starting transfers between devices, shifted(): lax.ppermute(x, axis, [(i, (i + by) % devices) for i in range(devices)])  6.35 us
    ppermute x2, starting transfers between devices, two_away(): lax.ppermute(wide, axes, [(2 * i, 2 * j) for i, j in moves])  4.53 us
    ppermute x4, waiting for transfers between devices, shifted(): lax.ppermute(x, axis, [(i, (i + by) % devices) for i in range(devices)])  3.89 us
    unnamed x10, local copies, waits for them, and re-layouts  3.53 us
    pallas_call x1, Pallas kernels, plan(): pl.pallas_call(lambda *refs: plan_kernel(blocks, shards, caps, *refs), ou...  3.45 us
    pallas_call x1, Pallas kernels, pack_keys(): pl.pallas_call(lambda *refs: key_kernel(blocks, shards, caps, *refs), out...  2.69 us
  transfers between devices with their start and end apart: 18, of which 7 were waited for; matrix products, arithmetic and copies ran while one was open for 0% of the time, Pallas kernels for 19%

profile of v4, /device:TPU:0, one launch (start us, length us, event | category | flops | bytes accessed | tf_op | source)
XLA Modules:
  0.0 51.1 jit_solution(1202629978117054704)
XLA Ops:
  0.0 5.0 %collective-permute-start.2 = (bf16[1024,128]{1,0:T(8,128)(2,1)}, bf16[1024,128]{1,0:T(8,128)(2,1)S(1)}, u32[]{:S(2)}, u32[]{:S(2)}) collective-permute-start(bf16[1024,128]{1,0:T(8,128)(2,1)} %bitcast.9), channel_id=1, source_target_pairs={{0,12},{4,0},{8,4},{12,8},{1,13},{5,1},{9,5},{13,9},{2,14},{6,2},{... | collective-permute-start | bytes 786440 | tf_op jit(solution)/shard_map/ppermute | solution.py:332
  5.0 2.7 %shard_map.46 = (bf16[896,128]{1,0:T(8,128)(2,1)}, bf16[640,128]{1,0:T(8,128)(2,1)}, bf16[384,128]{1,0:T(8,128)(2,1)S(1)}) custom-call(s32[6,64]{1,0:T(8,128)} %bitcast.13, bf16[1024,128]{1,0:T(8,128)(2,1)} %bitcast.10), custom_call_target="tpu_custom_call" | custom-call | tf_op jit(solution)/shard_map/pallas_call | solution.py:166
  7.7 1.9 %collective-permute-start.3 = (bf16[896,128]{1,0:T(8,128)(2,1)}, bf16[896,128]{1,0:T(8,128)(2,1)S(1)}, u32[]{:S(2)}, u32[]{:S(2)}) collective-permute-start(bf16[896,128]{1,0:T(8,128)(2,1)} %get-tuple-element.72), channel_id=1, source_target_pairs={{0,8},{4,12},{8,0},{12,4},{2,10},{6,14},{10,2},{14,6},{16,24},{20,... | collective-permute-start | bytes 688136 | tf_op jit(solution)/shard_map/ppermute | solution.py:357
  9.7 0.7 %collective-permute-start.4 = (bf16[640,128]{1,0:T(8,128)(2,1)}, bf16[640,128]{1,0:T(8,128)(2,1)S(1)}, u32[]{:S(2)}, u32[]{:S(2)}) collective-permute-start(bf16[640,128]{1,0:T(8,128)(2,1)} %get-tuple-element.73), channel_id=1, source_target_pairs={{1,9},{5,13},{9,1},{13,5},{3,11},{7,15},{11,3},{15,7},{17,25},{21,... | collective-permute-start | bytes 491528 | tf_op jit(solution)/shard_map/ppermute | solution.py:358
  10.4 0.0 copy-start
  10.4 0.9 %copy-done = bf16[1024,1,128]{2,0,1:T(8,128)(2,1)S(1)} copy-done((bf16[1024,1,128]{2,0,1:T(8,128)(2,1)S(1)}, bf16[1024,1,128]{2,0,1:T(8,128)(2,1)}, u32[]{:S(2)}) %copy-start) | copy-done | bytes 262168
  11.3 0.0 copy-start.2
  11.3 0.9 %copy-done.2 = bf16[1024,1,128]{2,0,1:T(8,128)(2,1)S(1)} copy-done((bf16[1024,1,128]{2,0,1:T(8,128)(2,1)S(1)}, bf16[1024,1,128]{2,0,1:T(8,128)(2,1)}, u32[]{:S(2)}) %copy-start.2) | copy-done | bytes 262168
  12.3 0.0 copy-start.3
  12.3 0.9 %copy-done.3 = bf16[1024,1,128]{2,0,1:T(8,128)(2,1)S(1)} copy-done((bf16[1024,1,128]{2,0,1:T(8,128)(2,1)S(1)}, bf16[1024,1,128]{2,0,1:T(8,128)(2,1)}, u32[]{:S(2)}) %copy-start.3) | copy-done | bytes 262168
  13.2 0.0 copy-start.4
  13.2 0.7 %copy-done.4 = s32[64,6]{0,1:T(8,128)S(1)} copy-done((s32[64,6]{0,1:T(8,128)S(1)}, s32[64,6]{0,1:T(8,128)}, u32[]{:S(2)}) %copy-start.4) | copy-done | bytes 1560
  13.9 3.4 %shard_map.47 = (bf16[896,128]{1,0:T(8,128)(2,1)S(1)}, bf16[640,128]{1,0:T(8,128)(2,1)S(1)}, bf16[384,128]{1,0:T(8,128)(2,1)S(1)}, bf16[128,256]{1,0:T(8,128)(2,...) custom-call(s32[6,64]{1,0:T(8,128)S(1)} %bitcast.14, ...), custom_call_target="tpu_custom_call" | custom-call | flops 100663296 | bytes 4194304 | tf_op jit(solution)/shard_map/pallas_call | solution.py:182
  17.9 0.1 collective-permute-start.6
  18.0 0.5 collective-permute-start.5
  18.5 0.0 collective-permute-done.4.refs_8_
  18.5 1.6 %collective-permute-done.3.refs_7_ = bf16[896,128]{1,0:T(8,128)(2,1)S(1)} collective-permute-done((bf16[896,128]{1,0:T(8,128)(2,1)}, bf16[896,128]{1,0:T(8,128)(2,1)S(1)}, u32[]{:S(2)}, u32[]{:S(2)}) %collective-permute-start.3) | collective-permute-done | bytes 229408 | tf_op jit(solution)/shard_map/ppermute | solution.py:357
  20.2 0.0 collective-permute-done.2.refs_5_
  20.2 0.1 maximum_select_fusion
  20.2 0.1 collective-permute-start.7
  20.3 0.0 collective-permute-done.6
  20.3 3.9 %collective-permute-done.5 = bf16[128,256]{1,0:T(8,128)(2,1)S(1)} collective-permute-done((bf16[128,256]{1,0:T(8,128)(2,1)S(1)}, bf16[128,256]{1,0:T(8,128)(2,1)S(1)}, u32[]{:S(2)}, u32[]{:S(2)}) %collective-permute-start.5) | collective-permute-done | bytes 65568 | tf_op jit(solution)/shard_map/ppermute | solution.py:332
  24.2 0.7 %collective-permute-start.11 = (bf16[1024,128]{1,0:T(8,128)(2,1)}, bf16[1024,128]{1,0:T(8,128)(2,1)S(1)}, u32[]{:S(2)}, u32[]{:S(2)}) collective-permute-start(bf16[1024,128]{1,0:T(8,128)(2,1)} %bitcast.6), channel_id=1, source_target_pairs={{0,12},{4,0},{8,4},{12,8},{1,13},{5,1},{9,5},{13,9},{2,14},{6,2},{... | collective-permute-start | bytes 786440 | tf_op jit(solution)/shard_map/ppermute | solution.py:332
  25.0 0.0 collective-permute-done.7.refs_6_
  25.0 0.0 copy-start.1
  25.0 2.2 %shard_map.48 = (f32[8,6,128,128]{3,2,1,0:T(8,128)S(1)}, f32[64,128]{1,0:T(8,128)S(1)}, f32[64,128]{1,0:T(8,128)S(1)}) custom-call(s32[8,9]{1,0:T(8,128)S(1)} %get-tuple-element.69.refs_0_, bf16[1024,128]{1,0:T(8,128)(2,1)S(1)} %get-tuple-element.70.refs_1_, f32[8,3,128,128]{3,2,1,0:T(8,128)S(1)} %get-tuple-element.74.refs_2_, ...), custom_call_target="tpu_custom_call" | custom-call | flops 100663296 | bytes 6291456 | tf_op jit(solution)/shard_map/pallas_call | solution.py:411
  27.2 1.3 %collective-permute-start.10 = (f32[64,128]{1,0:T(8,128)S(1)}, f32[64,128]{1,0:T(8,128)S(1)}, u32[]{:S(2)}, u32[]{:S(2)}) collective-permute-start(f32[64,128]{1,0:T(8,128)S(1)} %get-tuple-element.89), channel_id=1, source_target_pairs={{0,4},{4,0},{8,12},{12,8},{1,5},{5,1},{9,13},{13,9},{2,6},{6,2},{1... | collective-permute-start | bytes 98312 | tf_op jit(solution)/shard_map/ppermute | solution.py:343
  28.5 0.0 collective-permute-start.8
  28.5 2.2 %collective-permute-start.9 = (f32[64,128]{1,0:T(8,128)S(1)}, f32[64,128]{1,0:T(8,128)S(1)}, u32[]{:S(2)}, u32[]{:S(2)}) collective-permute-start(f32[64,128]{1,0:T(8,128)S(1)} %get-tuple-element.89), channel_id=1, source_target_pairs={{0,8},{4,12},{8,0},{12,4},{1,9},{5,13},{9,1},{13,5},{2,10},{6,14},... | collective-permute-start | bytes 98312 | tf_op jit(solution)/shard_map/ppermute | solution.py:343
  30.7 2.6 %collective-permute-start.17 = (bf16[896,128]{1,0:T(8,128)(2,1)S(1)}, bf16[896,128]{1,0:T(8,128)(2,1)S(1)}, u32[]{:S(2)}, u32[]{:S(2)}) collective-permute-start(bf16[896,128]{1,0:T(8,128)(2,1)S(1)} %get-tuple-element.96), channel_id=1, source_target_pairs={{0,8},{4,12},{8,0},{12,4},{2,10},{6,14},{10,2},{14,6},{16,24},{20,... | collective-permute-start | bytes 688136 | tf_op jit(solution)/shard_map/ppermute | solution.py:357
  33.4 0.0 collective-permute-done.10
  33.4 0.7 %collective-permute-start.18 = (bf16[640,128]{1,0:T(8,128)(2,1)S(1)}, bf16[640,128]{1,0:T(8,128)(2,1)S(1)}, u32[]{:S(2)}, u32[]{:S(2)}) collective-permute-start(bf16[640,128]{1,0:T(8,128)(2,1)S(1)} %get-tuple-element.97), channel_id=1, source_target_pairs={{1,9},{5,13},{9,1},{13,5},{3,11},{7,15},{11,3},{15,7},{17,25},{21,... | collective-permute-start | bytes 491528 | tf_op jit(solution)/shard_map/ppermute | solution.py:358
  34.0 0.4 collective-permute-done.8
  34.5 0.0 collective-permute-done.9
  34.5 0.0 collective-permute-done.11.refs_8_
  34.5 0.6 %collective-permute-start.12 = (f32[64,128]{1,0:T(8,128)S(1)}, f32[64,128]{1,0:T(8,128)S(1)}, u32[]{:S(2)}, u32[]{:S(2)}) collective-permute-start(f32[64,128]{1,0:T(8,128)S(1)} %add_add_fusion.1.refs_2_), channel_id=1, source_target_pairs={{0,1},{1,0},{2,3},{3,2},{4,5},{5,4},{6,7},{7,6},{8,9},{9,8},{10,11... | collective-permute-start | bytes 98312 | tf_op jit(solution)/shard_map/ppermute | solution.py:336
  35.1 0.9 %collective-permute-done.12.refs_3_ = f32[64,128]{1,0:T(8,128)S(1)} collective-permute-done((f32[64,128]{1,0:T(8,128)S(1)}, f32[64,128]{1,0:T(8,128)S(1)}, u32[]{:S(2)}, u32[]{:S(2)}) %collective-permute-start.12) | collective-permute-done | bytes 32800 | tf_op jit(solution)/shard_map/ppermute | solution.py:336
  36.0 1.1 %shard_map.49 = (f32[64,128]{1,0:T(8,128)S(1)}, f32[64,128]{1,0:T(8,128)S(1)}, f32[64,128]{1,0:T(8,128)S(1)}) custom-call(s32[8,9]{1,0:T(8,128)S(1)} %get-tuple-element.69.refs_0_, f32[8,6,128,128]{3,2,1,0:T(8,128)S(1)} %get-tuple-element.84.refs_1_, f32[64,128]{1,0:T(8,128)S(1)} %add_add_fusion.1.refs_2_, f32[64,128]{1,0:T(8,128)S(1)} %collective-permute-done.12.refs_3_), custom_call_target="tpu_custom_call" | custom-call | flops 7864320 | bytes 4194304 | tf_op jit(solution)/shard_map/pallas_call | solution.py:438
  37.1 3.4 %collective-permute-start.13 = (f32[64,128]{1,0:T(8,128)S(1)}, f32[64,128]{1,0:T(8,128)S(1)}, u32[]{:S(2)}, u32[]{:S(2)}) collective-permute-start(f32[64,128]{1,0:T(8,128)S(1)} %get-tuple-element.94), channel_id=1, source_target_pairs={{0,12},{4,8},{8,4},{12,0},{1,13},{5,9},{9,5},{13,1},{2,14},{6,10},... | collective-permute-start | bytes 98312 | tf_op jit(solution)/shard_map/ppermute | solution.py:343
  40.5 1.5 %collective-permute-start.14 = (f32[64,128]{1,0:T(8,128)S(1)}, f32[64,128]{1,0:T(8,128)S(1)}, u32[]{:S(2)}, u32[]{:S(2)}) collective-permute-start(f32[64,128]{1,0:T(8,128)S(1)} %get-tuple-element.94), channel_id=1, source_target_pairs={{0,8},{4,12},{8,0},{12,4},{1,9},{5,13},{9,1},{13,5},{2,10},{6,14},... | collective-permute-start | bytes 98312 | tf_op jit(solution)/shard_map/ppermute | solution.py:343
  42.0 0.0 collective-permute-start.15
  42.0 0.0 collective-permute-done.18.refs_11_
  42.0 4.8 %collective-permute-done.17.refs_10_ = bf16[896,128]{1,0:T(8,128)(2,1)S(1)} collective-permute-done((bf16[896,128]{1,0:T(8,128)(2,1)S(1)}, bf16[896,128]{1,0:T(8,128)(2,1)S(1)}, u32[]{:S(2)}, u32[]{:S(2)}) %collective-permute-start.17) | collective-permute-done | bytes 229408 | tf_op jit(solution)/shard_map/ppermute | solution.py:357
  46.8 0.1 maximum_select_fusion.1
  46.9 0.1 collective-permute-start.19
  47.0 0.0 collective-permute-done.13
  47.0 0.4 collective-permute-done.14
  47.4 0.0 collective-permute-done.15
  47.4 0.1 collective-permute-start.16
  47.6 1.1 %collective-permute-done.16.refs_4_ = f32[64,128]{1,0:T(8,128)S(1)} collective-permute-done((f32[64,128]{1,0:T(8,128)S(1)}, f32[64,128]{1,0:T(8,128)S(1)}, u32[]{:S(2)}, u32[]{:S(2)}) %collective-permute-start.16) | collective-permute-done | bytes 32800 | tf_op jit(solution)/shard_map/ppermute | solution.py:336
  48.7 0.0 collective-permute-done.19.refs_9_
  48.7 0.0 copy-done.1
  48.7 2.3 %shard_map.50 = bf16[1024,128]{1,0:T(8,128)(2,1)} custom-call(s32[8,9]{1,0:T(8,128)S(1)} %get-tuple-element.69.refs_0_, f32[8,6,128,128]{3,2,1,0:T(8,128)S(1)} %get-tuple-element.84.refs_1_, f32[64,128]{1,0:T(8,128)S(1)} %get-tuple-element.92.refs_2_, f32[64,128]{1,0:T(8,128)S(1)} %add_add_fusion.refs_3_, f32[64,128]{1,0:T(8,128)S(1)} %collective-permute-done.16.refs_4_, ...), custom_call_target="tpu_custom_call" | custom-call | flops 201326592 | bytes 6291456 | tf_op jit(solution)/shard_map/pallas_call | solution.py:456
  (7 shorter events, 0.1 us)
Async XLA Ops:
  0.0 20.2 %collective-permute-start.2 = (bf16[1024,128]{1,0:T(8,128)(2,1)}, bf16[1024,128]{1,0:T(8,128)(2,1)S(1)}, u32[]{:S(2)}, u32[]{:S(2)}) collective-permute-start(bf16[1024,128]{1,0:T(8,128)(2,1)} %bitcast.9), channel_id=1, source_target_pairs={{0,12},{4,0},{8,4},{12,8},{1,13},{5,1},{9,5},{13,9},{2,14},{6,2},{... | collective-permute-start | bytes 786440 | tf_op jit(solution)/shard_map/ppermute | solution.py:332
  7.7 12.4 %collective-permute-start.3 = (bf16[896,128]{1,0:T(8,128)(2,1)}, bf16[896,128]{1,0:T(8,128)(2,1)S(1)}, u32[]{:S(2)}, u32[]{:S(2)}) collective-permute-start(bf16[896,128]{1,0:T(8,128)(2,1)} %get-tuple-element.72), channel_id=1, source_target_pairs={{0,8},{4,12},{8,0},{12,4},{2,10},{6,14},{10,2},{14,6},{16,24},{20,... | collective-permute-start | bytes 688136 | tf_op jit(solution)/shard_map/ppermute | solution.py:357
  9.7 8.8 %collective-permute-start.4 = (bf16[640,128]{1,0:T(8,128)(2,1)}, bf16[640,128]{1,0:T(8,128)(2,1)S(1)}, u32[]{:S(2)}, u32[]{:S(2)}) collective-permute-start(bf16[640,128]{1,0:T(8,128)(2,1)} %get-tuple-element.73), channel_id=1, source_target_pairs={{1,9},{5,13},{9,1},{13,5},{3,11},{7,15},{11,3},{15,7},{17,25},{21,... | collective-permute-start | bytes 491528 | tf_op jit(solution)/shard_map/ppermute | solution.py:358
  10.4 1.0 %copy-start = (bf16[1024,1,128]{2,0,1:T(8,128)(2,1)S(1)}, bf16[1024,1,128]{2,0,1:T(8,128)(2,1)}, u32[]{:S(2)}) copy-start(bf16[1024,1,128]{2,0,1:T(8,128)(2,1)} %param.8) | copy-start | bytes 786436
  11.3 0.9 %copy-start.2 = (bf16[1024,1,128]{2,0,1:T(8,128)(2,1)S(1)}, bf16[1024,1,128]{2,0,1:T(8,128)(2,1)}, u32[]{:S(2)}) copy-start(bf16[1024,1,128]{2,0,1:T(8,128)(2,1)} %param.7) | copy-start | bytes 786436
  12.3 0.9 %copy-start.3 = (bf16[1024,1,128]{2,0,1:T(8,128)(2,1)S(1)}, bf16[1024,1,128]{2,0,1:T(8,128)(2,1)}, u32[]{:S(2)}) copy-start(bf16[1024,1,128]{2,0,1:T(8,128)(2,1)} %param.6) | copy-start | bytes 786436
  13.2 0.7 %copy-start.4 = (s32[64,6]{0,1:T(8,128)S(1)}, s32[64,6]{0,1:T(8,128)}, u32[]{:S(2)}) copy-start(s32[64,6]{0,1:T(8,128)} %param.9) | copy-start | bytes 4612
  17.9 2.4 %collective-permute-start.6 = (bf16[128,256]{1,0:T(8,128)(2,1)S(1)}, bf16[128,256]{1,0:T(8,128)(2,1)S(1)}, u32[]{:S(2)}, u32[]{:S(2)}) collective-permute-start(bf16[128,256]{1,0:T(8,128)(2,1)S(1)} %get-tuple-element.76), channel_id=1, source_target_pairs={{0,13},{1,0},{4,1},{5,4},{8,5},{9,8},{12,9},{13,12},{2,15},{3,2},{... | collective-permute-start | bytes 196616 | tf_op jit(solution)/shard_map/ppermute | solution.py:332
  18.0 6.2 %collective-permute-start.5 = (bf16[128,256]{1,0:T(8,128)(2,1)S(1)}, bf16[128,256]{1,0:T(8,128)(2,1)S(1)}, u32[]{:S(2)}, u32[]{:S(2)}) collective-permute-start(bf16[128,256]{1,0:T(8,128)(2,1)S(1)} %get-tuple-element.75), channel_id=1, source_target_pairs={{0,1},{1,4},{4,5},{5,8},{8,9},{9,12},{12,13},{13,0},{2,3},{3,6},{6... | collective-permute-start | bytes 196616 | tf_op jit(solution)/shard_map/ppermute | solution.py:332
  20.2 4.7 %collective-permute-start.7 = (bf16[1024,128]{1,0:T(8,128)(2,1)S(1)}, bf16[1024,128]{1,0:T(8,128)(2,1)S(1)}, u32[]{:S(2)}, u32[]{:S(2)}) collective-permute-start(bf16[1024,128]{1,0:T(8,128)(2,1)S(1)} %maximum_select_fusion), channel_id=1, source_target_pairs={{0,1},{1,0},{2,3},{3,2},{4,5},{5,4},{6,7},{7,6},{8,9},{9,8},{10,11... | collective-permute-start | bytes 786440 | tf_op jit(solution)/shard_map/ppermute | solution.py:336
  24.2 10.3 %collective-permute-start.11 = (bf16[1024,128]{1,0:T(8,128)(2,1)}, bf16[1024,128]{1,0:T(8,128)(2,1)S(1)}, u32[]{:S(2)}, u32[]{:S(2)}) collective-permute-start(bf16[1024,128]{1,0:T(8,128)(2,1)} %bitcast.6), channel_id=1, source_target_pairs={{0,12},{4,0},{8,4},{12,8},{1,13},{5,1},{9,5},{13,9},{2,14},{6,2},{... | collective-permute-start | bytes 786440 | tf_op jit(solution)/shard_map/ppermute | solution.py:332
  25.0 23.7 %copy-start.1 = (bf16[1024,1,128]{2,0,1:T(8,128)(2,1)S(1)}, bf16[1024,1,128]{2,0,1:T(8,128)(2,1)}, u32[]{:S(2)}) copy-start(bf16[1024,1,128]{2,0,1:T(8,128)(2,1)} %param.8) | copy-start | bytes 786436
  27.2 6.2 %collective-permute-start.10 = (f32[64,128]{1,0:T(8,128)S(1)}, f32[64,128]{1,0:T(8,128)S(1)}, u32[]{:S(2)}, u32[]{:S(2)}) collective-permute-start(f32[64,128]{1,0:T(8,128)S(1)} %get-tuple-element.89), channel_id=1, source_target_pairs={{0,4},{4,0},{8,12},{12,8},{1,5},{5,1},{9,13},{13,9},{2,6},{6,2},{1... | collective-permute-start | bytes 98312 | tf_op jit(solution)/shard_map/ppermute | solution.py:343
  28.5 6.0 %collective-permute-start.8 = (f32[64,128]{1,0:T(8,128)S(1)}, f32[64,128]{1,0:T(8,128)S(1)}, u32[]{:S(2)}, u32[]{:S(2)}) collective-permute-start(f32[64,128]{1,0:T(8,128)S(1)} %get-tuple-element.89), channel_id=1, source_target_pairs={{0,12},{4,8},{8,4},{12,0},{1,13},{5,9},{9,5},{13,1},{2,14},{6,10},... | collective-permute-start | bytes 98312 | tf_op jit(solution)/shard_map/ppermute | solution.py:343
  28.5 6.0 %collective-permute-start.9 = (f32[64,128]{1,0:T(8,128)S(1)}, f32[64,128]{1,0:T(8,128)S(1)}, u32[]{:S(2)}, u32[]{:S(2)}) collective-permute-start(f32[64,128]{1,0:T(8,128)S(1)} %get-tuple-element.89), channel_id=1, source_target_pairs={{0,8},{4,12},{8,0},{12,4},{1,9},{5,13},{9,1},{13,5},{2,10},{6,14},... | collective-permute-start | bytes 98312 | tf_op jit(solution)/shard_map/ppermute | solution.py:343
  30.7 16.1 %collective-permute-start.17 = (bf16[896,128]{1,0:T(8,128)(2,1)S(1)}, bf16[896,128]{1,0:T(8,128)(2,1)S(1)}, u32[]{:S(2)}, u32[]{:S(2)}) collective-permute-start(bf16[896,128]{1,0:T(8,128)(2,1)S(1)} %get-tuple-element.96), channel_id=1, source_target_pairs={{0,8},{4,12},{8,0},{12,4},{2,10},{6,14},{10,2},{14,6},{16,24},{20,... | collective-permute-start | bytes 688136 | tf_op jit(solution)/shard_map/ppermute | solution.py:357
  33.4 8.7 %collective-permute-start.18 = (bf16[640,128]{1,0:T(8,128)(2,1)S(1)}, bf16[640,128]{1,0:T(8,128)(2,1)S(1)}, u32[]{:S(2)}, u32[]{:S(2)}) collective-permute-start(bf16[640,128]{1,0:T(8,128)(2,1)S(1)} %get-tuple-element.97), channel_id=1, source_target_pairs={{1,9},{5,13},{9,1},{13,5},{3,11},{7,15},{11,3},{15,7},{17,25},{21,... | collective-permute-start | bytes 491528 | tf_op jit(solution)/shard_map/ppermute | solution.py:358
  34.5 1.4 %collective-permute-start.12 = (f32[64,128]{1,0:T(8,128)S(1)}, f32[64,128]{1,0:T(8,128)S(1)}, u32[]{:S(2)}, u32[]{:S(2)}) collective-permute-start(f32[64,128]{1,0:T(8,128)S(1)} %add_add_fusion.1.refs_2_), channel_id=1, source_target_pairs={{0,1},{1,0},{2,3},{3,2},{4,5},{5,4},{6,7},{7,6},{8,9},{9,8},{10,11... | collective-permute-start | bytes 98312 | tf_op jit(solution)/shard_map/ppermute | solution.py:336
  37.1 9.9 %collective-permute-start.13 = (f32[64,128]{1,0:T(8,128)S(1)}, f32[64,128]{1,0:T(8,128)S(1)}, u32[]{:S(2)}, u32[]{:S(2)}) collective-permute-start(f32[64,128]{1,0:T(8,128)S(1)} %get-tuple-element.94), channel_id=1, source_target_pairs={{0,12},{4,8},{8,4},{12,0},{1,13},{5,9},{9,5},{13,1},{2,14},{6,10},... | collective-permute-start | bytes 98312 | tf_op jit(solution)/shard_map/ppermute | solution.py:343
  40.5 6.9 %collective-permute-start.14 = (f32[64,128]{1,0:T(8,128)S(1)}, f32[64,128]{1,0:T(8,128)S(1)}, u32[]{:S(2)}, u32[]{:S(2)}) collective-permute-start(f32[64,128]{1,0:T(8,128)S(1)} %get-tuple-element.94), channel_id=1, source_target_pairs={{0,8},{4,12},{8,0},{12,4},{1,9},{5,13},{9,1},{13,5},{2,10},{6,14},... | collective-permute-start | bytes 98312 | tf_op jit(solution)/shard_map/ppermute | solution.py:343
  42.0 5.4 %collective-permute-start.15 = (f32[64,128]{1,0:T(8,128)S(1)}, f32[64,128]{1,0:T(8,128)S(1)}, u32[]{:S(2)}, u32[]{:S(2)}) collective-permute-start(f32[64,128]{1,0:T(8,128)S(1)} %get-tuple-element.94), channel_id=1, source_target_pairs={{0,4},{4,0},{8,12},{12,8},{1,5},{5,1},{9,13},{13,9},{2,6},{6,2},{1... | collective-permute-start | bytes 98312 | tf_op jit(solution)/shard_map/ppermute | solution.py:343
  46.9 1.8 %collective-permute-start.19 = (bf16[1024,128]{1,0:T(8,128)(2,1)S(1)}, bf16[1024,128]{1,0:T(8,128)(2,1)S(1)}, u32[]{:S(2)}, u32[]{:S(2)}) collective-permute-start(bf16[1024,128]{1,0:T(8,128)(2,1)S(1)} %maximum_select_fusion.1), channel_id=1, source_target_pairs={{0,1},{1,0},{2,3},{3,2},{4,5},{5,4},{6,7},{7,6},{8,9},{9,8},{10,11... | collective-permute-start | bytes 786440 | tf_op jit(solution)/shard_map/ppermute | solution.py:336
  47.4 1.3 %collective-permute-start.16 = (f32[64,128]{1,0:T(8,128)S(1)}, f32[64,128]{1,0:T(8,128)S(1)}, u32[]{:S(2)}, u32[]{:S(2)}) collective-permute-start(f32[64,128]{1,0:T(8,128)S(1)} %add_add_fusion.refs_3_), channel_id=1, source_target_pairs={{0,1},{1,0},{2,3},{3,2},{4,5},{5,4},{6,7},{7,6},{8,9},{9,8},{10,11... | collective-permute-start | bytes 98312 | tf_op jit(solution)/shard_map/ppermute | solution.py:336

commit v5 on v4

--- a/solution.py
+++ b/solution.py
@@ -403,10 +403,9 @@
     low = shifted(edges_low, axes, 1)
     high = shifted(edges_high, axes, -1)
 
-    near_scores, v_in, k_near, k_wide, k_slim = lax.optimization_barrier(
-        (near_scores, v, k_near, k_wide, k_slim)
-    )
+    near_scores, v_in = lax.optimization_barrier((near_scores, v))
     v_near = shifted(v_in, "seq", -1)
+    k_near, k_wide, k_slim = lax.optimization_barrier((k_near, k_wide, k_slim))
     k_other = with_swap(k_near, k_wide, k_rest, caps, rep)
     exps, sums, sent = pl.pallas_call(
         lambda *refs: score_kernel(blocks, caps, *refs),

time: 51.5 us -> 50.6 us (0.983)
  waiting for transfers between devices: 13.2 us -> 9.39 us
  starting transfers between devices: 21.6 us -> 24.4 us
    ppermute x4, waiting for transfers between devices: 3.89 us -> 1.56 us  [shifted(): lax.ppermute(x, axis, [(i, (i + by) % devices) for i in range(devices)])]
    ppermute x4, starting transfers between devices: 6.35 us -> 8.42 us  [shifted(): lax.ppermute(x, axis, [(i, (i + by) % devices) for i in range(devices)])]
    ppermute x2, waiting for transfers between devices: 6.45 us -> 4.89 us  [two_away(): lax.ppermute(wide, axes, [(2 * i, 2 * j) for i, j in moves])]
    ppermute x4, starting transfers between devices: 0.87 us -> 1.54 us  [swapped(): return lax.ppermute(x, 'rep', [(0, 1), (1, 0)])]
    ppermute x2, starting transfers between devices: 4.53 us -> 5.07 us  [two_away(): lax.ppermute(wide, axes, [(2 * i, 2 * j) for i, j in moves])]
  transfers between devices with their start and end apart: 18 -> 18, of which waited for: 7 -> 5; matrix products, arithmetic and copies ran while one was open for 0% -> 0% of each run, Pallas kernels for 19% -> 19%
where the time goes in v5:
time: 50.6 us; the launch traced here: 50.1 us
  starting transfers between devices  24.4 us (48%)
  Pallas kernels  11.8 us (23%)
  waiting for transfers between devices  9.39 us (19%)
  local copies, waits for them, and re-layouts  3.56 us (7%)
  between operations  0.79 us (2%)
    ppermute x4, starting transfers between devices, shifted(): lax.ppermute(x, axis, [(i, (i + by) % devices) for i in range(devices)])  8.42 us
    ppermute x6, starting transfers between devices, over_seq(): lax.ppermute(sent, 'seq', pairs(by))  8 us
    ppermute x2, starting transfers between devices, two_away(): lax.ppermute(wide, axes, [(2 * i, 2 * j) for i, j in moves])  5.07 us
    ppermute x2, waiting for transfers between devices, two_away(): lax.ppermute(wide, axes, [(2 * i, 2 * j) for i, j in moves])  4.89 us
    unnamed x10, local copies, waits for them, and re-layouts  3.54 us
    pallas_call x1, Pallas kernels, plan(): pl.pallas_call(lambda *refs: plan_kernel(blocks, shards, caps, *refs), ou...  3.45 us
    pallas_call x1, Pallas kernels, pack_keys(): pl.pallas_call(lambda *refs: key_kernel(blocks, shards, caps, *refs), out...  2.69 us
    ppermute x4, waiting for transfers between devices, swapped(): return lax.ppermute(x, 'rep', [(0, 1), (1, 0)])  2.38 us
  transfers between devices with their start and end apart: 18, of which 5 were waited for; matrix products, arithmetic and copies ran while one was open for 0% of the time, Pallas kernels for 19%

profile of v5, /device:TPU:0, one launch (start us, length us, event | category | flops | bytes accessed | tf_op | source)
XLA Modules:
  0.0 50.1 jit_solution(6100112726414485053)
XLA Ops:
  0.0 5.0 %collective-permute-start.4 = (bf16[1024,128]{1,0:T(8,128)(2,1)}, bf16[1024,128]{1,0:T(8,128)(2,1)S(1)}, u32[]{:S(2)}, u32[]{:S(2)}) collective-permute-start(bf16[1024,128]{1,0:T(8,128)(2,1)} %bitcast.9), channel_id=1, source_target_pairs={{0,12},{4,0},{8,4},{12,8},{1,13},{5,1},{9,5},{13,9},{2,14},{6,2},{... | collective-permute-start | bytes 786440 | tf_op jit(solution)/shard_map/ppermute | solution.py:332
  5.0 2.7 %shard_map.46 = (bf16[896,128]{1,0:T(8,128)(2,1)}, bf16[640,128]{1,0:T(8,128)(2,1)}, bf16[384,128]{1,0:T(8,128)(2,1)S(1)}) custom-call(s32[6,64]{1,0:T(8,128)} %bitcast.13, bf16[1024,128]{1,0:T(8,128)(2,1)} %bitcast.10), custom_call_target="tpu_custom_call" | custom-call | tf_op jit(solution)/shard_map/pallas_call | solution.py:166
  7.7 1.9 %collective-permute-start.5 = (bf16[896,128]{1,0:T(8,128)(2,1)}, bf16[896,128]{1,0:T(8,128)(2,1)S(1)}, u32[]{:S(2)}, u32[]{:S(2)}) collective-permute-start(bf16[896,128]{1,0:T(8,128)(2,1)} %get-tuple-element.75), channel_id=1, source_target_pairs={{0,8},{4,12},{8,0},{12,4},{2,10},{6,14},{10,2},{14,6},{16,24},{20,... | collective-permute-start | bytes 688136 | tf_op jit(solution)/shard_map/ppermute | solution.py:357
  9.7 0.7 %collective-permute-start.6 = (bf16[640,128]{1,0:T(8,128)(2,1)}, bf16[640,128]{1,0:T(8,128)(2,1)S(1)}, u32[]{:S(2)}, u32[]{:S(2)}) collective-permute-start(bf16[640,128]{1,0:T(8,128)(2,1)} %get-tuple-element.76), channel_id=1, source_target_pairs={{1,9},{5,13},{9,1},{13,5},{3,11},{7,15},{11,3},{15,7},{17,25},{21,... | collective-permute-start | bytes 491528 | tf_op jit(solution)/shard_map/ppermute | solution.py:358
  10.4 0.0 copy-start
  10.4 0.9 %copy-done = bf16[1024,1,128]{2,0,1:T(8,128)(2,1)S(1)} copy-done((bf16[1024,1,128]{2,0,1:T(8,128)(2,1)S(1)}, bf16[1024,1,128]{2,0,1:T(8,128)(2,1)}, u32[]{:S(2)}) %copy-start) | copy-done | bytes 262168
  11.3 0.0 copy-start.2
  11.3 0.9 %copy-done.2 = bf16[1024,1,128]{2,0,1:T(8,128)(2,1)S(1)} copy-done((bf16[1024,1,128]{2,0,1:T(8,128)(2,1)S(1)}, bf16[1024,1,128]{2,0,1:T(8,128)(2,1)}, u32[]{:S(2)}) %copy-start.2) | copy-done | bytes 262168
  12.3 0.0 copy-start.3
  12.3 0.9 %copy-done.3 = bf16[1024,1,128]{2,0,1:T(8,128)(2,1)S(1)} copy-done((bf16[1024,1,128]{2,0,1:T(8,128)(2,1)S(1)}, bf16[1024,1,128]{2,0,1:T(8,128)(2,1)}, u32[]{:S(2)}) %copy-start.3) | copy-done | bytes 262168
  13.2 0.0 copy-start.4
  13.2 0.7 %copy-done.4 = s32[64,6]{0,1:T(8,128)S(1)} copy-done((s32[64,6]{0,1:T(8,128)S(1)}, s32[64,6]{0,1:T(8,128)}, u32[]{:S(2)}) %copy-start.4) | copy-done | bytes 1560
  13.9 3.4 %shard_map.47 = (bf16[896,128]{1,0:T(8,128)(2,1)S(1)}, bf16[640,128]{1,0:T(8,128)(2,1)S(1)}, bf16[384,128]{1,0:T(8,128)(2,1)S(1)}, bf16[128,256]{1,0:T(8,128)(2,...) custom-call(s32[6,64]{1,0:T(8,128)S(1)} %bitcast.14, ...), custom_call_target="tpu_custom_call" | custom-call | flops 100663296 | bytes 4194304 | tf_op jit(solution)/shard_map/pallas_call | solution.py:182
  17.9 0.1 collective-permute-start.3
  18.0 0.5 collective-permute-start.2
  18.5 0.0 collective-permute-done.6.refs_8_
  18.5 2.8 %collective-permute-start.11 = (bf16[1024,128]{1,0:T(8,128)(2,1)}, bf16[1024,128]{1,0:T(8,128)(2,1)S(1)}, u32[]{:S(2)}, u32[]{:S(2)}) collective-permute-start(bf16[1024,128]{1,0:T(8,128)(2,1)} %bitcast.6), channel_id=1, source_target_pairs={{0,12},{4,0},{8,4},{12,8},{1,13},{5,1},{9,5},{13,9},{2,14},{6,2},{... | collective-permute-start | bytes 786440 | tf_op jit(solution)/shard_map/ppermute | solution.py:332
  21.3 0.0 collective-permute-done.5.refs_7_
  21.3 0.0 collective-permute-done.4.refs_5_
  21.3 0.1 maximum_select_fusion
  21.4 1.3 %collective-permute-start.7 = (bf16[1024,128]{1,0:T(8,128)(2,1)S(1)}, bf16[1024,128]{1,0:T(8,128)(2,1)S(1)}, u32[]{:S(2)}, u32[]{:S(2)}) collective-permute-start(bf16[1024,128]{1,0:T(8,128)(2,1)S(1)} %maximum_select_fusion), channel_id=1, source_target_pairs={{0,1},{1,0},{2,3},{3,2},{4,5},{5,4},{6,7},{7,6},{8,9},{9,8},{10,11... | collective-permute-start | bytes 786440 | tf_op jit(solution)/shard_map/ppermute | solution.py:336
  22.7 0.0 collective-permute-done.3
  22.8 1.6 %collective-permute-done.2 = bf16[128,256]{1,0:T(8,128)(2,1)S(1)} collective-permute-done((bf16[128,256]{1,0:T(8,128)(2,1)S(1)}, bf16[128,256]{1,0:T(8,128)(2,1)S(1)}, u32[]{:S(2)}, u32[]{:S(2)}) %collective-permute-start.2) | collective-permute-done | bytes 65568 | tf_op jit(solution)/shard_map/ppermute | solution.py:332
  24.3 0.0 collective-permute-done.7.refs_6_
  24.3 0.0 copy-start.1
  24.3 2.2 %shard_map.48 = (f32[8,6,128,128]{3,2,1,0:T(8,128)S(1)}, f32[64,128]{1,0:T(8,128)S(1)}, f32[64,128]{1,0:T(8,128)S(1)}) custom-call(s32[8,9]{1,0:T(8,128)S(1)} %get-tuple-element.69.refs_0_, bf16[1024,128]{1,0:T(8,128)(2,1)S(1)} %get-tuple-element.70.refs_1_, f32[8,3,128,128]{3,2,1,0:T(8,128)S(1)} %get-tuple-element.72.refs_2_, ...), custom_call_target="tpu_custom_call" | custom-call | flops 100663296 | bytes 6291456 | tf_op jit(solution)/shard_map/pallas_call | solution.py:410
  26.6 0.1 collective-permute-start.10
  26.6 1.8 %collective-permute-start.8 = (f32[64,128]{1,0:T(8,128)S(1)}, f32[64,128]{1,0:T(8,128)S(1)}, u32[]{:S(2)}, u32[]{:S(2)}) collective-permute-start(f32[64,128]{1,0:T(8,128)S(1)} %get-tuple-element.89), channel_id=1, source_target_pairs={{0,12},{4,8},{8,4},{12,0},{1,13},{5,9},{9,5},{13,1},{2,14},{6,10},... | collective-permute-start | bytes 98312 | tf_op jit(solution)/shard_map/ppermute | solution.py:343
  28.5 1.7 %collective-permute-start.9 = (f32[64,128]{1,0:T(8,128)S(1)}, f32[64,128]{1,0:T(8,128)S(1)}, u32[]{:S(2)}, u32[]{:S(2)}) collective-permute-start(f32[64,128]{1,0:T(8,128)S(1)} %get-tuple-element.89), channel_id=1, source_target_pairs={{0,8},{4,12},{8,0},{12,4},{1,9},{5,13},{9,1},{13,5},{2,10},{6,14},... | collective-permute-start | bytes 98312 | tf_op jit(solution)/shard_map/ppermute | solution.py:343
  30.1 3.1 %collective-permute-start.17 = (bf16[896,128]{1,0:T(8,128)(2,1)S(1)}, bf16[896,128]{1,0:T(8,128)(2,1)S(1)}, u32[]{:S(2)}, u32[]{:S(2)}) collective-permute-start(bf16[896,128]{1,0:T(8,128)(2,1)S(1)} %get-tuple-element.96), channel_id=1, source_target_pairs={{0,8},{4,12},{8,0},{12,4},{2,10},{6,14},{10,2},{14,6},{16,24},{20,... | collective-permute-start | bytes 688136 | tf_op jit(solution)/shard_map/ppermute | solution.py:357
  33.3 0.0 collective-permute-done.10
  33.3 0.7 %collective-permute-start.18 = (bf16[640,128]{1,0:T(8,128)(2,1)S(1)}, bf16[640,128]{1,0:T(8,128)(2,1)S(1)}, u32[]{:S(2)}, u32[]{:S(2)}) collective-permute-start(bf16[640,128]{1,0:T(8,128)(2,1)S(1)} %get-tuple-element.97), channel_id=1, source_target_pairs={{1,9},{5,13},{9,1},{13,5},{3,11},{7,15},{11,3},{15,7},{17,25},{21,... | collective-permute-start | bytes 491528 | tf_op jit(solution)/shard_map/ppermute | solution.py:358
  34.0 0.0 collective-permute-done.8
  34.0 0.0 collective-permute-done.9
  34.0 0.0 collective-permute-done.11.refs_8_
  34.0 0.1 collective-permute-start.12
  34.1 1.2 %collective-permute-done.12.refs_3_ = f32[64,128]{1,0:T(8,128)S(1)} collective-permute-done((f32[64,128]{1,0:T(8,128)S(1)}, f32[64,128]{1,0:T(8,128)S(1)}, u32[]{:S(2)}, u32[]{:S(2)}) %collective-permute-start.12) | collective-permute-done | bytes 32800 | tf_op jit(solution)/shard_map/ppermute | solution.py:336
  35.3 1.2 %shard_map.49 = (f32[64,128]{1,0:T(8,128)S(1)}, f32[64,128]{1,0:T(8,128)S(1)}, f32[64,128]{1,0:T(8,128)S(1)}) custom-call(s32[8,9]{1,0:T(8,128)S(1)} %get-tuple-element.69.refs_0_, f32[8,6,128,128]{3,2,1,0:T(8,128)S(1)} %get-tuple-element.84.refs_1_, f32[64,128]{1,0:T(8,128)S(1)} %add_add_fusion.1.refs_2_, f32[64,128]{1,0:T(8,128)S(1)} %collective-permute-done.12.refs_3_), custom_call_target="tpu_custom_call" | custom-call | flops 7864320 | bytes 4194304 | tf_op jit(solution)/shard_map/pallas_call | solution.py:437
  36.5 2.1 %collective-permute-start.13 = (f32[64,128]{1,0:T(8,128)S(1)}, f32[64,128]{1,0:T(8,128)S(1)}, u32[]{:S(2)}, u32[]{:S(2)}) collective-permute-start(f32[64,128]{1,0:T(8,128)S(1)} %get-tuple-element.94), channel_id=1, source_target_pairs={{0,12},{4,8},{8,4},{12,0},{1,13},{5,9},{9,5},{13,1},{2,14},{6,10},... | collective-permute-start | bytes 98312 | tf_op jit(solution)/shard_map/ppermute | solution.py:343
  38.6 0.5 collective-permute-start.14
  39.1 1.8 %collective-permute-start.15 = (f32[64,128]{1,0:T(8,128)S(1)}, f32[64,128]{1,0:T(8,128)S(1)}, u32[]{:S(2)}, u32[]{:S(2)}) collective-permute-start(f32[64,128]{1,0:T(8,128)S(1)} %get-tuple-element.94), channel_id=1, source_target_pairs={{0,4},{4,0},{8,12},{12,8},{1,5},{5,1},{9,13},{13,9},{2,6},{6,2},{1... | collective-permute-start | bytes 98312 | tf_op jit(solution)/shard_map/ppermute | solution.py:343
  40.9 0.0 collective-permute-done.18.refs_11_
  40.9 4.9 %collective-permute-done.17.refs_10_ = bf16[896,128]{1,0:T(8,128)(2,1)S(1)} collective-permute-done((bf16[896,128]{1,0:T(8,128)(2,1)S(1)}, bf16[896,128]{1,0:T(8,128)(2,1)S(1)}, u32[]{:S(2)}, u32[]{:S(2)}) %collective-permute-start.17) | collective-permute-done | bytes 229408 | tf_op jit(solution)/shard_map/ppermute | solution.py:357
  45.8 0.1 maximum_select_fusion.1
  45.9 0.1 collective-permute-start.19
  46.0 0.0 collective-permute-done.13
  46.0 0.5 %collective-permute-done.14 = f32[64,128]{1,0:T(8,128)S(1)} collective-permute-done((f32[64,128]{1,0:T(8,128)S(1)}, f32[64,128]{1,0:T(8,128)S(1)}, u32[]{:S(2)}, u32[]{:S(2)}) %collective-permute-start.14) | collective-permute-done | bytes 32800 | tf_op jit(solution)/shard_map/ppermute | solution.py:343
  46.5 0.0 collective-permute-done.15
  46.5 0.1 collective-permute-start.16
  46.6 1.2 %collective-permute-done.16.refs_4_ = f32[64,128]{1,0:T(8,128)S(1)} collective-permute-done((f32[64,128]{1,0:T(8,128)S(1)}, f32[64,128]{1,0:T(8,128)S(1)}, u32[]{:S(2)}, u32[]{:S(2)}) %collective-permute-start.16) | collective-permute-done | bytes 32800 | tf_op jit(solution)/shard_map/ppermute | solution.py:336
  47.8 0.0 collective-permute-done.19.refs_9_
  47.8 0.0 copy-done.1
  47.8 2.3 %shard_map.50 = bf16[1024,128]{1,0:T(8,128)(2,1)} custom-call(s32[8,9]{1,0:T(8,128)S(1)} %get-tuple-element.69.refs_0_, f32[8,6,128,128]{3,2,1,0:T(8,128)S(1)} %get-tuple-element.84.refs_1_, f32[64,128]{1,0:T(8,128)S(1)} %get-tuple-element.92.refs_2_, f32[64,128]{1,0:T(8,128)S(1)} %add_add_fusion.refs_3_, f32[64,128]{1,0:T(8,128)S(1)} %collective-permute-done.16.refs_4_, ...), custom_call_target="tpu_custom_call" | custom-call | flops 201326592 | bytes 6291456 | tf_op jit(solution)/shard_map/pallas_call | solution.py:455
  (7 shorter events, 0.1 us)
Async XLA Ops:
  0.0 21.3 %collective-permute-start.4 = (bf16[1024,128]{1,0:T(8,128)(2,1)}, bf16[1024,128]{1,0:T(8,128)(2,1)S(1)}, u32[]{:S(2)}, u32[]{:S(2)}) collective-permute-start(bf16[1024,128]{1,0:T(8,128)(2,1)} %bitcast.9), channel_id=1, source_target_pairs={{0,12},{4,0},{8,4},{12,8},{1,13},{5,1},{9,5},{13,9},{2,14},{6,2},{... | collective-permute-start | bytes 786440 | tf_op jit(solution)/shard_map/ppermute | solution.py:332
  7.7 13.6 %collective-permute-start.5 = (bf16[896,128]{1,0:T(8,128)(2,1)}, bf16[896,128]{1,0:T(8,128)(2,1)S(1)}, u32[]{:S(2)}, u32[]{:S(2)}) collective-permute-start(bf16[896,128]{1,0:T(8,128)(2,1)} %get-tuple-element.75), channel_id=1, source_target_pairs={{0,8},{4,12},{8,0},{12,4},{2,10},{6,14},{10,2},{14,6},{16,24},{20,... | collective-permute-start | bytes 688136 | tf_op jit(solution)/shard_map/ppermute | solution.py:357
  9.7 8.8 %collective-permute-start.6 = (bf16[640,128]{1,0:T(8,128)(2,1)}, bf16[640,128]{1,0:T(8,128)(2,1)S(1)}, u32[]{:S(2)}, u32[]{:S(2)}) collective-permute-start(bf16[640,128]{1,0:T(8,128)(2,1)} %get-tuple-element.76), channel_id=1, source_target_pairs={{1,9},{5,13},{9,1},{13,5},{3,11},{7,15},{11,3},{15,7},{17,25},{21,... | collective-permute-start | bytes 491528 | tf_op jit(solution)/shard_map/ppermute | solution.py:358
  10.4 1.0 %copy-start = (bf16[1024,1,128]{2,0,1:T(8,128)(2,1)S(1)}, bf16[1024,1,128]{2,0,1:T(8,128)(2,1)}, u32[]{:S(2)}) copy-start(bf16[1024,1,128]{2,0,1:T(8,128)(2,1)} %param.8) | copy-start | bytes 786436
  11.3 0.9 %copy-start.2 = (bf16[1024,1,128]{2,0,1:T(8,128)(2,1)S(1)}, bf16[1024,1,128]{2,0,1:T(8,128)(2,1)}, u32[]{:S(2)}) copy-start(bf16[1024,1,128]{2,0,1:T(8,128)(2,1)} %param.7) | copy-start | bytes 786436
  12.3 0.9 %copy-start.3 = (bf16[1024,1,128]{2,0,1:T(8,128)(2,1)S(1)}, bf16[1024,1,128]{2,0,1:T(8,128)(2,1)}, u32[]{:S(2)}) copy-start(bf16[1024,1,128]{2,0,1:T(8,128)(2,1)} %param.6) | copy-start | bytes 786436
  13.2 0.7 %copy-start.4 = (s32[64,6]{0,1:T(8,128)S(1)}, s32[64,6]{0,1:T(8,128)}, u32[]{:S(2)}) copy-start(s32[64,6]{0,1:T(8,128)} %param.9) | copy-start | bytes 4612
  17.9 4.8 %collective-permute-start.3 = (bf16[128,256]{1,0:T(8,128)(2,1)S(1)}, bf16[128,256]{1,0:T(8,128)(2,1)S(1)}, u32[]{:S(2)}, u32[]{:S(2)}) collective-permute-start(bf16[128,256]{1,0:T(8,128)(2,1)S(1)} %get-tuple-element.74), channel_id=1, source_target_pairs={{0,13},{1,0},{4,1},{5,4},{8,5},{9,8},{12,9},{13,12},{2,15},{3,2},{... | collective-permute-start | bytes 196616 | tf_op jit(solution)/shard_map/ppermute | solution.py:332
  18.0 6.3 %collective-permute-start.2 = (bf16[128,256]{1,0:T(8,128)(2,1)S(1)}, bf16[128,256]{1,0:T(8,128)(2,1)S(1)}, u32[]{:S(2)}, u32[]{:S(2)}) collective-permute-start(bf16[128,256]{1,0:T(8,128)(2,1)S(1)} %get-tuple-element.73), channel_id=1, source_target_pairs={{0,1},{1,4},{4,5},{5,8},{8,9},{9,12},{12,13},{13,0},{2,3},{3,6},{6... | collective-permute-start | bytes 196616 | tf_op jit(solution)/shard_map/ppermute | solution.py:332
  18.5 15.5 %collective-permute-start.11 = (bf16[1024,128]{1,0:T(8,128)(2,1)}, bf16[1024,128]{1,0:T(8,128)(2,1)S(1)}, u32[]{:S(2)}, u32[]{:S(2)}) collective-permute-start(bf16[1024,128]{1,0:T(8,128)(2,1)} %bitcast.6), channel_id=1, source_target_pairs={{0,12},{4,0},{8,4},{12,8},{1,13},{5,1},{9,5},{13,9},{2,14},{6,2},{... | collective-permute-start | bytes 786440 | tf_op jit(solution)/shard_map/ppermute | solution.py:332
  21.4 2.9 %collective-permute-start.7 = (bf16[1024,128]{1,0:T(8,128)(2,1)S(1)}, bf16[1024,128]{1,0:T(8,128)(2,1)S(1)}, u32[]{:S(2)}, u32[]{:S(2)}) collective-permute-start(bf16[1024,128]{1,0:T(8,128)(2,1)S(1)} %maximum_select_fusion), channel_id=1, source_target_pairs={{0,1},{1,0},{2,3},{3,2},{4,5},{5,4},{6,7},{7,6},{8,9},{9,8},{10,11... | collective-permute-start | bytes 786440 | tf_op jit(solution)/shard_map/ppermute | solution.py:336
  24.3 23.5 %copy-start.1 = (bf16[1024,1,128]{2,0,1:T(8,128)(2,1)S(1)}, bf16[1024,1,128]{2,0,1:T(8,128)(2,1)}, u32[]{:S(2)}) copy-start(bf16[1024,1,128]{2,0,1:T(8,128)(2,1)} %param.8) | copy-start | bytes 786436
  26.6 6.7 %collective-permute-start.10 = (f32[64,128]{1,0:T(8,128)S(1)}, f32[64,128]{1,0:T(8,128)S(1)}, u32[]{:S(2)}, u32[]{:S(2)}) collective-permute-start(f32[64,128]{1,0:T(8,128)S(1)} %get-tuple-element.89), channel_id=1, source_target_pairs={{0,4},{4,0},{8,12},{12,8},{1,5},{5,1},{9,13},{13,9},{2,6},{6,2},{1... | collective-permute-start | bytes 98312 | tf_op jit(solution)/shard_map/ppermute | solution.py:343
  26.6 7.3 %collective-permute-start.8 = (f32[64,128]{1,0:T(8,128)S(1)}, f32[64,128]{1,0:T(8,128)S(1)}, u32[]{:S(2)}, u32[]{:S(2)}) collective-permute-start(f32[64,128]{1,0:T(8,128)S(1)} %get-tuple-element.89), channel_id=1, source_target_pairs={{0,12},{4,8},{8,4},{12,0},{1,13},{5,9},{9,5},{13,1},{2,14},{6,10},... | collective-permute-start | bytes 98312 | tf_op jit(solution)/shard_map/ppermute | solution.py:343
  28.5 5.5 %collective-permute-start.9 = (f32[64,128]{1,0:T(8,128)S(1)}, f32[64,128]{1,0:T(8,128)S(1)}, u32[]{:S(2)}, u32[]{:S(2)}) collective-permute-start(f32[64,128]{1,0:T(8,128)S(1)} %get-tuple-element.89), channel_id=1, source_target_pairs={{0,8},{4,12},{8,0},{12,4},{1,9},{5,13},{9,1},{13,5},{2,10},{6,14},... | collective-permute-start | bytes 98312 | tf_op jit(solution)/shard_map/ppermute | solution.py:343
  30.1 15.7 %collective-permute-start.17 = (bf16[896,128]{1,0:T(8,128)(2,1)S(1)}, bf16[896,128]{1,0:T(8,128)(2,1)S(1)}, u32[]{:S(2)}, u32[]{:S(2)}) collective-permute-start(bf16[896,128]{1,0:T(8,128)(2,1)S(1)} %get-tuple-element.96), channel_id=1, source_target_pairs={{0,8},{4,12},{8,0},{12,4},{2,10},{6,14},{10,2},{14,6},{16,24},{20,... | collective-permute-start | bytes 688136 | tf_op jit(solution)/shard_map/ppermute | solution.py:357
  33.3 7.6 %collective-permute-start.18 = (bf16[640,128]{1,0:T(8,128)(2,1)S(1)}, bf16[640,128]{1,0:T(8,128)(2,1)S(1)}, u32[]{:S(2)}, u32[]{:S(2)}) collective-permute-start(bf16[640,128]{1,0:T(8,128)(2,1)S(1)} %get-tuple-element.97), channel_id=1, source_target_pairs={{1,9},{5,13},{9,1},{13,5},{3,11},{7,15},{11,3},{15,7},{17,25},{21,... | collective-permute-start | bytes 491528 | tf_op jit(solution)/shard_map/ppermute | solution.py:358
  34.0 1.3 %collective-permute-start.12 = (f32[64,128]{1,0:T(8,128)S(1)}, f32[64,128]{1,0:T(8,128)S(1)}, u32[]{:S(2)}, u32[]{:S(2)}) collective-permute-start(f32[64,128]{1,0:T(8,128)S(1)} %add_add_fusion.1.refs_2_), channel_id=1, source_target_pairs={{0,1},{1,0},{2,3},{3,2},{4,5},{5,4},{6,7},{7,6},{8,9},{9,8},{10,11... | collective-permute-start | bytes 98312 | tf_op jit(solution)/shard_map/ppermute | solution.py:336
  36.5 9.5 %collective-permute-start.13 = (f32[64,128]{1,0:T(8,128)S(1)}, f32[64,128]{1,0:T(8,128)S(1)}, u32[]{:S(2)}, u32[]{:S(2)}) collective-permute-start(f32[64,128]{1,0:T(8,128)S(1)} %get-tuple-element.94), channel_id=1, source_target_pairs={{0,12},{4,8},{8,4},{12,0},{1,13},{5,9},{9,5},{13,1},{2,14},{6,10},... | collective-permute-start | bytes 98312 | tf_op jit(solution)/shard_map/ppermute | solution.py:343
  38.6 7.9 %collective-permute-start.14 = (f32[64,128]{1,0:T(8,128)S(1)}, f32[64,128]{1,0:T(8,128)S(1)}, u32[]{:S(2)}, u32[]{:S(2)}) collective-permute-start(f32[64,128]{1,0:T(8,128)S(1)} %get-tuple-element.94), channel_id=1, source_target_pairs={{0,8},{4,12},{8,0},{12,4},{1,9},{5,13},{9,1},{13,5},{2,10},{6,14},... | collective-permute-start | bytes 98312 | tf_op jit(solution)/shard_map/ppermute | solution.py:343
  39.1 7.4 %collective-permute-start.15 = (f32[64,128]{1,0:T(8,128)S(1)}, f32[64,128]{1,0:T(8,128)S(1)}, u32[]{:S(2)}, u32[]{:S(2)}) collective-permute-start(f32[64,128]{1,0:T(8,128)S(1)} %get-tuple-element.94), channel_id=1, source_target_pairs={{0,4},{4,0},{8,12},{12,8},{1,5},{5,1},{9,13},{13,9},{2,6},{6,2},{1... | collective-permute-start | bytes 98312 | tf_op jit(solution)/shard_map/ppermute | solution.py:343
  45.9 1.9 %collective-permute-start.19 = (bf16[1024,128]{1,0:T(8,128)(2,1)S(1)}, bf16[1024,128]{1,0:T(8,128)(2,1)S(1)}, u32[]{:S(2)}, u32[]{:S(2)}) collective-permute-start(bf16[1024,128]{1,0:T(8,128)(2,1)S(1)} %maximum_select_fusion.1), channel_id=1, source_target_pairs={{0,1},{1,0},{2,3},{3,2},{4,5},{5,4},{6,7},{7,6},{8,9},{9,8},{10,11... | collective-permute-start | bytes 786440 | tf_op jit(solution)/shard_map/ppermute | solution.py:336
  46.5 1.3 %collective-permute-start.16 = (f32[64,128]{1,0:T(8,128)S(1)}, f32[64,128]{1,0:T(8,128)S(1)}, u32[]{:S(2)}, u32[]{:S(2)}) collective-permute-start(f32[64,128]{1,0:T(8,128)S(1)} %add_add_fusion.refs_3_), channel_id=1, source_target_pairs={{0,1},{1,0},{2,3},{3,2},{4,5},{5,4},{6,7},{7,6},{8,9},{9,8},{10,11... | collective-permute-start | bytes 98312 | tf_op jit(solution)/shard_map/ppermute | solution.py:336

commit v6 on v5

--- a/solution.py
+++ b/solution.py
@@ -10,7 +10,7 @@
 BLOCK = 128
 ITERS = 2
 LISTED = 6
-SENT = jnp.float32
+SENT = jnp.bfloat16
 VMEM = pl.BlockSpec(memory_space=pltpu.VMEM)
 ANY = pl.BlockSpec(memory_space=pl.ANY)
 HBM = pl.BlockSpec(memory_space=pltpu.HBM)
@@ -112,7 +112,7 @@
 
 def plan_kernel(blocks, shards, caps, pattern_hbm, q_hbm, k_ref, v_ref, *refs):
     outs, edges = refs[:3], refs[3:5]
-    score_ref, q_ref, lists_ref, crowded_ref = refs[5:9]
+    score_ref, q_ref, lists_ref, excess_ref = refs[5:9]
     own, pattern_ref, order_ref, rank_ref, sems, near_sems, sem = refs[9:]
     position, rep = lax.axis_index(("seq", "rep")), lax.axis_index("rep")
     width = k_ref.shape[1]
@@ -143,11 +143,11 @@
                 at = jnp.where(entry >= 0, entry - source * blocks, 0)
                 at = at if slot == 3 else rank_ref[slot - 4, at]
                 lists_ref[i, pattern_ref.shape[0] + slot - 3] = at
-    crowded = jnp.int32(0)
+    excess = jnp.int32(0)
     for source in range(shards):
         count = sum(listed_bits(pattern_ref, blocks, shards, source, source % 2 == 0))
-        crowded = jnp.maximum(crowded, jnp.where(count > caps[source % 2], 1, 0))
-    crowded_ref[0] = crowded
+        excess = jnp.maximum(excess, jnp.minimum(count - caps[source % 2], 2))
+    excess_ref[0] = excess
     held.wait()
     for i in range(blocks):
         query = block_rows(q_ref, i)
@@ -359,11 +359,22 @@
     )
 
 
-def remainder(crowded, *rest):
-    return lax.cond(
-        crowded,
-        lambda *x: tuple(shifted(part, "seq", -2) for part in x),
-        lambda *x: x,
+def remainder(excess, caps, rep, *rest):
+    def first(*parts):
+        at = jnp.where(rep == 0, (caps[0] - caps[1]) * BLOCK, 0)
+        sent = [lax.dynamic_slice_in_dim(part, at, BLOCK, 0) for part in parts]
+        sent = [shifted(part, "seq", -2) for part in sent]
+        return tuple(
+            lax.dynamic_update_slice_in_dim(part, new, at, 0) for part, new in zip(parts, sent)
+        )
+
+    return lax.switch(
+        excess,
+        (
+            lambda *parts: parts,
+            first,
+            lambda *parts: tuple(shifted(part, "seq", -2) for part in parts),
+        ),
         *rest,
     )
 
@@ -387,19 +398,19 @@
     k = key_rows.reshape(tok_local, width)
     v = value_rows.reshape(tok_local, width)
 
-    caps = (blocks - blocks // 8, blocks - 3 * blocks // 8)
+    caps = (blocks - blocks // 8, blocks - blocks // 2)
     columns = pattern.T
     k_near = shifted(k, "seq", -1)
     k_wide, k_slim, k_rest = pack_keys(blocks, shards, caps, columns, k)
     k_in, columns, k_wide, k_slim, k_rest = lax.optimization_barrier(
         (k, columns, k_wide, k_slim, k_rest)
     )
-    *v_packs, edges_low, edges_high, near_scores, q_held, lists, crowded = plan(
+    *v_packs, edges_low, edges_high, near_scores, q_held, lists, excess = plan(
         blocks, shards, caps, columns, q, k_in, v
     )
     v_wide, v_slim, v_rest = v_packs
     k_wide, k_slim = two_away(k_wide, k_slim)
-    k_rest, v_rest = remainder(crowded[0] > 0, k_rest, v_rest)
+    k_rest, v_rest = remainder(excess[0], caps, rep, k_rest, v_rest)
     low = shifted(edges_low, axes, 1)
     high = shifted(edges_high, axes, -1)
 
@@ -433,7 +444,6 @@
     v_wide, v_slim = two_away(v_wide, v_slim)
     mine, v_near = lax.optimization_barrier((mine, v_near))
     v_wide, v_slim = lax.optimization_barrier((v_wide, v_slim))
-    v_other = with_swap(v_near, v_wide, v_rest, caps, rep)
     factor, sums, sent = pl.pallas_call(
         lambda *refs: round_kernel(blocks, *refs),
         out_shape=(
@@ -449,8 +459,11 @@
         ],
         cost_estimate=pl.CostEstimate(flops=7864320, bytes_accessed=4194304, transcendentals=0),
         compiler_params=pltpu.CompilerParams(vmem_limit_bytes=LIMIT),
-    )(lists, exps, mine, swapped(mine.astype(SENT)))
-
+    )(lists, exps, mine, swapped(mine))
+
+    v_far, factor = lax.optimization_barrier(((v_near, v_wide, v_rest), factor))
+    v_near, v_wide, v_rest = v_far
+    v_other = with_swap(v_near, v_wide, v_rest, caps, rep)
     mine = over_seq(sums, sent)
     out = pl.pallas_call(
         lambda *refs: output_kernel(blocks, caps, *refs),
@@ -468,7 +481,7 @@
         cost_estimate=pl.CostEstimate(flops=201326592, bytes_accessed=6291456, transcendentals=0),
         compiler_params=pltpu.CompilerParams(vmem_limit_bytes=LIMIT),
     )(
-        lists, exps, factor, mine, swapped(mine.astype(SENT)), v, low[:, width:], high[:, width:],
+        lists, exps, factor, mine, swapped(mine), v, low[:, width:], high[:, width:],
         v_near, v_other, v_wide, v_slim, v_rest,
     )
     return out.reshape(tok_local, heads_local, width)

time: 50.6 us -> 48.5 us (0.958)
  waiting for transfers between devices: 9.39 us -> 7.79 us
    ppermute x2, waiting for transfers between devices: 4.89 us -> 3.33 us  [two_away(): lax.ppermute(wide, axes, [(2 * i, 2 * j) for i, j in moves])]
    ppermute x2, starting transfers between devices: 5.07 us -> 3.83 us  [two_away(): lax.ppermute(wide, axes, [(2 * i, 2 * j) for i, j in moves])]
    ppermute x6, starting transfers between devices: 8 us -> 8.91 us  [over_seq(): lax.ppermute(sent, 'seq', pairs(by))]
    ppermute x4, waiting for transfers between devices: 1.56 us -> 2.42 us  [shifted(): lax.ppermute(x, axis, [(i, (i + by) % devices) for i in range(devices)])]
    ppermute x4, waiting for transfers between devices: 2.38 us -> 1.84 us  [swapped(): return lax.ppermute(x, 'rep', [(0, 1), (1, 0)])]
  transfers between devices with their start and end apart: 18 -> 18, of which waited for: 5 -> 5; matrix products, arithmetic and copies ran while one was open for 0% -> 0% of each run, Pallas kernels for 19% -> 20%
where the time goes in v6:
time: 48.5 us; the launch traced here: 48 us
  starting transfers between devices  23.9 us (49%)
  Pallas kernels  11.8 us (24%)
  waiting for transfers between devices  7.79 us (16%)
  local copies, waits for them, and re-layouts  3.55 us (7%)
  between operations  0.81 us (2%)
    ppermute x6, starting transfers between devices, over_seq(): lax.ppermute(sent, 'seq', pairs(by))  8.91 us
    ppermute x4, starting transfers between devices, shifted(): lax.ppermute(x, axis, [(i, (i + by) % devices) for i in range(devices)])  8.41 us
    ppermute x2, starting transfers between devices, two_away(): lax.ppermute(wide, axes, [(2 * i, 2 * j) for i, j in moves])  3.83 us
    unnamed x10, local copies, waits for them, and re-layouts  3.54 us
    pallas_call x1, Pallas kernels, plan(): pl.pallas_call(lambda *refs: plan_kernel(blocks, shards, caps, *refs), ou...  3.46 us
    ppermute x2, waiting for transfers between devices, two_away(): lax.ppermute(wide, axes, [(2 * i, 2 * j) for i, j in moves])  3.33 us
    pallas_call x1, Pallas kernels, pack_keys(): pl.pallas_call(lambda *refs: key_kernel(blocks, shards, caps, *refs), out...  2.66 us
    ppermute x4, waiting for transfers between devices, shifted(): lax.ppermute(x, axis, [(i, (i + by) % devices) for i in range(devices)])  2.42 us
  transfers between devices with their start and end apart: 18, of which 5 were waited for; matrix products, arithmetic and copies ran while one was open for 0% of the time, Pallas kernels for 20%

profile of v6, /device:TPU:0, one launch (start us, length us, event | category | flops | bytes accessed | tf_op | source)
XLA Modules:
  0.0 48.0 jit_solution(10105223048640604398)
XLA Ops:
  0.0 5.0 %collective-permute-start.6 = (bf16[1024,128]{1,0:T(8,128)(2,1)}, bf16[1024,128]{1,0:T(8,128)(2,1)S(1)}, u32[]{:S(2)}, u32[]{:S(2)}) collective-permute-start(bf16[1024,128]{1,0:T(8,128)(2,1)} %bitcast.9), channel_id=1, source_target_pairs={{0,12},{4,0},{8,4},{12,8},{1,13},{5,1},{9,5},{13,9},{2,14},{6,2},{... | collective-permute-start | bytes 786440 | tf_op jit(solution)/shard_map/ppermute | solution.py:332
  5.0 2.7 %shard_map.46 = (bf16[896,128]{1,0:T(8,128)(2,1)}, bf16[512,128]{1,0:T(8,128)(2,1)}, bf16[512,128]{1,0:T(8,128)(2,1)S(1)}) custom-call(s32[6,64]{1,0:T(8,128)} %bitcast.13, bf16[1024,128]{1,0:T(8,128)(2,1)} %bitcast.10), custom_call_target="tpu_custom_call" | custom-call | tf_op jit(solution)/shard_map/pallas_call | solution.py:166
  7.7 1.9 %collective-permute-start.7 = (bf16[896,128]{1,0:T(8,128)(2,1)}, bf16[896,128]{1,0:T(8,128)(2,1)S(1)}, u32[]{:S(2)}, u32[]{:S(2)}) collective-permute-start(bf16[896,128]{1,0:T(8,128)(2,1)} %get-tuple-element.86), channel_id=1, source_target_pairs={{0,8},{4,12},{8,0},{12,4},{2,10},{6,14},{10,2},{14,6},{16,24},{20,... | collective-permute-start | bytes 688136 | tf_op jit(solution)/shard_map/ppermute | solution.py:357
  9.6 0.7 %collective-permute-start.8 = (bf16[512,128]{1,0:T(8,128)(2,1)}, bf16[512,128]{1,0:T(8,128)(2,1)S(1)}, u32[]{:S(2)}, u32[]{:S(2)}) collective-permute-start(bf16[512,128]{1,0:T(8,128)(2,1)} %get-tuple-element.87), channel_id=1, source_target_pairs={{1,9},{5,13},{9,1},{13,5},{3,11},{7,15},{11,3},{15,7},{17,25},{21,... | collective-permute-start | bytes 393224 | tf_op jit(solution)/shard_map/ppermute | solution.py:358
  10.3 0.0 copy-start
  10.3 0.9 %copy-done = bf16[1024,1,128]{2,0,1:T(8,128)(2,1)S(1)} copy-done((bf16[1024,1,128]{2,0,1:T(8,128)(2,1)S(1)}, bf16[1024,1,128]{2,0,1:T(8,128)(2,1)}, u32[]{:S(2)}) %copy-start) | copy-done | bytes 262168
  11.3 0.0 copy-start.2
  11.3 0.9 %copy-done.2 = bf16[1024,1,128]{2,0,1:T(8,128)(2,1)S(1)} copy-done((bf16[1024,1,128]{2,0,1:T(8,128)(2,1)S(1)}, bf16[1024,1,128]{2,0,1:T(8,128)(2,1)}, u32[]{:S(2)}) %copy-start.2) | copy-done | bytes 262168
  12.2 0.0 copy-start.3
  12.2 0.9 %copy-done.3 = bf16[1024,1,128]{2,0,1:T(8,128)(2,1)S(1)} copy-done((bf16[1024,1,128]{2,0,1:T(8,128)(2,1)S(1)}, bf16[1024,1,128]{2,0,1:T(8,128)(2,1)}, u32[]{:S(2)}) %copy-start.3) | copy-done | bytes 262168
  13.2 0.0 copy-start.4
  13.2 0.7 %copy-done.4 = s32[64,6]{0,1:T(8,128)S(1)} copy-done((s32[64,6]{0,1:T(8,128)S(1)}, s32[64,6]{0,1:T(8,128)}, u32[]{:S(2)}) %copy-start.4) | copy-done | bytes 1560
  13.9 3.5 %shard_map.47 = (bf16[896,128]{1,0:T(8,128)(2,1)S(1)}, bf16[512,128]{1,0:T(8,128)(2,1)S(1)}, bf16[512,128]{1,0:T(8,128)(2,1)S(1)}, bf16[128,256]{1,0:T(8,128)(2,...) custom-call(s32[6,64]{1,0:T(8,128)S(1)} %bitcast.14, ...), custom_call_target="tpu_custom_call" | custom-call | flops 100663296 | bytes 4194304 | tf_op jit(solution)/shard_map/pallas_call | solution.py:182
  18.0 0.1 collective-permute-start.5
  18.0 0.5 %collective-permute-start.4 = (bf16[128,256]{1,0:T(8,128)(2,1)S(1)}, bf16[128,256]{1,0:T(8,128)(2,1)S(1)}, u32[]{:S(2)}, u32[]{:S(2)}) collective-permute-start(bf16[128,256]{1,0:T(8,128)(2,1)S(1)} %get-tuple-element.84), channel_id=1, source_target_pairs={{0,1},{1,4},{4,5},{5,8},{8,9},{9,12},{12,13},{13,0},{2,3},{3,6},{6... | collective-permute-start | bytes 196616 | tf_op jit(solution)/shard_map/ppermute | solution.py:332
  18.5 0.0 collective-permute-done.8.refs_8_
  18.5 2.8 %collective-permute-start.13 = (bf16[1024,128]{1,0:T(8,128)(2,1)}, bf16[1024,128]{1,0:T(8,128)(2,1)S(1)}, u32[]{:S(2)}, u32[]{:S(2)}) collective-permute-start(bf16[1024,128]{1,0:T(8,128)(2,1)} %bitcast.6), channel_id=1, source_target_pairs={{0,12},{4,0},{8,4},{12,8},{1,13},{5,1},{9,5},{13,9},{2,14},{6,2},{... | collective-permute-start | bytes 786440 | tf_op jit(solution)/shard_map/ppermute | solution.py:332
  21.4 0.0 collective-permute-done.7.refs_7_
  21.4 0.0 collective-permute-done.6.refs_5_
  21.4 0.1 maximum_select_fusion
  21.4 0.5 collective-permute-start.9
  21.9 0.0 collective-permute-done.5
  21.9 2.4 %collective-permute-done.4 = bf16[128,256]{1,0:T(8,128)(2,1)S(1)} collective-permute-done((bf16[128,256]{1,0:T(8,128)(2,1)S(1)}, bf16[128,256]{1,0:T(8,128)(2,1)S(1)}, u32[]{:S(2)}, u32[]{:S(2)}) %collective-permute-start.4) | collective-permute-done | bytes 65568 | tf_op jit(solution)/shard_map/ppermute | solution.py:332
  24.3 0.0 collective-permute-done.9.refs_6_
  24.3 0.0 copy-start.1
  24.4 2.2 %shard_map.48 = (f32[8,6,128,128]{3,2,1,0:T(8,128)S(1)}, f32[64,128]{1,0:T(8,128)S(1)}, bf16[64,128]{1,0:T(8,128)(2,1)S(1)}) custom-call(s32[8,9]{1,0:T(8,128)S(1)} %get-tuple-element.80.refs_0_, bf16[1024,128]{1,0:T(8,128)(2,1)S(1)} %get-tuple-element.81.refs_1_, f32[8,3,128,128]{3,2,1,0:T(8,128)S(1)} %get-tuple-element.83.refs_2_, ...), custom_call_target="tpu_custom_call" | custom-call | flops 100663296 | bytes 6291456 | tf_op jit(solution)/shard_map/pallas_call | solution.py:421
  26.6 0.7 %collective-permute-start.10 = (bf16[64,128]{1,0:T(8,128)(2,1)S(1)}, bf16[64,128]{1,0:T(8,128)(2,1)S(1)}, u32[]{:S(2)}, u32[]{:S(2)}) collective-permute-start(bf16[64,128]{1,0:T(8,128)(2,1)S(1)} %get-tuple-element.100), channel_id=1, source_target_pairs={{0,12},{4,8},{8,4},{12,0},{1,13},{5,9},{9,5},{13,1},{2,14},{6,10},... | collective-permute-start | bytes 49160 | tf_op jit(solution)/shard_map/ppermute | solution.py:343
  27.3 0.0 collective-permute-start.11
  27.3 3.7 %collective-permute-start.12 = (bf16[64,128]{1,0:T(8,128)(2,1)S(1)}, bf16[64,128]{1,0:T(8,128)(2,1)S(1)}, u32[]{:S(2)}, u32[]{:S(2)}) collective-permute-start(bf16[64,128]{1,0:T(8,128)(2,1)S(1)} %get-tuple-element.100), channel_id=1, source_target_pairs={{0,4},{4,0},{8,12},{12,8},{1,5},{5,1},{9,13},{13,9},{2,6},{6,2},{1... | collective-permute-start | bytes 49160 | tf_op jit(solution)/shard_map/ppermute | solution.py:343
  31.0 1.9 %collective-permute-start.14 = (bf16[896,128]{1,0:T(8,128)(2,1)S(1)}, bf16[896,128]{1,0:T(8,128)(2,1)S(1)}, u32[]{:S(2)}, u32[]{:S(2)}) collective-permute-start(bf16[896,128]{1,0:T(8,128)(2,1)S(1)} %get-tuple-element.103), channel_id=1, source_target_pairs={{0,8},{4,12},{8,0},{12,4},{2,10},{6,14},{10,2},{14,6},{16,24},{20,... | collective-permute-start | bytes 688136 | tf_op jit(solution)/shard_map/ppermute | solution.py:357
  32.9 0.0 collective-permute-done.10
  32.9 0.7 %collective-permute-start.15 = (bf16[512,128]{1,0:T(8,128)(2,1)S(1)}, bf16[512,128]{1,0:T(8,128)(2,1)S(1)}, u32[]{:S(2)}, u32[]{:S(2)}) collective-permute-start(bf16[512,128]{1,0:T(8,128)(2,1)S(1)} %get-tuple-element.104), channel_id=1, source_target_pairs={{1,9},{5,13},{9,1},{13,5},{3,11},{7,15},{11,3},{15,7},{17,25},{21,... | collective-permute-start | bytes 393224 | tf_op jit(solution)/shard_map/ppermute | solution.py:358
  33.6 0.0 collective-permute-done.11
  33.6 0.0 collective-permute-done.12
  33.7 0.0 collective-permute-done.13.refs_8_
  33.7 0.5 %collective-permute-start.16 = (f32[64,128]{1,0:T(8,128)S(1)}, f32[64,128]{1,0:T(8,128)S(1)}, u32[]{:S(2)}, u32[]{:S(2)}) collective-permute-start(f32[64,128]{1,0:T(8,128)S(1)} %convert_add_fusion.1.refs_2_), channel_id=1, source_target_pairs={{0,1},{1,0},{2,3},{3,2},{4,5},{5,4},{6,7},{7,6},{8,9},{9,8},{10,11... | collective-permute-start | bytes 98312 | tf_op jit(solution)/shard_map/ppermute | solution.py:336
  34.2 0.9 %collective-permute-done.16.refs_3_ = f32[64,128]{1,0:T(8,128)S(1)} collective-permute-done((f32[64,128]{1,0:T(8,128)S(1)}, f32[64,128]{1,0:T(8,128)S(1)}, u32[]{:S(2)}, u32[]{:S(2)}) %collective-permute-start.16) | collective-permute-done | bytes 32800 | tf_op jit(solution)/shard_map/ppermute | solution.py:336
  35.1 1.1 %shard_map.49 = (f32[64,128]{1,0:T(8,128)S(1)}, f32[64,128]{1,0:T(8,128)S(1)}, bf16[64,128]{1,0:T(8,128)(2,1)S(1)}) custom-call(s32[8,9]{1,0:T(8,128)S(1)} %get-tuple-element.80.refs_0_, f32[8,6,128,128]{3,2,1,0:T(8,128)S(1)} %get-tuple-element.95.refs_1_, f32[64,128]{1,0:T(8,128)S(1)} %convert_add_fusion.1.refs_2_, ...), custom_call_target="tpu_custom_call" | custom-call | flops 7864320 | bytes 4194304 | tf_op jit(solution)/shard_map/pallas_call | solution.py:447
  36.2 2.3 %collective-permute-start.17 = (bf16[64,128]{1,0:T(8,128)(2,1)S(1)}, bf16[64,128]{1,0:T(8,128)(2,1)S(1)}, u32[]{:S(2)}, u32[]{:S(2)}) collective-permute-start(bf16[64,128]{1,0:T(8,128)(2,1)S(1)} %get-tuple-element.111), channel_id=1, source_target_pairs={{0,12},{4,8},{8,4},{12,0},{1,13},{5,9},{9,5},{13,1},{2,14},{6,10},... | collective-permute-start | bytes 49160 | tf_op jit(solution)/shard_map/ppermute | solution.py:343
  38.5 0.6 %collective-permute-start.18 = (bf16[64,128]{1,0:T(8,128)(2,1)S(1)}, bf16[64,128]{1,0:T(8,128)(2,1)S(1)}, u32[]{:S(2)}, u32[]{:S(2)}) collective-permute-start(bf16[64,128]{1,0:T(8,128)(2,1)S(1)} %get-tuple-element.111), channel_id=1, source_target_pairs={{0,8},{4,12},{8,0},{12,4},{1,9},{5,13},{9,1},{13,5},{2,10},{6,14},... | collective-permute-start | bytes 49160 | tf_op jit(solution)/shard_map/ppermute | solution.py:343
  39.2 1.5 %collective-permute-start.19 = (bf16[64,128]{1,0:T(8,128)(2,1)S(1)}, bf16[64,128]{1,0:T(8,128)(2,1)S(1)}, u32[]{:S(2)}, u32[]{:S(2)}) collective-permute-start(bf16[64,128]{1,0:T(8,128)(2,1)S(1)} %get-tuple-element.111), channel_id=1, source_target_pairs={{0,4},{4,0},{8,12},{12,8},{1,5},{5,1},{9,13},{13,9},{2,6},{6,2},{1... | collective-permute-start | bytes 49160 | tf_op jit(solution)/shard_map/ppermute | solution.py:343
  40.7 0.0 collective-permute-done.15.refs_11_
  40.7 3.3 %collective-permute-done.14.refs_10_ = bf16[896,128]{1,0:T(8,128)(2,1)S(1)} collective-permute-done((bf16[896,128]{1,0:T(8,128)(2,1)S(1)}, bf16[896,128]{1,0:T(8,128)(2,1)S(1)}, u32[]{:S(2)}, u32[]{:S(2)}) %collective-permute-start.14) | collective-permute-done | bytes 229408 | tf_op jit(solution)/shard_map/ppermute | solution.py:357
  44.0 0.1 maximum_select_fusion.1
  44.1 0.1 collective-permute-start.21
  44.1 0.0 collective-permute-done.17
  44.1 0.2 collective-permute-done.18
  44.3 0.0 collective-permute-done.19
  44.4 0.4 collective-permute-start.20
  44.7 1.0 %collective-permute-done.20.refs_4_ = f32[64,128]{1,0:T(8,128)S(1)} collective-permute-done((f32[64,128]{1,0:T(8,128)S(1)}, f32[64,128]{1,0:T(8,128)S(1)}, u32[]{:S(2)}, u32[]{:S(2)}) %collective-permute-start.20) | collective-permute-done | bytes 32800 | tf_op jit(solution)/shard_map/ppermute | solution.py:336
  45.7 0.0 collective-permute-done.21.refs_9_
  45.7 0.0 copy-done.1
  45.7 2.3 %shard_map.50 = bf16[1024,128]{1,0:T(8,128)(2,1)} custom-call(s32[8,9]{1,0:T(8,128)S(1)} %get-tuple-element.80.refs_0_, f32[8,6,128,128]{3,2,1,0:T(8,128)S(1)} %get-tuple-element.95.refs_1_, f32[64,128]{1,0:T(8,128)S(1)} %get-tuple-element.109.refs_2_, f32[64,128]{1,0:T(8,128)S(1)} %convert_add_fusion.refs_3_, ...), custom_call_target="tpu_custom_call" | custom-call | flops 201326592 | bytes 6291456 | tf_op jit(solution)/shard_map/pallas_call | solution.py:468
  (7 shorter events, 0.1 us)
Async XLA Ops:
  0.0 21.4 %collective-permute-start.6 = (bf16[1024,128]{1,0:T(8,128)(2,1)}, bf16[1024,128]{1,0:T(8,128)(2,1)S(1)}, u32[]{:S(2)}, u32[]{:S(2)}) collective-permute-start(bf16[1024,128]{1,0:T(8,128)(2,1)} %bitcast.9), channel_id=1, source_target_pairs={{0,12},{4,0},{8,4},{12,8},{1,13},{5,1},{9,5},{13,9},{2,14},{6,2},{... | collective-permute-start | bytes 786440 | tf_op jit(solution)/shard_map/ppermute | solution.py:332
  7.7 13.6 %collective-permute-start.7 = (bf16[896,128]{1,0:T(8,128)(2,1)}, bf16[896,128]{1,0:T(8,128)(2,1)S(1)}, u32[]{:S(2)}, u32[]{:S(2)}) collective-permute-start(bf16[896,128]{1,0:T(8,128)(2,1)} %get-tuple-element.86), channel_id=1, source_target_pairs={{0,8},{4,12},{8,0},{12,4},{2,10},{6,14},{10,2},{14,6},{16,24},{20,... | collective-permute-start | bytes 688136 | tf_op jit(solution)/shard_map/ppermute | solution.py:357
  9.6 8.9 %collective-permute-start.8 = (bf16[512,128]{1,0:T(8,128)(2,1)}, bf16[512,128]{1,0:T(8,128)(2,1)S(1)}, u32[]{:S(2)}, u32[]{:S(2)}) collective-permute-start(bf16[512,128]{1,0:T(8,128)(2,1)} %get-tuple-element.87), channel_id=1, source_target_pairs={{1,9},{5,13},{9,1},{13,5},{3,11},{7,15},{11,3},{15,7},{17,25},{21,... | collective-permute-start | bytes 393224 | tf_op jit(solution)/shard_map/ppermute | solution.py:358
  10.3 1.0 %copy-start = (bf16[1024,1,128]{2,0,1:T(8,128)(2,1)S(1)}, bf16[1024,1,128]{2,0,1:T(8,128)(2,1)}, u32[]{:S(2)}) copy-start(bf16[1024,1,128]{2,0,1:T(8,128)(2,1)} %param.9) | copy-start | bytes 786436
  11.3 0.9 %copy-start.2 = (bf16[1024,1,128]{2,0,1:T(8,128)(2,1)S(1)}, bf16[1024,1,128]{2,0,1:T(8,128)(2,1)}, u32[]{:S(2)}) copy-start(bf16[1024,1,128]{2,0,1:T(8,128)(2,1)} %param.8) | copy-start | bytes 786436
  12.2 0.9 %copy-start.3 = (bf16[1024,1,128]{2,0,1:T(8,128)(2,1)S(1)}, bf16[1024,1,128]{2,0,1:T(8,128)(2,1)}, u32[]{:S(2)}) copy-start(bf16[1024,1,128]{2,0,1:T(8,128)(2,1)} %param.7) | copy-start | bytes 786436
  13.2 0.7 %copy-start.4 = (s32[64,6]{0,1:T(8,128)S(1)}, s32[64,6]{0,1:T(8,128)}, u32[]{:S(2)}) copy-start(s32[64,6]{0,1:T(8,128)} %param.10) | copy-start | bytes 4612
  18.0 3.9 %collective-permute-start.5 = (bf16[128,256]{1,0:T(8,128)(2,1)S(1)}, bf16[128,256]{1,0:T(8,128)(2,1)S(1)}, u32[]{:S(2)}, u32[]{:S(2)}) collective-permute-start(bf16[128,256]{1,0:T(8,128)(2,1)S(1)} %get-tuple-element.85), channel_id=1, source_target_pairs={{0,13},{1,0},{4,1},{5,4},{8,5},{9,8},{12,9},{13,12},{2,15},{3,2},{... | collective-permute-start | bytes 196616 | tf_op jit(solution)/shard_map/ppermute | solution.py:332
  18.0 6.3 %collective-permute-start.4 = (bf16[128,256]{1,0:T(8,128)(2,1)S(1)}, bf16[128,256]{1,0:T(8,128)(2,1)S(1)}, u32[]{:S(2)}, u32[]{:S(2)}) collective-permute-start(bf16[128,256]{1,0:T(8,128)(2,1)S(1)} %get-tuple-element.84), channel_id=1, source_target_pairs={{0,1},{1,4},{4,5},{5,8},{8,9},{9,12},{12,13},{13,0},{2,3},{3,6},{6... | collective-permute-start | bytes 196616 | tf_op jit(solution)/shard_map/ppermute | solution.py:332
  18.5 15.1 %collective-permute-start.13 = (bf16[1024,128]{1,0:T(8,128)(2,1)}, bf16[1024,128]{1,0:T(8,128)(2,1)S(1)}, u32[]{:S(2)}, u32[]{:S(2)}) collective-permute-start(bf16[1024,128]{1,0:T(8,128)(2,1)} %bitcast.6), channel_id=1, source_target_pairs={{0,12},{4,0},{8,4},{12,8},{1,13},{5,1},{9,5},{13,9},{2,14},{6,2},{... | collective-permute-start | bytes 786440 | tf_op jit(solution)/shard_map/ppermute | solution.py:332
  21.4 2.9 %collective-permute-start.9 = (bf16[1024,128]{1,0:T(8,128)(2,1)S(1)}, bf16[1024,128]{1,0:T(8,128)(2,1)S(1)}, u32[]{:S(2)}, u32[]{:S(2)}) collective-permute-start(bf16[1024,128]{1,0:T(8,128)(2,1)S(1)} %maximum_select_fusion), channel_id=1, source_target_pairs={{0,1},{1,0},{2,3},{3,2},{4,5},{5,4},{6,7},{7,6},{8,9},{9,8},{10,11... | collective-permute-start | bytes 786440 | tf_op jit(solution)/shard_map/ppermute | solution.py:336
  24.3 21.4 %copy-start.1 = (bf16[1024,1,128]{2,0,1:T(8,128)(2,1)S(1)}, bf16[1024,1,128]{2,0,1:T(8,128)(2,1)}, u32[]{:S(2)}) copy-start(bf16[1024,1,128]{2,0,1:T(8,128)(2,1)} %param.9) | copy-start | bytes 786436
  26.6 6.4 %collective-permute-start.10 = (bf16[64,128]{1,0:T(8,128)(2,1)S(1)}, bf16[64,128]{1,0:T(8,128)(2,1)S(1)}, u32[]{:S(2)}, u32[]{:S(2)}) collective-permute-start(bf16[64,128]{1,0:T(8,128)(2,1)S(1)} %get-tuple-element.100), channel_id=1, source_target_pairs={{0,12},{4,8},{8,4},{12,0},{1,13},{5,9},{9,5},{13,1},{2,14},{6,10},... | collective-permute-start | bytes 49160 | tf_op jit(solution)/shard_map/ppermute | solution.py:343
  27.3 6.3 %collective-permute-start.11 = (bf16[64,128]{1,0:T(8,128)(2,1)S(1)}, bf16[64,128]{1,0:T(8,128)(2,1)S(1)}, u32[]{:S(2)}, u32[]{:S(2)}) collective-permute-start(bf16[64,128]{1,0:T(8,128)(2,1)S(1)} %get-tuple-element.100), channel_id=1, source_target_pairs={{0,8},{4,12},{8,0},{12,4},{1,9},{5,13},{9,1},{13,5},{2,10},{6,14},... | collective-permute-start | bytes 49160 | tf_op jit(solution)/shard_map/ppermute | solution.py:343
  27.3 6.3 %collective-permute-start.12 = (bf16[64,128]{1,0:T(8,128)(2,1)S(1)}, bf16[64,128]{1,0:T(8,128)(2,1)S(1)}, u32[]{:S(2)}, u32[]{:S(2)}) collective-permute-start(bf16[64,128]{1,0:T(8,128)(2,1)S(1)} %get-tuple-element.100), channel_id=1, source_target_pairs={{0,4},{4,0},{8,12},{12,8},{1,5},{5,1},{9,13},{13,9},{2,6},{6,2},{1... | collective-permute-start | bytes 49160 | tf_op jit(solution)/shard_map/ppermute | solution.py:343
  31.0 13.0 %collective-permute-start.14 = (bf16[896,128]{1,0:T(8,128)(2,1)S(1)}, bf16[896,128]{1,0:T(8,128)(2,1)S(1)}, u32[]{:S(2)}, u32[]{:S(2)}) collective-permute-start(bf16[896,128]{1,0:T(8,128)(2,1)S(1)} %get-tuple-element.103), channel_id=1, source_target_pairs={{0,8},{4,12},{8,0},{12,4},{2,10},{6,14},{10,2},{14,6},{16,24},{20,... | collective-permute-start | bytes 688136 | tf_op jit(solution)/shard_map/ppermute | solution.py:357
  32.9 7.7 %collective-permute-start.15 = (bf16[512,128]{1,0:T(8,128)(2,1)S(1)}, bf16[512,128]{1,0:T(8,128)(2,1)S(1)}, u32[]{:S(2)}, u32[]{:S(2)}) collective-permute-start(bf16[512,128]{1,0:T(8,128)(2,1)S(1)} %get-tuple-element.104), channel_id=1, source_target_pairs={{1,9},{5,13},{9,1},{13,5},{3,11},{7,15},{11,3},{15,7},{17,25},{21,... | collective-permute-start | bytes 393224 | tf_op jit(solution)/shard_map/ppermute | solution.py:358
  33.7 1.4 %collective-permute-start.16 = (f32[64,128]{1,0:T(8,128)S(1)}, f32[64,128]{1,0:T(8,128)S(1)}, u32[]{:S(2)}, u32[]{:S(2)}) collective-permute-start(f32[64,128]{1,0:T(8,128)S(1)} %convert_add_fusion.1.refs_2_), channel_id=1, source_target_pairs={{0,1},{1,0},{2,3},{3,2},{4,5},{5,4},{6,7},{7,6},{8,9},{9,8},{10,11... | collective-permute-start | bytes 98312 | tf_op jit(solution)/shard_map/ppermute | solution.py:336
  36.2 7.9 %collective-permute-start.17 = (bf16[64,128]{1,0:T(8,128)(2,1)S(1)}, bf16[64,128]{1,0:T(8,128)(2,1)S(1)}, u32[]{:S(2)}, u32[]{:S(2)}) collective-permute-start(bf16[64,128]{1,0:T(8,128)(2,1)S(1)} %get-tuple-element.111), channel_id=1, source_target_pairs={{0,12},{4,8},{8,4},{12,0},{1,13},{5,9},{9,5},{13,1},{2,14},{6,10},... | collective-permute-start | bytes 49160 | tf_op jit(solution)/shard_map/ppermute | solution.py:343
  38.5 5.8 %collective-permute-start.18 = (bf16[64,128]{1,0:T(8,128)(2,1)S(1)}, bf16[64,128]{1,0:T(8,128)(2,1)S(1)}, u32[]{:S(2)}, u32[]{:S(2)}) collective-permute-start(bf16[64,128]{1,0:T(8,128)(2,1)S(1)} %get-tuple-element.111), channel_id=1, source_target_pairs={{0,8},{4,12},{8,0},{12,4},{1,9},{5,13},{9,1},{13,5},{2,10},{6,14},... | collective-permute-start | bytes 49160 | tf_op jit(solution)/shard_map/ppermute | solution.py:343
  39.2 5.2 %collective-permute-start.19 = (bf16[64,128]{1,0:T(8,128)(2,1)S(1)}, bf16[64,128]{1,0:T(8,128)(2,1)S(1)}, u32[]{:S(2)}, u32[]{:S(2)}) collective-permute-start(bf16[64,128]{1,0:T(8,128)(2,1)S(1)} %get-tuple-element.111), channel_id=1, source_target_pairs={{0,4},{4,0},{8,12},{12,8},{1,5},{5,1},{9,13},{13,9},{2,6},{6,2},{1... | collective-permute-start | bytes 49160 | tf_op jit(solution)/shard_map/ppermute | solution.py:343
  44.1 1.7 %collective-permute-start.21 = (bf16[1024,128]{1,0:T(8,128)(2,1)S(1)}, bf16[1024,128]{1,0:T(8,128)(2,1)S(1)}, u32[]{:S(2)}, u32[]{:S(2)}) collective-permute-start(bf16[1024,128]{1,0:T(8,128)(2,1)S(1)} %maximum_select_fusion.1), channel_id=1, source_target_pairs={{0,1},{1,0},{2,3},{3,2},{4,5},{5,4},{6,7},{7,6},{8,9},{9,8},{10,11... | collective-permute-start | bytes 786440 | tf_op jit(solution)/shard_map/ppermute | solution.py:336
  44.4 1.4 %collective-permute-start.20 = (f32[64,128]{1,0:T(8,128)S(1)}, f32[64,128]{1,0:T(8,128)S(1)}, u32[]{:S(2)}, u32[]{:S(2)}) collective-permute-start(f32[64,128]{1,0:T(8,128)S(1)} %convert_add_fusion.refs_3_), channel_id=1, source_target_pairs={{0,1},{1,0},{2,3},{3,2},{4,5},{5,4},{6,7},{7,6},{8,9},{9,8},{10,11... | collective-permute-start | bytes 98312 | tf_op jit(solution)/shard_map/ppermute | solution.py:336
